TPU v7x, 128 devices: a whole 4x4x4 slice. The times are simulated.
128 devices in a mesh: gx: 4 (over z_hi, core), gy: 4 (over y), gz: 8 (over z_lo, x).
Axes of the slice: x: 4, y: 4, z: 4 (z_hi: 2, z_lo: 2; z = z_hi * 2 + z_lo), core: 2. Of those that a mesh axis runs over, the one named last changes fastest.
Arguments:
- velocities: float32 [3, 5242880], P(None, ('gx', 'gy', 'gz')), may hold values from -6 to 6
- particle_cells: int32 [2, 5242880], P(None, ('gx', 'gy', 'gz')), may hold values from 0 to 4095
- grid_shift: int32 [2, 3], replicated, may hold values from -1 to 1, as said below
- axis_index: int32 [2, 16, 32, 1024], P(None, 'gx', 'gy', 'gz'), may hold values from 0 to 7
- migrate_dir: int32 [5242880], P(('gx', 'gy', 'gz')), may hold values from 0 to 6, as said below
- migrate_slot: int32 [5242880], P(('gx', 'gy', 'gz')), may hold values from 0 to 159, as said below
- contact_colloid: int32 [262144], P(('gx', 'gy', 'gz')), may hold values from 0 to 32767, as said below
- contact_particle: int32 [262144], P(('gx', 'gy', 'gz')), may hold values from 0 to 40959
- contact_weight: float32 [262144], P(('gx', 'gy', 'gz')), may hold values from 0.05 to 1
- colloid_velocity: float32 [3, 32768], P(None, ('gx', 'gy', 'gz')), may hold values from -6 to 6
Outputs:
- cell_velocity: float32 [3, 16, 32, 1024], P(None, 'gx', 'gy', 'gz')
- migrated: float32 [3, 5365760], P(None, ('gx', 'gy', 'gz'))
- colloid_force: float32 [3, 32768], P(None, ('gx', 'gy', 'gz'))
Inputs may be any that keep to these rules, and one draw needn't show every extreme that they name: `grid_shift`: every entry is -1 or 1, and along every dimension the sign changes from each step to the next. `migrate_dir`: code 0 keeps a particle on its device. On every device at most 160 particles take any one nonzero code, and on every device some nonzero code is taken by exactly 160 particles. `migrate_slot`: among the particles of one device with the same nonzero code, the slots are distinct and run from 0 to that code's count minus 1; the slot is 0 where the code is 0. `contact_colloid`: the owner of every contact's colloid is the contact's own device or one of its six face neighbours along gx, gy, gz (periodic).
All inputs are finite; a program needn't handle non-finite values.
Results may differ from a plain program's by a relative error of at most 0.00015.
Values sent between devices are 32-bit elements; how exact they have to be, the bound alone decides.
No kernel may reach another device: no remote copies, remote signals or barrier semaphores. Data moves between devices by JAX's collectives and lax.ppermute only.
A program may use at most 128 MiB of HBM per device.

v0:
```python
import math

import jax
import jax.numpy as jnp
import numpy as np
from jax import lax
from jax.sharding import PartitionSpec as P

COLLOIDS_PER_UNIT = 256
CAP = 160


SEND_PLACES = ((1, 0, 0), (0, 1, 1), (0, 1, 0), (1, 0, 1), (0, 0, 1), (1, 1, 0))
TAKE_PLACES = ((0, 1, 1), (3, 2, 2), (1, 0, 1), (2, 3, 2), (1, 1, 0), (2, 2, 3))


def with_halo(block, sides, width):
    for axis, dim in sides:
        count = lax.axis_size(axis)
        forward = [(i, i + 1) for i in range(count - 1)]
        forward.append((count - 1, 0))
        backward = [(target, source) for source, target in forward]
        low = lax.ppermute(
            lax.slice_in_dim(block, block.shape[dim] - width, None, axis=dim), axis, forward
        )
        high = lax.ppermute(lax.slice_in_dim(block, 0, width, axis=dim), axis, backward)
        block = jnp.concatenate([low, block, high], axis=dim)
    return block


def rotation_table():
    angle = 130.0 * math.pi / 180.0
    cosine = math.cos(angle)
    sine_value = math.sin(angle)
    entries = []
    for number in range(8):
        signs = [1.0 if number >> bit & 1 else -1.0 for bit in range(3)]
        unit = np.array(signs) / math.sqrt(3.0)
        cross = np.array(
            [[0.0, -unit[2], unit[1]], [unit[2], 0.0, -unit[0]], [-unit[1], unit[0], 0.0]]
        )
        matrix = cosine * np.eye(3) + (1.0 - cosine) * np.outer(unit, unit) + sine_value * cross
        entries.append(matrix.reshape(9))
    return np.array(entries)


def cell_rotation(axis_ids, table):
    matrix = jnp.zeros((9,) + axis_ids.shape, jnp.float32)
    for number in range(8):
        chosen = jnp.where(axis_ids == number, 1.0, 0.0).astype(jnp.float32)
        matrix = matrix + chosen[None] * table[number].reshape((9,) + (1,) * axis_ids.ndim)
    return matrix


def apply_rotation(matrix, vector):
    rows = [
        matrix[3 * row] * vector[0]
        + matrix[3 * row + 1] * vector[1]
        + matrix[3 * row + 2] * vector[2]
        for row in range(3)
    ]
    return jnp.stack(rows)


def fold_rims(field, axis, length):
    lower = lax.slice_in_dim(field, 0, 1, axis=axis)
    inner = lax.slice_in_dim(field, 2, length + 2, axis=axis)
    upper = lax.slice_in_dim(field, length + 3, length + 4, axis=axis)
    low_widths = [(0, 0)] * field.ndim
    low_widths[axis] = (0, length - 1)
    high_widths = [(0, 0)] * field.ndim
    high_widths[axis] = (length - 1, 0)
    return inner + jnp.pad(lower, low_widths) + jnp.pad(upper, high_widths)


def face_cube(blocks):
    cube = jnp.zeros((2, 2, 2) + blocks[0].shape, jnp.float32)
    for place, block in zip(SEND_PLACES, blocks):
        cube = cube.at[place].set(block)
    return cube


def face_take(beside_all):
    return [beside_all[place] for place in TAKE_PLACES]


def body(
    velocities,
    particle_cells,
    grid_shift,
    axis_index,
    migrate_dir,
    migrate_slot,
    contact_colloid,
    contact_particle,
    contact_weight,
    colloid_velocity,
):
    table = jnp.asarray(rotation_table(), jnp.float32)
    cells_x, cells_y, cells_z = (axis_index.shape[1], axis_index.shape[2], axis_index.shape[3])
    extent = (cells_x + 2, cells_y + 2, cells_z + 2)
    extent_total = extent[0] * extent[1] * extent[2]
    velocity_now = velocities
    mean = jnp.zeros((3, cells_x, cells_y, cells_z), jnp.float32)
    for step in range(particle_cells.shape[0]):
        local = particle_cells[step]
        place_x = local // (cells_y * cells_z) + grid_shift[step, 0] + 1
        place_y = local // cells_z % cells_y + grid_shift[step, 1] + 1
        place_z = local % cells_z + grid_shift[step, 2] + 1
        wide_cell = (place_x * extent[1] + place_y) * extent[2] + place_z
        momentum = (
            jnp.zeros((3, extent_total), jnp.float32)
            .at[:, wide_cell]
            .add(velocity_now)
            .reshape((3,) + extent)
        )
        counts = (
            jnp.zeros((1, extent_total), jnp.float32)
            .at[:, wide_cell]
            .add(1.0)
            .reshape((1,) + extent)
        )
        momentum, counts = (
            with_halo(momentum, (("gx", 1), ("gy", 2), ("gz", 3)), 1),
            with_halo(counts, (("gx", 1), ("gy", 2), ("gz", 3)), 1),
        )
        for axis, length in ((1, cells_x), (2, cells_y), (3, cells_z)):
            momentum = fold_rims(momentum, axis, length)
            counts = fold_rims(counts, axis, length)
        mean = momentum / jnp.maximum(counts, 1.0)
        matrix = cell_rotation(axis_index[step], table)
        offset = mean - apply_rotation(matrix, mean)
        packed = jnp.concatenate([matrix, offset], axis=0)
        beside_all = with_halo(packed, (("gx", 1), ("gy", 2), ("gz", 3)), 1)
        reach = beside_all.reshape(12, extent_total)
        picked = reach[:, wide_cell]
        velocity_now = apply_rotation(picked[:9], velocity_now) + picked[9:]
    size_x = lax.axis_size("gx")
    size_y = lax.axis_size("gy")
    size_z = lax.axis_size("gz")
    mine_x = lax.axis_index("gx")
    mine_y = lax.axis_index("gy")
    mine_z = lax.axis_index("gz")
    leaving = migrate_dir > 0
    target = jnp.where(leaving, (migrate_dir - 1) * CAP + migrate_slot, 6 * CAP)
    blocks = (
        jnp.zeros((3, 6 * CAP), jnp.float32)
        .at[:, target]
        .set(velocity_now, mode="drop")
        .reshape(3, 6, CAP)
    )
    kept = jnp.where(leaving[None], 0.0, velocity_now)
    cube = face_cube([blocks[:, number] for number in range(6)])
    beside_all = with_halo(cube, (("gx", 0), ("gy", 1), ("gz", 2)), 1)
    arrivals = jnp.stack(face_take(beside_all), axis=1)
    migrated = jnp.concatenate([kept, arrivals.reshape(3, 6 * CAP)], axis=1)
    weighted = contact_weight[None] * velocity_now[:, contact_particle]
    owning_device = contact_colloid // COLLOIDS_PER_UNIT
    apart_x = (owning_device // (size_y * size_z) - mine_x) % size_x
    apart_y = (owning_device // size_z % size_y - mine_y) % size_y
    apart_z = (owning_device % size_z - mine_z) % size_z
    slot_code = jnp.where(
        apart_x == 1,
        1,
        jnp.where(
            apart_x == size_x - 1,
            2,
            jnp.where(
                apart_y == 1,
                3,
                jnp.where(
                    apart_y == size_y - 1,
                    4,
                    jnp.where(apart_z == 1, 5, jnp.where(apart_z == size_z - 1, 6, 0)),
                ),
            ),
        ),
    )
    position = slot_code * COLLOIDS_PER_UNIT + contact_colloid % COLLOIDS_PER_UNIT
    sums = (
        jnp.zeros((3, 7 * COLLOIDS_PER_UNIT), jnp.float32)
        .at[:, position]
        .add(weighted)
        .reshape(3, 7, COLLOIDS_PER_UNIT)
    )
    weight_sums = (
        jnp.zeros((1, 7 * COLLOIDS_PER_UNIT), jnp.float32)
        .at[:, position]
        .add(contact_weight[None])
        .reshape(1, 7, COLLOIDS_PER_UNIT)
    )
    cube_sums = face_cube([sums[:, number + 1] for number in range(6)])
    cube_weights = face_cube([weight_sums[:, number + 1] for number in range(6)])
    around_sums, around_weights = (
        with_halo(cube_sums, (("gx", 0), ("gy", 1), ("gz", 2)), 1),
        with_halo(cube_weights, (("gx", 0), ("gy", 1), ("gz", 2)), 1),
    )
    sum_wv = sums[:, 0]
    sum_w = weight_sums[:, 0]
    for piece in face_take(around_sums):
        sum_wv = sum_wv + piece
    for piece in face_take(around_weights):
        sum_w = sum_w + piece
    colloid_force = (sum_wv - sum_w * colloid_velocity) / jnp.maximum(sum_w, 1.0)
    return (mean, migrated, colloid_force)


def solution(mesh):
    placed = (
        P(None, ("gx", "gy", "gz")),
        P(None, ("gx", "gy", "gz")),
        P(),
        P(None, "gx", "gy", "gz"),
        P(("gx", "gy", "gz")),
        P(("gx", "gy", "gz")),
        P(("gx", "gy", "gz")),
        P(("gx", "gy", "gz")),
        P(("gx", "gy", "gz")),
        P(None, ("gx", "gy", "gz")),
    )
    return jax.shard_map(
        body,
        mesh=mesh,
        in_specs=placed,
        out_specs=(
            P(None, "gx", "gy", "gz"),
            P(None, ("gx", "gy", "gz")),
            P(None, ("gx", "gy", "gz")),
        ),
        check_vma=False,
    )
```

profile of v0, /device:TPU:6, one launch (start us, length us, event | category | flops | bytes accessed | tf_op | source)
XLA Modules:
  0.0 1533.7 jit_solution(12446584493028977020)
XLA Ops:
  2.2 10.3 compare_select_fusion
  12.5 213.7 %scatter_custom_fusion.1 = f32[7800]{0:T(1024)S(1)} fusion(s32[40960]{0:T(1024)S(1)} %bitcast.198, f32[40960]{0:T(1024)S(1)} %broadcast.921, f32[]{:T(128)} %constant.646.clone.1), kind=kCustom, calls=%fused_computation.246 | custom fusion | flops 40960 | bytes 31204 | tf_op jit(solution)/shard_map/scatter-add | solution.py:120
  226.5 3.4 collective-permute-start.7
  229.9 213.7 %scatter_custom_fusion.3 = f32[7800]{0:T(1024)S(1)} fusion(s32[40960]{0:T(1024)S(1)} %bitcast.195, f32[40960]{0:T(1024)S(1)} %broadcast.921, f32[]{:T(128)} %constant.646.clone.1), kind=kCustom, calls=%fused_computation.244 | custom fusion | flops 40960 | bytes 31204 | tf_op jit(solution)/shard_map/scatter-add | solution.py:120
  447.1 11.1 copy.129
  458.1 219.8 %scatter_custom_fusion = f32[3,7800]{0,1:T(8,128)} fusion(s32[40960]{0:T(1024)S(1)} %bitcast.199, f32[40960,3]{1,0:T(8,128)} %copy.129, f32[]{:T(128)} %constant.646.clone.1), kind=kCustom, calls=%fused_computation.12 | custom fusion | flops 122880 | bytes 94112 | tf_op jit(solution)/shard_map/scatter-add | solution.py:114
  682.3 11.4 scatter_custom_fusion.6
  718.7 4.5 collective-permute-done.29
  731.2 3.6 collective-permute-done.4
  738.0 3.2 collective-permute-start.13
  749.9 13.5 collective-permute-start.17
  764.3 3.4 collective-permute-done.17
  772.8 137.2 %gather_fusion = f32[40960,12]{1,0:T(8,128)} fusion(f32[12,7800]{0,1:T(8,128)} %copy.135, s32[40960]{0:T(1024)S(1)} %broadcast_clamp_fusion.1), kind=kCustom, calls=%fused_computation | custom fusion | bytes 4096000 | tf_op jit(solution)/shard_map/gather | solution.py:136
  910.0 11.5 copy.136
  924.2 10.0 copy.137
  934.3 219.7 %scatter_custom_fusion.2 = f32[3,7800]{0,1:T(8,128)} fusion(s32[40960]{0:T(1024)} %bitcast.197, f32[40960,3]{1,0:T(8,128)} %copy.137, f32[]{:T(128)} %constant.646.clone.1), kind=kCustom, calls=%fused_computation.10 | custom fusion | flops 122880 | bytes 94112 | tf_op jit(solution)/shard_map/scatter-add | solution.py:114
  1165.4 3.2 collective-permute-start.21
  1209.7 137.2 %gather_fusion.1 = f32[40960,12]{1,0:T(8,128)} fusion(f32[12,7800]{0,1:T(8,128)} %copy.143, s32[40960]{0:T(1024)S(1)} %copy-done.5), kind=kCustom, calls=%fused_computation.1 | custom fusion | bytes 4096000 | tf_op jit(solution)/shard_map/gather | solution.py:136
  1346.9 11.4 copy.144
  1361.2 10.0 copy.155
  1371.3 24.3 %scatter_custom_fusion.5 = f32[3,1792]{0,1:T(8,128)S(1)} fusion(s32[2048]{0:T(1024)} %copy-done.20, f32[2048]{0:T(1024)S(1)} %copy-done.17, f32[]{:T(128)} %constant.646.clone.1, f32[3,40960]{0,1:T(8,128)} %copy.155, s32[2048]{0:T(1024)S(1)} %get-tuple-element.341), kind=kCustom, calls=%fused_computation.16 | custom fusion | flops 12288 | bytes 21009920 | tf_op jit(solution)/shard_map/scatter-add | solution.py:183
  1396.1 10.0 copy.145
  1406.2 100.7 %scatter_custom_fusion.4 = f32[3,960]{0,1:T(8,128)S(1)} fusion(s32[40960]{0:T(1024)} %compare_select_fusion.6, f32[40960,3]{1,0:T(8,128)} %copy.145, f32[]{:T(128)} %constant.646.clone.1), kind=kCustom, calls=%fused_computation.45 | custom fusion | bytes 12032 | tf_op jit(solution)/shard_map/scatter | solution.py:149
  1521.5 4.1 collective-permute-start.40
  (334 shorter events, 140.7 us)
Async XLA Ops:
  226.4 468.9 %collective-permute-start.6 = (f32[1,1,10,130]{3,2,1,0:T(8,128)S(1)}, f32[1,1,10,130]{3,2,1,0:T(8,128)S(1)}, u32[]{:S(2)}, u32[]{:S(2)}) collective-permute-start(f32[1,1,10,130]{3,2,1,0:T(8,128)S(1)} %get-tuple-element.295), channel_id=1, source_target_pairs={{0,32},{32,64},{64,96},{96,0},{1,33},{33,65},{65,97},{97,1},{2,34}... | collective-permute-start | bytes 15608 | tf_op jit(solution)/shard_map/ppermute | solution.py:23
  226.5 471.8 %collective-permute-start.7 = (f32[1,1,10,130]{3,2,1,0:T(8,128)S(1)}, f32[1,1,10,130]{3,2,1,0:T(8,128)S(1)}, u32[]{:S(2)}, u32[]{:S(2)}) collective-permute-start(f32[1,1,10,130]{3,2,1,0:T(8,128)S(1)} %get-tuple-element.294), channel_id=1, source_target_pairs={{32,0},{64,32},{96,64},{0,96},{33,1},{65,33},{97,65},{1,97},{34,2}... | collective-permute-start | bytes 15608 | tf_op jit(solution)/shard_map/ppermute | solution.py:26
  443.8 255.2 %collective-permute-start.24 = (f32[1,1,10,130]{3,2,1,0:T(8,128)S(1)}, f32[1,1,10,130]{3,2,1,0:T(8,128)S(1)}, u32[]{:S(2)}, u32[]{:S(2)}) collective-permute-start(f32[1,1,10,130]{3,2,1,0:T(8,128)S(1)} %get-tuple-element.293), channel_id=1, source_target_pairs={{0,32},{32,64},{64,96},{96,0},{1,33},{33,65},{65,97},{97,1},{2,34}... | collective-permute-start | bytes 15608 | tf_op jit(solution)/shard_map/ppermute | solution.py:23
  444.4 256.2 %collective-permute-start.25 = (f32[1,1,10,130]{3,2,1,0:T(8,128)S(1)}, f32[1,1,10,130]{3,2,1,0:T(8,128)S(1)}, u32[]{:S(2)}, u32[]{:S(2)}) collective-permute-start(f32[1,1,10,130]{3,2,1,0:T(8,128)S(1)} %get-tuple-element.292), channel_id=1, source_target_pairs={{32,0},{64,32},{96,64},{0,96},{33,1},{65,33},{97,65},{1,97},{34,2}... | collective-permute-start | bytes 15608 | tf_op jit(solution)/shard_map/ppermute | solution.py:26
  681.5 42.0 %collective-permute-start = (f32[3,1,10,130]{3,2,1,0:T(8,128)S(1)}, f32[3,1,10,130]{3,2,1,0:T(8,128)S(1)}, u32[]{:S(2)}, u32[]{:S(2)}) collective-permute-start(f32[3,1,10,130]{3,2,1,0:T(8,128)S(1)} %get-tuple-element.269), channel_id=1, source_target_pairs={{0,32},{32,64},{64,96},{96,0},{1,33},{33,65},{65,97},{97,1},{2,34}... | collective-permute-start | bytes 46808 | tf_op jit(solution)/shard_map/ppermute | solution.py:23
  695.3 28.3 %collective-permute-start.1 = (f32[3,1,10,130]{3,2,1,0:T(8,128)S(1)}, f32[3,1,10,130]{3,2,1,0:T(8,128)S(1)}, u32[]{:S(2)}, u32[]{:S(2)}) collective-permute-start(f32[3,1,10,130]{3,2,1,0:T(8,128)S(1)} %get-tuple-element.268), channel_id=1, source_target_pairs={{32,0},{64,32},{96,64},{0,96},{33,1},{65,33},{97,65},{1,97},{34,2}... | collective-permute-start | bytes 46808 | tf_op jit(solution)/shard_map/ppermute | solution.py:26
  698.3 65.1 %collective-permute-start.48 = (f32[1,2,2,1,256]{4,3,2,1,0:T(1,128)S(1)}, f32[1,2,2,1,256]{4,3,2,1,0:T(1,128)S(1)}, u32[]{:S(2)}, u32[]{:S(2)}) collective-permute-start(f32[1,2,2,1,256]{4,3,2,1,0:T(1,128)S(1)} %get-tuple-element.326), channel_id=1, source_target_pairs={{0,32},{32,64},{64,96},{96,0},{1,33},{33,65},{65,97},{97,1},{2,34}... | collective-permute-start | bytes 12296 | tf_op jit(solution)/shard_map/ppermute | solution.py:23
  709.9 6.9 collective-permute-start.11
  718.7 44.7 %collective-permute-start.49 = (f32[1,2,2,1,256]{4,3,2,1,0:T(1,128)S(1)}, f32[1,2,2,1,256]{4,3,2,1,0:T(1,128)S(1)}, u32[]{:S(2)}, u32[]{:S(2)}) collective-permute-start(f32[1,2,2,1,256]{4,3,2,1,0:T(1,128)S(1)} %get-tuple-element.327), channel_id=1, source_target_pairs={{32,0},{64,32},{96,64},{0,96},{33,1},{65,33},{97,65},{1,97},{34,2}... | collective-permute-start | bytes 12296 | tf_op jit(solution)/shard_map/ppermute | solution.py:26
  729.1 8.0 collective-permute-start.5
  749.1 14.3 collective-permute-start.16
  749.9 17.8 %collective-permute-start.17 = (f32[12,6,10,1]{0,3,2,1:T(1,128)S(1)}, f32[12,6,10,1]{0,3,2,1:T(1,128)S(1)}, u32[]{:S(2)}, u32[]{:S(2)}) collective-permute-start(f32[12,6,10,1]{0,3,2,1:T(1,128)S(1)} %copy.132), channel_id=1, source_target_pairs={{1,0},{2,1},{3,2},{4,3},{5,4},{6,5},{7,6},{0,7},{9,8},{10,9},{11,1... | collective-permute-start | bytes 8648 | tf_op jit(solution)/shard_map/ppermute | solution.py:26
  1158.0 10.6 collective-permute-start.50
  1159.1 9.5 collective-permute-start.51
  1170.7 8.6 collective-permute-start.23
  1172.7 11.4 collective-permute-start.52
  1175.0 9.2 collective-permute-start.53
  1507.7 6.8 collective-permute-start.36
  1511.0 6.9 collective-permute-start.42
  1514.5 6.8 collective-permute-start.38
  1518.0 7.7 collective-permute-start.44
  1518.0 7.6 collective-permute-start.45
  1521.5 6.6 collective-permute-start.41
  1525.8 6.8 collective-permute-start.47
  (64 other events, 1534.7 us)
where the time goes:
time: 1540 us; the launch traced here: 1530 us
  other arithmetic  929 us (60%)
  local copies, waits for them, and re-layouts  470 us (31%)
  starting transfers between devices  91.3 us (6%)
  waiting for transfers between devices  41.3 us (3%)
    scatter-add x2, other arithmetic, body(): momentum = jnp.zeros((3, extent_total), jnp.float32).at[:, wide_cell].add...  439 us
    scatter-add x2, other arithmetic, body(): counts = jnp.zeros((1, extent_total), jnp.float32).at[:, wide_cell].add(1...  427 us
    gather x4, local copies, waits for them, and re-layouts, body(): picked = reach[:, wide_cell]  297 us
    scatter x1, local copies, waits for them, and re-layouts, body(): blocks = jnp.zeros((3, 6 * CAP), jnp.float32).at[:, target].set(velocity_...  101 us
    ppermute x27, starting transfers between devices, with_halo(): lax.ppermute(lax.slice_in_dim(block, 0, width, axis=dim), axis, backward)  68.9 us
  transfers between devices with their start and end apart: 54, of which 23 were waited for; matrix products, arithmetic and copies ran while one was open for 31% of the time, Pallas kernels for 0%

commit v1 on v0

v1 whole, which is shorter than its diff:
```python
import math

import jax
import jax.numpy as jnp
from jax import lax
from jax.experimental import pallas as pl
from jax.experimental.pallas import tpu as pltpu
from jax.sharding import PartitionSpec as P

COLLOIDS_PER_UNIT = 256
CAP = 160
LANES = 128
BLOCK = 2048
SUB = 1024
CONTACT_BLOCK = 512
ANGLE = 130.0 * math.pi / 180.0
COS = math.cos(ANGLE)
ALONG = (1.0 - math.cos(ANGLE)) / 3.0
ACROSS = math.sin(ANGLE) / math.sqrt(3.0)
VMEM_LIMIT = 48 << 20


def split(x):
    high = x.astype(jnp.bfloat16).astype(jnp.float32)
    return high, x - high


def one_hot(ids, rows):
    places = lax.broadcasted_iota(jnp.int32, (rows, ids.shape[1]), 0)
    return jnp.where(places == ids, 1.0, 0.0).astype(jnp.bfloat16)


def row_mask(ids, rows):
    return lax.broadcasted_iota(jnp.int32, (rows, ids.shape[1]), 0) == ids


def spread(mask, values):
    return jnp.concatenate([jnp.where(mask, v, 0.0).astype(jnp.bfloat16) for v in values], axis=0)


def add_up(left, right):
    return lax.dot_general(
        left, right, (((1,), (1,)), ((), ())), preferred_element_type=jnp.float32
    )


def rotate(axis, v):
    e = [jnp.where((axis >> bit & 1) == 1, 1.0, -1.0) for bit in range(3)]
    d = (e[0] * v[0] + e[1] * v[1] + e[2] * v[2]) * ALONG
    return [
        COS * v[i]
        + e[i] * d
        + ACROSS * (e[(i + 1) % 3] * v[(i + 2) % 3] - e[(i + 2) % 3] * v[(i + 1) % 3])
        for i in range(3)
    ]


def cell_sums(v, cells):
    mask = row_mask(cells >> 7, 32)
    parts = [split(row) for row in v]
    ones = jnp.ones_like(v[0])
    left = spread(mask, [p[0] for p in parts] + [p[1] for p in parts] + [ones])
    return add_up(left, one_hot(cells & 127, LANES))


def mean_of(total):
    return (total[0:96] + total[96:192]) / jnp.maximum(
        jnp.concatenate([total[192:224]] * 3, axis=0), 1.0
    )


def cell_table(mean, axis):
    m = [mean[32 * i : 32 * i + 32] for i in range(3)]
    turned = rotate(axis, m)
    offset = jnp.concatenate([m[i] - turned[i] for i in range(3)], axis=0)
    high, low = split(offset)
    high = jnp.concatenate([high, axis.astype(jnp.float32)], axis=0)
    low = jnp.concatenate([low, jnp.zeros_like(m[0])], axis=0)
    return jnp.concatenate([high, low], axis=1).astype(jnp.bfloat16)


def pick(table, ids, rows):
    hot = one_hot(ids & 127, LANES)
    wide = jnp.dot(
        table, jnp.concatenate([hot, hot], axis=0), preferred_element_type=jnp.float32
    )
    mask = row_mask(ids >> 7, rows)
    return [
        jnp.sum(jnp.where(mask, wide[rows * f : rows * f + rows], 0.0), axis=0, keepdims=True)
        for f in range(wide.shape[0] // rows)
    ]


def collide(table, cells, v):
    picked = pick(table, cells, 32)
    turned = rotate(picked[3].astype(jnp.int32), v)
    return [turned[i] + picked[i] for i in range(3)]


def blocks_of(count):
    return count // BLOCK


def sum_kernel(v_ref, cells_ref, mean_ref, total):
    total[...] = jnp.zeros_like(total)

    def step(i, carry):
        for part in range(BLOCK // SUB):
            at = pl.ds(pl.multiple_of(i * BLOCK + part * SUB, SUB), SUB)
            v = [v_ref[c : c + 1, at] for c in range(3)]
            total[...] += cell_sums(v, cells_ref[0:1, at])
        return carry

    lax.fori_loop(0, blocks_of(v_ref.shape[1]), step, 0)
    mean_ref[...] = mean_of(total[...])


def turn_kernel(v_ref, cells_ref, mean_ref, axis_ref, out_ref, next_ref, total, table):
    total[...] = jnp.zeros_like(total)
    table[...] = cell_table(mean_ref[...], axis_ref[...])

    def step(i, carry):
        for part in range(BLOCK // SUB):
            at = pl.ds(pl.multiple_of(i * BLOCK + part * SUB, SUB), SUB)
            v = [v_ref[c : c + 1, at] for c in range(3)]
            new = collide(table[...], cells_ref[0:1, at], v)
            for c in range(3):
                out_ref[c : c + 1, at] = new[c]
            total[...] += cell_sums(new, cells_ref[1:2, at])
        return carry

    lax.fori_loop(0, blocks_of(v_ref.shape[1]), step, 0)
    next_ref[...] = mean_of(total[...])


def last_kernel(
    v_ref,
    cells_ref,
    mean_ref,
    axis_ref,
    dir_ref,
    slot_ref,
    particle_ref,
    place_ref,
    weight_ref,
    kept_ref,
    moved_ref,
    force_ref,
    moved,
    table,
    held,
):
    moved[...] = jnp.zeros_like(moved)
    table[...] = cell_table(mean_ref[...], axis_ref[...])
    rows = SUB // LANES

    def step(i, carry):
        for part in range(BLOCK // SUB):
            start = pl.multiple_of(i * BLOCK + part * SUB, SUB)
            at = pl.ds(start, SUB)
            v = [v_ref[c : c + 1, at] for c in range(3)]
            new = collide(table[...], cells_ref[1:2, at], v)
            code = dir_ref[0:1, at]
            key = jnp.where(code > 0, (code - 1) * 256 + slot_ref[0:1, at], 4096)
            line = pl.multiple_of(i * (BLOCK // LANES) + part * rows, rows)
            for c in range(3):
                kept_ref[c : c + 1, at] = jnp.where(code > 0, 0.0, new[c])
                held[c, pl.ds(line, rows), :] = new[c].reshape(rows, LANES)
            parts = [split(row) for row in new]
            left = spread(row_mask(key >> 7, 16), [p[0] for p in parts] + [p[1] for p in parts])
            moved[...] += add_up(left, one_hot(key & 127, LANES))
        return carry

    lax.fori_loop(0, blocks_of(v_ref.shape[1]), step, 0)
    moved_ref[...] = moved[0:48] + moved[48:96]

    lines = held.shape[1]
    high, low = split(held[...].reshape(3 * lines, LANES))
    wide = jnp.concatenate([high, low], axis=1).astype(jnp.bfloat16)
    force = jnp.zeros((128, LANES), jnp.float32)
    for part in range(particle_ref.shape[1] // CONTACT_BLOCK):
        at = slice(part * CONTACT_BLOCK, (part + 1) * CONTACT_BLOCK)
        weight = weight_ref[0:1, at]
        terms = [weight * row for row in pick(wide, particle_ref[0:1, at], lines)] + [weight]
        place = place_ref[0:1, at]
        parts = [split(row) for row in terms]
        left = spread(row_mask(place >> 7, 16), [p[0] for p in parts] + [p[1] for p in parts])
        force = force + add_up(left, one_hot(place & 127, LANES))
    force_ref[...] = force[0:64] + force[64:128]


def call(kernel, name, outs, scratch, flops, args):
    vmem = pl.BlockSpec(memory_space=pltpu.VMEM)
    return pl.pallas_call(
        kernel,
        name=name,
        out_shape=[jax.ShapeDtypeStruct(shape, jnp.float32) for shape in outs],
        in_specs=[vmem] * len(args),
        out_specs=[vmem] * len(outs),
        scratch_shapes=scratch,
        compiler_params=pltpu.CompilerParams(vmem_limit_bytes=VMEM_LIMIT),
        cost_estimate=pl.CostEstimate(flops=flops, bytes_accessed=2 << 20, transcendentals=0),
    )(*args)


def ring(axis, by):
    count = lax.axis_size(axis)
    return [(i, (i + by) % count) for i in range(count)]


def first(x, dim):
    return lax.slice_in_dim(x, 0, 1, axis=dim)


def last(x, dim):
    return lax.slice_in_dim(x, x.shape[dim] - 1, x.shape[dim], axis=dim)


def ahead(x, rim, dim):
    return jnp.concatenate([lax.slice_in_dim(x, 1, x.shape[dim], axis=dim), rim], axis=dim)


def behind(x, rim, dim):
    return jnp.concatenate([rim, lax.slice_in_dim(x, 0, x.shape[dim] - 1, axis=dim)], axis=dim)


def shifted_axes(axis_index, up):
    at = axis_index
    for dim, axis in enumerate(("gx", "gy", "gz")):
        rise = jnp.where(up[dim], at[0], at[1])
        fall = jnp.where(up[dim], at[1], at[0])
        upper = lax.ppermute(first(rise, dim), axis, ring(axis, -1))
        lower = lax.ppermute(last(fall, dim), axis, ring(axis, 1))
        rise = ahead(rise, upper, dim)
        fall = behind(fall, lower, dim)
        at = jnp.stack([jnp.where(up[dim], rise, fall), jnp.where(up[dim], fall, rise)])
    return at


def body(
    velocities,
    particle_cells,
    grid_shift,
    axis_index,
    migrate_dir,
    migrate_slot,
    contact_colloid,
    contact_particle,
    contact_weight,
    colloid_velocity,
):
    particles = velocities.shape[1]
    contacts = contact_colloid.shape[0]
    cells_x, cells_y, cells_z = axis_index.shape[1:]
    up = [grid_shift[0, dim] > 0 for dim in range(3)]

    size_x = lax.axis_size("gx")
    size_y = lax.axis_size("gy")
    size_z = lax.axis_size("gz")
    owner = contact_colloid // COLLOIDS_PER_UNIT
    apart_x = (owner // (size_y * size_z) - lax.axis_index("gx")) % size_x
    apart_y = (owner // size_z % size_y - lax.axis_index("gy")) % size_y
    apart_z = (owner % size_z - lax.axis_index("gz")) % size_z
    code = jnp.where(apart_z == 1, 5, jnp.where(apart_z == size_z - 1, 6, 0))
    code = jnp.where(apart_y == 1, 3, jnp.where(apart_y == size_y - 1, 4, code))
    code = jnp.where(apart_x == 1, 1, jnp.where(apart_x == size_x - 1, 2, code))
    place = code * COLLOIDS_PER_UNIT + contact_colloid % COLLOIDS_PER_UNIT

    axes = shifted_axes(axis_index, up).reshape(2, cells_x * cells_y, cells_z)
    total = pltpu.VMEM((224, LANES), jnp.float32)
    table = pltpu.VMEM((128, 256), jnp.bfloat16)
    pair_flops = 2 * 224 * 128 * particles
    (mean0,) = call(
        sum_kernel, "sums", [(96, LANES)], [total], pair_flops, (velocities, particle_cells)
    )
    moving, mean1 = call(
        turn_kernel,
        "turn",
        [(3, particles), (96, LANES)],
        [total, table],
        2 * pair_flops,
        (velocities, particle_cells, mean0, axes[0]),
    )
    kept, moved, force = call(
        last_kernel,
        "last",
        [(3, particles + 6 * CAP), (48, LANES), (64, LANES)],
        [
            pltpu.VMEM((96, LANES), jnp.float32),
            table,
            pltpu.VMEM((3, particles // LANES, LANES), jnp.float32),
        ],
        2 * pair_flops,
        (
            moving,
            particle_cells,
            mean1,
            axes[1],
            migrate_dir.reshape(1, particles),
            migrate_slot.reshape(1, particles),
            contact_particle.reshape(1, contacts),
            place.reshape(1, contacts),
            contact_weight.reshape(1, contacts),
        ),
    )
    moved = moved.reshape(3, 16, LANES)
    force = force.reshape(4, 16, LANES)
    mean = mean1.reshape(3, cells_x, cells_y, cells_z)
    sums = force[:, 0:2].reshape(4, COLLOIDS_PER_UNIT)
    arrivals = []
    for dim, axis in enumerate(("gx", "gy", "gz")):
        rims = (last(mean, dim + 1), first(mean, dim + 1))
        got = []
        for side, by in enumerate((1, -1)):
            number = 2 * dim + side
            sent = jnp.concatenate(
                [
                    moved[:, 2 * number : 2 * number + 2].reshape(-1),
                    force[:, 2 * number + 2 : 2 * number + 4].reshape(-1),
                    rims[side].reshape(-1),
                ]
            )
            came = lax.ppermute(sent, axis, ring(axis, by))
            arrivals.append(came[0:768].reshape(3, 256)[:, :CAP])
            sums = sums + came[768:1792].reshape(4, COLLOIDS_PER_UNIT)
            got.append(came[1792:].reshape(rims[side].shape))
        mean = jnp.where(up[dim], ahead(mean, got[1], dim + 1), behind(mean, got[0], dim + 1))
    migrated = lax.dynamic_update_slice(kept, jnp.concatenate(arrivals, axis=1), (0, particles))
    colloid_force = (sums[0:3] - sums[3:4] * colloid_velocity) / jnp.maximum(sums[3:4], 1.0)
    return (mean, migrated, colloid_force)


def solution(mesh):
    flat = P(("gx", "gy", "gz"))
    tall = P(None, ("gx", "gy", "gz"))
    grid = P(None, "gx", "gy", "gz")
    return jax.shard_map(
        body,
        mesh=mesh,
        in_specs=(tall, tall, P(), grid, flat, flat, flat, flat, flat, tall),
        out_specs=(grid, tall, tall),
        check_vma=False,
    )
```

time: 1540 us -> 94.6 us (0.06)
  other arithmetic: 929 us -> 2.3 us
  local copies, waits for them, and re-layouts: 470 us -> 7.64 us
  starting transfers between devices: 91.3 us -> 17.4 us
  Pallas kernels: 0 us -> 49.1 us
  waiting for transfers between devices: 41.3 us -> 14.4 us
    scatter-add x6 -> x0, other arithmetic: 902 us -> none  [the longest x2 439 us: body(): momentum = jnp.zeros((3, extent_total), jnp.float32).at[:, wide_cell].add...]
    gather x4 -> x0, local copies, waits for them, and re-layouts: 297 us -> none  [body(): picked = reach[:, wide_cell]]
    scatter x19 -> x0, local copies, waits for them, and re-layouts: 101 us -> none  [the longest x1 101 us: body(): blocks = jnp.zeros((3, 6 * CAP), jnp.float32).at[:, target].set(velocity_...]
    ppermute x54 -> x12, starting transfers between devices: 91.3 us -> 17.4 us  [the longest x6 8.93 us: body(): came = lax.ppermute(sent, axis, ring(axis, by))]
    pallas_call x0 -> x3, Pallas kernels: none -> 49.1 us  [call(): pl.pallas_call(kernel, name=name, out_shape=[jax.ShapeDtypeStruct(shape,...]
    add x3 -> x0, local copies, waits for them, and re-layouts: 30.1 us -> none  [body(): velocity_now = apply_rotation(picked[:9], velocity_now) + picked[9:]]
    ppermute x54 -> x12, waiting for transfers between devices: 41.3 us -> 14.4 us  [the longest x6 6.63 us: body(): came = lax.ppermute(sent, axis, ring(axis, by))]
  transfers between devices with their start and end apart: 54 -> 12, of which waited for: 23 -> 8; matrix products, arithmetic and copies ran while one was open for 31% -> 1% of each run, Pallas kernels for 0% -> 9%
where the time goes in v1:
time: 94.6 us; the launch traced here: 93.8 us
  Pallas kernels  49.1 us (52%)
  starting transfers between devices  17.4 us (18%)
  waiting for transfers between devices  14.4 us (15%)
  local copies, waits for them, and re-layouts  7.64 us (8%)
  between operations  3 us (3%)
  other arithmetic  2.3 us (2%)
    pallas_call x3, Pallas kernels, call(): pl.pallas_call(kernel, name=name, out_shape=[jax.ShapeDtypeStruct(shape,...  49.1 us
    ppermute x6, starting transfers between devices, body(): came = lax.ppermute(sent, axis, ring(axis, by))  8.93 us
    ppermute x3, starting transfers between devices, shifted_axes(): upper = lax.ppermute(first(rise, dim), axis, ring(axis, -1))  7.49 us
    ppermute x6, waiting for transfers between devices, body(): came = lax.ppermute(sent, axis, ring(axis, by))  6.63 us
    ppermute x3, waiting for transfers between devices, shifted_axes(): lower = lax.ppermute(last(fall, dim), axis, ring(axis, 1))  4.76 us
    unnamed x19, local copies, waits for them, and re-layouts  4.3 us
    ppermute x3, waiting for transfers between devices, shifted_axes(): upper = lax.ppermute(first(rise, dim), axis, ring(axis, -1))  3.05 us
  transfers between devices with their start and end apart: 12, of which 8 were waited for; matrix products, arithmetic and copies ran while one was open for 1% of the time, Pallas kernels for 9%

profile of v1, /device:TPU:6, one launch (start us, length us, event | category | flops | bytes accessed | tf_op | source)
XLA Modules:
  0.0 93.8 jit_solution(12420189021231395856)
XLA Ops:
  0.6 1.4 %fusion.26 = (s32[1,1]{1,0:T(1,128)}, s32[1,1]{1,0:T(1,128)}, s32[1,1]{1,0:T(1,128)}) fusion(s32[2,3]{1,0:T(2,128)} %param.12), kind=kLoop, calls=%fused_computation.95 | loop fusion | bytes 24 | tf_op jit(solution)/shard_map/slice | solution.py:255
  2.7 0.7 slice_select_fusion.1
  3.4 3.3 %collective-permute-start = (s32[1,8,128]{2,1,0:T(8,128)S(1)}, s32[1,8,128]{2,1,0:T(8,128)S(1)}, u32[]{:S(2)}, u32[]{:S(2)}) collective-permute-start(s32[1,8,128]{2,1,0:T(8,128)S(1)} %slice_bitcast_fusion.10), channel_id=1, source_target_pairs={{0,96},{32,0},{64,32},{96,64},{1,97},{33,1},{65,33},{97,65},{2,98}... | collective-permute-start | bytes 12296 | tf_op jit(solution)/shard_map/ppermute | solution.py:232
  6.7 0.7 copy-done.7
  8.1 3.1 %collective-permute-done.1 = s32[1,8,128]{2,1,0:T(8,128)S(1)} collective-permute-done((s32[1,8,128]{2,1,0:T(8,128)S(1)}, s32[1,8,128]{2,1,0:T(8,128)S(1)}, u32[]{:S(2)}, u32[]{:S(2)}) %collective-permute-start.1) | collective-permute-done | bytes 4128 | tf_op jit(solution)/shard_map/ppermute | solution.py:233
  11.3 3.1 %collective-permute-start.2 = (s32[4,1,128]{2,1,0:T(1,128)S(1)}, s32[4,1,128]{2,1,0:T(1,128)S(1)}, u32[]{:S(2)}, u32[]{:S(2)}) collective-permute-start(s32[4,1,128]{2,1,0:T(1,128)S(1)} %slice.404), channel_id=1, source_target_pairs={{0,24},{8,0},{16,8},{24,16},{1,25},{9,1},{17,9},{25,17},{2,26},{10... | collective-permute-start | bytes 6152 | tf_op jit(solution)/shard_map/ppermute | solution.py:232
  14.4 1.1 %copy-done = f32[3,40960]{1,0:T(4,128)S(1)} copy-done((f32[3,40960]{1,0:T(4,128)S(1)}, f32[3,40960]{1,0:T(4,128)}, u32[]{:S(2)}) %copy-start) | copy-done | bytes 491544
  15.5 1.0 %copy-done.1 = s32[2,40960]{1,0:T(2,128)S(1)} copy-done((s32[2,40960]{1,0:T(2,128)S(1)}, s32[2,40960]{1,0:T(2,128)}, u32[]{:S(2)}) %copy-start.1) | copy-done | bytes 327704
  16.4 8.3 %sums.1.mean_ref = f32[96,128]{1,0:T(8,128)S(1)} custom-call(f32[3,40960]{1,0:T(4,128)S(1)} %copy-done, s32[2,40960]{1,0:T(2,128)S(1)} %copy-done.1), custom_call_target="tpu_custom_call" | custom-call | flops 2348810240 | bytes 2097152 | tf_op jit(solution)/shard_map/sums/pallas_call | solution.py:194
  25.5 1.0 %collective-permute-start.5 = (s32[4,8,1]{2,1,0:T(8,128)S(1)}, s32[4,8,1]{2,1,0:T(8,128)S(1)}, u32[]{:S(2)}, u32[]{:S(2)}) collective-permute-start(s32[4,8,1]{2,1,0:T(8,128)S(1)} %slice.409), channel_id=1, source_target_pairs={{0,1},{1,2},{2,3},{3,4},{4,5},{5,6},{6,7},{7,0},{8,9},{9,10},{10,1... | collective-permute-start | bytes 392 | tf_op jit(solution)/shard_map/ppermute | solution.py:233
  26.4 1.1 %collective-permute-start.4 = (s32[4,8,1]{2,1,0:T(8,128)S(1)}, s32[4,8,1]{2,1,0:T(8,128)S(1)}, u32[]{:S(2)}, u32[]{:S(2)}) collective-permute-start(s32[4,8,1]{2,1,0:T(8,128)S(1)} %bitcast.91), channel_id=1, source_target_pairs={{0,7},{1,0},{2,1},{3,2},{4,3},{5,4},{6,5},{7,6},{8,15},{9,8},{10,9... | collective-permute-start | bytes 392 | tf_op jit(solution)/shard_map/ppermute | solution.py:232
  27.6 1.6 %collective-permute-done.5 = s32[4,8,1]{2,1,0:T(8,128)S(1)} collective-permute-done((s32[4,8,1]{2,1,0:T(8,128)S(1)}, s32[4,8,1]{2,1,0:T(8,128)S(1)}, u32[]{:S(2)}, u32[]{:S(2)}) %collective-permute-start.5) | collective-permute-done | bytes 160 | tf_op jit(solution)/shard_map/ppermute | solution.py:233
  29.2 3.0 %collective-permute-done.4 = s32[4,8,1]{2,1,0:T(8,128)S(1)} collective-permute-done((s32[4,8,1]{2,1,0:T(8,128)S(1)}, s32[4,8,1]{2,1,0:T(8,128)S(1)}, u32[]{:S(2)}, u32[]{:S(2)}) %collective-permute-start.4) | collective-permute-done | bytes 160 | tf_op jit(solution)/shard_map/ppermute | solution.py:232
  32.4 21.9 %turn.1 = (f32[3,40960]{1,0:T(4,128)S(1)}, f32[96,128]{1,0:T(8,128)S(1)}) custom-call(f32[3,40960]{1,0:T(4,128)S(1)} %copy-done, s32[2,40960]{1,0:T(2,128)S(1)} %copy-done.1, f32[96,128]{1,0:T(8,128)S(1)} %sums.1.mean_ref, s32[32,128]{1,0:T(8,128)S(1)} %get-tuple-element.18.axis_ref), custom_call_target="tpu_custom_call" | custom-call | flops 4697620480 | bytes 2097152 | tf_op jit(solution)/shard_map/turn/pallas_call | solution.py:194
  54.4 0.8 copy-done.3
  55.2 18.8 %last.1 = (f32[3,41920]{1,0:T(4,128)}, f32[48,128]{1,0:T(8,128)S(1)}, f32[64,128]{1,0:T(8,128)S(1)}) custom-call(f32[3,40960]{1,0:T(4,128)S(1)} %get-tuple-element.9.v_ref, s32[2,40960]{1,0:T(2,128)S(1)} %copy-done.2, f32[96,128]{1,0:T(8,128)S(1)} %get-tuple-element.8.mean_ref, s32[32,128]{1,0:T(8,128)S(1)} %get-tuple-element.17.axis_ref, ...), custom_call_target="tpu_custom_call" | custom-call | flops 4697620480 | bytes 2097152 | tf_op jit(solution)/shard_map/last/pallas_call | solution.py:194
  74.3 3.3 %collective-permute-start.6 = (f32[4864]{0:T(1024)S(1)}, f32[4864]{0:T(1024)S(1)}, u32[]{:S(2)}, u32[]{:S(2)}) collective-permute-start(f32[4864]{0:T(1024)S(1)} %pad_maximum_fusion), channel_id=1, source_target_pairs={{0,96},{32,0},{64,32},{96,64},{1,97},{33,1},{65,33},{97,65},{2,98}... | collective-permute-start | bytes 58376 | tf_op jit(solution)/shard_map/ppermute | solution.py:323
  77.6 1.3 %collective-permute-done.7 = f32[4864]{0:T(1024)S(1)} collective-permute-done((f32[4864]{0:T(1024)S(1)}, f32[4864]{0:T(1024)S(1)}, u32[]{:S(2)}, u32[]{:S(2)}) %collective-permute-start.7) | collective-permute-done | bytes 19488 | tf_op jit(solution)/shard_map/ppermute | solution.py:323
  79.8 2.7 %collective-permute-start.8 = (f32[3328]{0:T(1024)S(1)}, f32[3328]{0:T(1024)S(1)}, u32[]{:S(2)}, u32[]{:S(2)}) collective-permute-start(f32[3328]{0:T(1024)S(1)} %pad_maximum_fusion.2), channel_id=1, source_target_pairs={{0,24},{8,0},{16,8},{24,16},{1,25},{9,1},{17,9},{25,17},{2,26},{10... | collective-permute-start | bytes 39944 | tf_op jit(solution)/shard_map/ppermute | solution.py:323
  82.6 1.5 %collective-permute-done.9 = f32[3328]{0:T(1024)S(1)} collective-permute-done((f32[3328]{0:T(1024)S(1)}, f32[3328]{0:T(1024)S(1)}, u32[]{:S(2)}, u32[]{:S(2)}) %collective-permute-start.9) | collective-permute-done | bytes 13344 | tf_op jit(solution)/shard_map/ppermute | solution.py:323
  84.8 2.0 %collective-permute-start.10 = (f32[1888]{0:T(1024)S(1)}, f32[1888]{0:T(1024)S(1)}, u32[]{:S(2)}, u32[]{:S(2)}) collective-permute-start(f32[1888]{0:T(1024)S(1)} %pad_maximum_fusion.4), channel_id=1, source_target_pairs={{0,7},{1,0},{2,1},{3,2},{4,3},{5,4},{6,5},{7,6},{8,15},{9,8},{10,9... | collective-permute-start | bytes 22664 | tf_op jit(solution)/shard_map/ppermute | solution.py:323
  86.9 1.3 %collective-permute-done.11 = f32[1888]{0:T(1024)S(1)} collective-permute-done((f32[1888]{0:T(1024)S(1)}, f32[1888]{0:T(1024)S(1)}, u32[]{:S(2)}, u32[]{:S(2)}) %collective-permute-start.11) | collective-permute-done | bytes 7584 | tf_op jit(solution)/shard_map/ppermute | solution.py:323
  88.2 2.4 %collective-permute-done.10 = f32[1888]{0:T(1024)S(1)} collective-permute-done((f32[1888]{0:T(1024)S(1)}, f32[1888]{0:T(1024)S(1)}, u32[]{:S(2)}, u32[]{:S(2)}) %collective-permute-start.10) | collective-permute-done | bytes 7584 | tf_op jit(solution)/shard_map/ppermute | solution.py:323
  93.1 0.7 maximum_select_fusion.2
  (102 shorter events, 4.6 us)
Async XLA Ops:
  3.4 4.7 %collective-permute-start = (s32[1,8,128]{2,1,0:T(8,128)S(1)}, s32[1,8,128]{2,1,0:T(8,128)S(1)}, u32[]{:S(2)}, u32[]{:S(2)}) collective-permute-start(s32[1,8,128]{2,1,0:T(8,128)S(1)} %slice_bitcast_fusion.10), channel_id=1, source_target_pairs={{0,96},{32,0},{64,32},{96,64},{1,97},{33,1},{65,33},{97,65},{2,98}... | collective-permute-start | bytes 12296 | tf_op jit(solution)/shard_map/ppermute | solution.py:232
  6.7 4.5 %collective-permute-start.1 = (s32[1,8,128]{2,1,0:T(8,128)S(1)}, s32[1,8,128]{2,1,0:T(8,128)S(1)}, u32[]{:S(2)}, u32[]{:S(2)}) collective-permute-start(s32[1,8,128]{2,1,0:T(8,128)S(1)} %slice_bitcast_fusion.9), channel_id=1, source_target_pairs={{0,32},{32,64},{64,96},{96,0},{1,33},{33,65},{65,97},{97,1},{2,34}... | collective-permute-start | bytes 12296 | tf_op jit(solution)/shard_map/ppermute | solution.py:233
  6.7 0.7 copy-start.7
  11.3 14.1 %collective-permute-start.2 = (s32[4,1,128]{2,1,0:T(1,128)S(1)}, s32[4,1,128]{2,1,0:T(1,128)S(1)}, u32[]{:S(2)}, u32[]{:S(2)}) collective-permute-start(s32[4,1,128]{2,1,0:T(1,128)S(1)} %slice.404), channel_id=1, source_target_pairs={{0,24},{8,0},{16,8},{24,16},{1,25},{9,1},{17,9},{25,17},{2,26},{10... | collective-permute-start | bytes 6152 | tf_op jit(solution)/shard_map/ppermute | solution.py:232
  14.4 11.0 %collective-permute-start.3 = (s32[4,1,128]{2,1,0:T(1,128)S(1)}, s32[4,1,128]{2,1,0:T(1,128)S(1)}, u32[]{:S(2)}, u32[]{:S(2)}) collective-permute-start(s32[4,1,128]{2,1,0:T(1,128)S(1)} %slice.405), channel_id=1, source_target_pairs={{0,8},{8,16},{16,24},{24,0},{1,9},{9,17},{17,25},{25,1},{2,10},{10... | collective-permute-start | bytes 6152 | tf_op jit(solution)/shard_map/ppermute | solution.py:233
  14.4 1.1 %copy-start = (f32[3,40960]{1,0:T(4,128)S(1)}, f32[3,40960]{1,0:T(4,128)}, u32[]{:S(2)}) copy-start(f32[3,40960]{1,0:T(4,128)} %v_ref.3) | copy-start | bytes 1474564
  15.5 1.0 %copy-start.1 = (s32[2,40960]{1,0:T(2,128)S(1)}, s32[2,40960]{1,0:T(2,128)}, u32[]{:S(2)}) copy-start(s32[2,40960]{1,0:T(2,128)} %cells_ref.5) | copy-start | bytes 983044
  25.5 3.8 %collective-permute-start.5 = (s32[4,8,1]{2,1,0:T(8,128)S(1)}, s32[4,8,1]{2,1,0:T(8,128)S(1)}, u32[]{:S(2)}, u32[]{:S(2)}) collective-permute-start(s32[4,8,1]{2,1,0:T(8,128)S(1)} %slice.409), channel_id=1, source_target_pairs={{0,1},{1,2},{2,3},{3,4},{4,5},{5,6},{6,7},{7,0},{8,9},{9,10},{10,1... | collective-permute-start | bytes 392 | tf_op jit(solution)/shard_map/ppermute | solution.py:233
  26.4 5.8 %collective-permute-start.4 = (s32[4,8,1]{2,1,0:T(8,128)S(1)}, s32[4,8,1]{2,1,0:T(8,128)S(1)}, u32[]{:S(2)}, u32[]{:S(2)}) collective-permute-start(s32[4,8,1]{2,1,0:T(8,128)S(1)} %bitcast.91), channel_id=1, source_target_pairs={{0,7},{1,0},{2,1},{3,2},{4,3},{5,4},{6,5},{7,6},{8,15},{9,8},{10,9... | collective-permute-start | bytes 392 | tf_op jit(solution)/shard_map/ppermute | solution.py:232
  32.4 22.0 %copy-start.2 = (s32[2,40960]{1,0:T(2,128)S(1)}, s32[2,40960]{1,0:T(2,128)}, u32[]{:S(2)}) copy-start(s32[2,40960]{1,0:T(2,128)} %cells_ref.5) | copy-start | bytes 983044
  32.4 22.0 %copy-start.4 = (s32[40960]{0:T(1024)S(1)}, s32[40960]{0:T(1024)}, u32[]{:S(2)}) copy-start(s32[40960]{0:T(1024)} %param.15) | copy-start | bytes 491524
  54.3 0.9 copy-start.3
  54.3 0.9 copy-start.6
  54.4 0.9 copy-start.5
  74.2 4.8 %collective-permute-start.7 = (f32[4864]{0:T(1024)S(1)}, f32[4864]{0:T(1024)S(1)}, u32[]{:S(2)}, u32[]{:S(2)}) collective-permute-start(f32[4864]{0:T(1024)S(1)} %pad_maximum_fusion.1), channel_id=1, source_target_pairs={{0,32},{32,64},{64,96},{96,0},{1,33},{33,65},{65,97},{97,1},{2,34}... | collective-permute-start | bytes 58376 | tf_op jit(solution)/shard_map/ppermute | solution.py:323
  74.3 4.8 %collective-permute-start.6 = (f32[4864]{0:T(1024)S(1)}, f32[4864]{0:T(1024)S(1)}, u32[]{:S(2)}, u32[]{:S(2)}) collective-permute-start(f32[4864]{0:T(1024)S(1)} %pad_maximum_fusion), channel_id=1, source_target_pairs={{0,96},{32,0},{64,32},{96,64},{1,97},{33,1},{65,33},{97,65},{2,98}... | collective-permute-start | bytes 58376 | tf_op jit(solution)/shard_map/ppermute | solution.py:323
  79.1 5.0 %collective-permute-start.9 = (f32[3328]{0:T(1024)S(1)}, f32[3328]{0:T(1024)S(1)}, u32[]{:S(2)}, u32[]{:S(2)}) collective-permute-start(f32[3328]{0:T(1024)S(1)} %pad_maximum_fusion.3), channel_id=1, source_target_pairs={{0,8},{8,16},{16,24},{24,0},{1,9},{9,17},{17,25},{25,1},{2,10},{10... | collective-permute-start | bytes 39944 | tf_op jit(solution)/shard_map/ppermute | solution.py:323
  79.8 4.4 %collective-permute-start.8 = (f32[3328]{0:T(1024)S(1)}, f32[3328]{0:T(1024)S(1)}, u32[]{:S(2)}, u32[]{:S(2)}) collective-permute-start(f32[3328]{0:T(1024)S(1)} %pad_maximum_fusion.2), channel_id=1, source_target_pairs={{0,24},{8,0},{16,8},{24,16},{1,25},{9,1},{17,9},{25,17},{2,26},{10... | collective-permute-start | bytes 39944 | tf_op jit(solution)/shard_map/ppermute | solution.py:323
  84.5 3.7 %collective-permute-start.11 = (f32[1888]{0:T(1024)S(1)}, f32[1888]{0:T(1024)S(1)}, u32[]{:S(2)}, u32[]{:S(2)}) collective-permute-start(f32[1888]{0:T(1024)S(1)} %pad_maximum_fusion.5), channel_id=1, source_target_pairs={{0,1},{1,2},{2,3},{3,4},{4,5},{5,6},{6,7},{7,0},{8,9},{9,10},{10,1... | collective-permute-start | bytes 22664 | tf_op jit(solution)/shard_map/ppermute | solution.py:323
  84.8 5.8 %collective-permute-start.10 = (f32[1888]{0:T(1024)S(1)}, f32[1888]{0:T(1024)S(1)}, u32[]{:S(2)}, u32[]{:S(2)}) collective-permute-start(f32[1888]{0:T(1024)S(1)} %pad_maximum_fusion.4), channel_id=1, source_target_pairs={{0,7},{1,0},{2,1},{3,2},{4,3},{5,4},{6,5},{7,6},{8,15},{9,8},{10,9... | collective-permute-start | bytes 22664 | tf_op jit(solution)/shard_map/ppermute | solution.py:323
  91.8 0.7 copy-start.8

commit v2 on v1

--- a/solution.py
+++ b/solution.py
@@ -10,9 +10,7 @@
 COLLOIDS_PER_UNIT = 256
 CAP = 160
 LANES = 128
-BLOCK = 2048
-SUB = 1024
-CONTACT_BLOCK = 512
+UNROLL = 4
 ANGLE = 130.0 * math.pi / 180.0
 COS = math.cos(ANGLE)
 ALONG = (1.0 - math.cos(ANGLE)) / 3.0
@@ -25,23 +23,37 @@
     return high, x - high
 
 
-def one_hot(ids, rows):
-    places = lax.broadcasted_iota(jnp.int32, (rows, ids.shape[1]), 0)
-    return jnp.where(places == ids, 1.0, 0.0).astype(jnp.bfloat16)
-
-
-def row_mask(ids, rows):
-    return lax.broadcasted_iota(jnp.int32, (rows, ids.shape[1]), 0) == ids
-
-
-def spread(mask, values):
-    return jnp.concatenate([jnp.where(mask, v, 0.0).astype(jnp.bfloat16) for v in values], axis=0)
+def places(rows):
+    return lax.broadcasted_iota(jnp.int32, (rows, LANES), 0).astype(jnp.float32).astype(jnp.bfloat16)
+
+
+def narrow(row, rows):
+    part = jnp.broadcast_to(row, (16, LANES)).astype(jnp.bfloat16)
+    return jnp.concatenate([part] * (rows // 16), axis=0)
+
+
+def one_hot(row, lanes):
+    one, zero = jnp.asarray(1, jnp.bfloat16), jnp.asarray(0, jnp.bfloat16)
+    return jnp.where(lanes == narrow(row, LANES), one, zero)
 
 
 def add_up(left, right):
     return lax.dot_general(
         left, right, (((1,), (1,)), ((), ())), preferred_element_type=jnp.float32
     )
+
+
+def fold(parts):
+    rows = lax.broadcasted_iota(jnp.int32, parts[0].shape, 0)
+    step = len(parts) // 2
+    while step:
+        low = (rows & step) == 0
+        parts = [
+            jnp.where(low, p + pltpu.roll(p, 8 - step, 0), q + pltpu.roll(q, step, 0))
+            for p, q in zip(parts[:step], parts[step:])
+        ]
+        step //= 2
+    return parts[0]
 
 
 def rotate(axis, v):
@@ -55,12 +67,22 @@
     ]
 
 
-def cell_sums(v, cells):
-    mask = row_mask(cells >> 7, 32)
-    parts = [split(row) for row in v]
-    ones = jnp.ones_like(v[0])
-    left = spread(mask, [p[0] for p in parts] + [p[1] for p in parts] + [ones])
-    return add_up(left, one_hot(cells & 127, LANES))
+def scatter(values, ids, rows, counted, lanes):
+    low = (ids & (LANES - 1)).astype(jnp.float32)
+    line = (ids >> 7).astype(jnp.float32)
+    parts = [split(x) for x in values]
+    parts = [p[0] for p in parts] + [p[1] for p in parts]
+    spots = places(rows)
+    one, zero = jnp.asarray(1, jnp.bfloat16), jnp.asarray(0, jnp.bfloat16)
+    left, right = [], []
+    for j in range(8):
+        mask = spots == narrow(line[j : j + 1], rows)
+        lines = [jnp.where(mask, narrow(x[j : j + 1], rows), zero) for x in parts]
+        if counted:
+            lines.append(jnp.where(mask, one, zero))
+        left.append(jnp.concatenate(lines, axis=0))
+        right.append(one_hot(low[j : j + 1], lanes))
+    return add_up(jnp.concatenate(left, axis=1), jnp.concatenate(right, axis=1))
 
 
 def mean_of(total):
@@ -79,39 +101,46 @@
     return jnp.concatenate([high, low], axis=1).astype(jnp.bfloat16)
 
 
-def pick(table, ids, rows):
-    hot = one_hot(ids & 127, LANES)
-    wide = jnp.dot(
-        table, jnp.concatenate([hot, hot], axis=0), preferred_element_type=jnp.float32
-    )
-    mask = row_mask(ids >> 7, rows)
-    return [
-        jnp.sum(jnp.where(mask, wide[rows * f : rows * f + rows], 0.0), axis=0, keepdims=True)
-        for f in range(wide.shape[0] // rows)
-    ]
-
-
-def collide(table, cells, v):
-    picked = pick(table, cells, 32)
+def pick(table, ids, rows, lanes):
+    low = (ids & (LANES - 1)).astype(jnp.float32)
+    line = ids >> 7
+    spots = lax.broadcasted_iota(jnp.int32, (rows, LANES), 0)
+    count = table.shape[0] // rows
+    parts = [[] for _ in range(count)]
+    for j in range(0, 8, 2):
+        hot = jnp.concatenate([one_hot(low[j + k : j + k + 1], lanes) for k in range(2)], axis=1)
+        wide = jnp.dot(
+            table, jnp.concatenate([hot, hot], axis=0), preferred_element_type=jnp.float32
+        )
+        for k in range(2):
+            mask = spots == jnp.broadcast_to(line[j + k : j + k + 1], (rows, LANES))
+            for f in range(count):
+                found = wide[rows * f : rows * f + rows, k * LANES : (k + 1) * LANES]
+                found = jnp.where(mask, found, 0.0)
+                parts[f].append(jnp.sum(found.reshape(rows // 8, 8, LANES), axis=0))
+    return [fold(p) for p in parts]
+
+
+def collide(table, cells, v, lanes):
+    picked = pick(table, cells, 32, lanes)
     turned = rotate(picked[3].astype(jnp.int32), v)
     return [turned[i] + picked[i] for i in range(3)]
 
 
-def blocks_of(count):
-    return count // BLOCK
-
-
 def sum_kernel(v_ref, cells_ref, mean_ref, total):
     total[...] = jnp.zeros_like(total)
 
     def step(i, carry):
-        for part in range(BLOCK // SUB):
-            at = pl.ds(pl.multiple_of(i * BLOCK + part * SUB, SUB), SUB)
-            v = [v_ref[c : c + 1, at] for c in range(3)]
-            total[...] += cell_sums(v, cells_ref[0:1, at])
+        lanes = places(LANES)
+        added = 0.0
+        for part in range(UNROLL):
+            at = pl.ds(pl.multiple_of((i * UNROLL + part) * 8, 8), 8)
+            v = [v_ref[at, c, :] for c in range(3)]
+            added += scatter(v, cells_ref[at, 0, :], 32, True, lanes)
+        total[...] += added
         return carry
 
-    lax.fori_loop(0, blocks_of(v_ref.shape[1]), step, 0)
+    lax.fori_loop(0, v_ref.shape[0] // (8 * UNROLL), step, 0)
     mean_ref[...] = mean_of(total[...])
 
 
@@ -120,16 +149,19 @@
     table[...] = cell_table(mean_ref[...], axis_ref[...])
 
     def step(i, carry):
-        for part in range(BLOCK // SUB):
-            at = pl.ds(pl.multiple_of(i * BLOCK + part * SUB, SUB), SUB)
-            v = [v_ref[c : c + 1, at] for c in range(3)]
-            new = collide(table[...], cells_ref[0:1, at], v)
+        lanes = places(LANES)
+        added = 0.0
+        for part in range(UNROLL):
+            at = pl.ds(pl.multiple_of((i * UNROLL + part) * 8, 8), 8)
+            v = [v_ref[at, c, :] for c in range(3)]
+            new = collide(table[...], cells_ref[at, 0, :], v, lanes)
             for c in range(3):
-                out_ref[c : c + 1, at] = new[c]
-            total[...] += cell_sums(new, cells_ref[1:2, at])
+                out_ref[c, at, :] = new[c]
+            added += scatter(new, cells_ref[at, 1, :], 32, True, lanes)
+        total[...] += added
         return carry
 
-    lax.fori_loop(0, blocks_of(v_ref.shape[1]), step, 0)
+    lax.fori_loop(0, v_ref.shape[0] // (8 * UNROLL), step, 0)
     next_ref[...] = mean_of(total[...])
 
 
@@ -152,40 +184,39 @@
 ):
     moved[...] = jnp.zeros_like(moved)
     table[...] = cell_table(mean_ref[...], axis_ref[...])
-    rows = SUB // LANES
 
     def step(i, carry):
-        for part in range(BLOCK // SUB):
-            start = pl.multiple_of(i * BLOCK + part * SUB, SUB)
-            at = pl.ds(start, SUB)
-            v = [v_ref[c : c + 1, at] for c in range(3)]
-            new = collide(table[...], cells_ref[1:2, at], v)
-            code = dir_ref[0:1, at]
-            key = jnp.where(code > 0, (code - 1) * 256 + slot_ref[0:1, at], 4096)
-            line = pl.multiple_of(i * (BLOCK // LANES) + part * rows, rows)
+        lanes = places(LANES)
+        added = 0.0
+        for part in range(UNROLL):
+            line = pl.multiple_of((i * UNROLL + part) * 8, 8)
+            at = pl.ds(line, 8)
+            v = [v_ref[c, at, :] for c in range(3)]
+            new = collide(table[...], cells_ref[at, 1, :], v, lanes)
+            code = dir_ref[at, :]
             for c in range(3):
-                kept_ref[c : c + 1, at] = jnp.where(code > 0, 0.0, new[c])
-                held[c, pl.ds(line, rows), :] = new[c].reshape(rows, LANES)
-            parts = [split(row) for row in new]
-            left = spread(row_mask(key >> 7, 16), [p[0] for p in parts] + [p[1] for p in parts])
-            moved[...] += add_up(left, one_hot(key & 127, LANES))
+                held[c, at, :] = new[c]
+                kept = jnp.where(code > 0, 0.0, new[c])
+                for j in range(8):
+                    kept_ref[c : c + 1, pl.ds((line + j) * LANES, LANES)] = kept[j : j + 1]
+            key = jnp.where(code > 0, (code - 1) * 256 + slot_ref[at, :], 4096)
+            added += scatter(new, key, 16, False, lanes)
+        moved[...] += added
         return carry
 
-    lax.fori_loop(0, blocks_of(v_ref.shape[1]), step, 0)
+    lax.fori_loop(0, v_ref.shape[1] // (8 * UNROLL), step, 0)
     moved_ref[...] = moved[0:48] + moved[48:96]
 
     lines = held.shape[1]
     high, low = split(held[...].reshape(3 * lines, LANES))
     wide = jnp.concatenate([high, low], axis=1).astype(jnp.bfloat16)
+    lanes = places(LANES)
     force = jnp.zeros((128, LANES), jnp.float32)
-    for part in range(particle_ref.shape[1] // CONTACT_BLOCK):
-        at = slice(part * CONTACT_BLOCK, (part + 1) * CONTACT_BLOCK)
-        weight = weight_ref[0:1, at]
-        terms = [weight * row for row in pick(wide, particle_ref[0:1, at], lines)] + [weight]
-        place = place_ref[0:1, at]
-        parts = [split(row) for row in terms]
-        left = spread(row_mask(place >> 7, 16), [p[0] for p in parts] + [p[1] for p in parts])
-        force = force + add_up(left, one_hot(place & 127, LANES))
+    for part in range(particle_ref.shape[0] // 8):
+        at = slice(8 * part, 8 * part + 8)
+        weight = weight_ref[at, :]
+        terms = [weight * x for x in pick(wide, particle_ref[at, :], lines, lanes)] + [weight]
+        force = force + scatter(terms, place_ref[at, :], 16, False, lanes)
     force_ref[...] = force[0:64] + force[64:128]
 
 
@@ -250,7 +281,6 @@
     colloid_velocity,
 ):
     particles = velocities.shape[1]
-    contacts = contact_colloid.shape[0]
     cells_x, cells_y, cells_z = axis_index.shape[1:]
     up = [grid_shift[0, dim] > 0 for dim in range(3)]
 
@@ -267,19 +297,22 @@
     place = code * COLLOIDS_PER_UNIT + contact_colloid % COLLOIDS_PER_UNIT
 
     axes = shifted_axes(axis_index, up).reshape(2, cells_x * cells_y, cells_z)
+    lines = particles // LANES
+    velocity = velocities.reshape(3, lines, LANES).transpose(1, 0, 2)
+    cells = particle_cells.reshape(2, lines, LANES).transpose(1, 0, 2)
     total = pltpu.VMEM((224, LANES), jnp.float32)
     table = pltpu.VMEM((128, 256), jnp.bfloat16)
     pair_flops = 2 * 224 * 128 * particles
     (mean0,) = call(
-        sum_kernel, "sums", [(96, LANES)], [total], pair_flops, (velocities, particle_cells)
+        sum_kernel, "sums", [(96, LANES)], [total], pair_flops, (velocity, cells)
     )
     moving, mean1 = call(
         turn_kernel,
         "turn",
-        [(3, particles), (96, LANES)],
+        [(3, lines, LANES), (96, LANES)],
         [total, table],
         2 * pair_flops,
-        (velocities, particle_cells, mean0, axes[0]),
+        (velocity, cells, mean0, axes[0]),
     )
     kept, moved, force = call(
         last_kernel,
@@ -288,19 +321,19 @@
         [
             pltpu.VMEM((96, LANES), jnp.float32),
             table,
-            pltpu.VMEM((3, particles // LANES, LANES), jnp.float32),
+            pltpu.VMEM((3, lines, LANES), jnp.float32),
         ],
         2 * pair_flops,
         (
             moving,
-            particle_cells,
+            cells,
             mean1,
             axes[1],
-            migrate_dir.reshape(1, particles),
-            migrate_slot.reshape(1, particles),
-            contact_particle.reshape(1, contacts),
-            place.reshape(1, contacts),
-            contact_weight.reshape(1, contacts),
+            migrate_dir.reshape(lines, LANES),
+            migrate_slot.reshape(lines, LANES),
+            contact_particle.reshape(-1, LANES),
+            place.reshape(-1, LANES),
+            contact_weight.reshape(-1, LANES),
         ),
     )
     moved = moved.reshape(3, 16, LANES)

time: 94.6 us -> 82 us (0.87)
  Pallas kernels: 49.1 us -> 36.5 us
    pallas_call x3, Pallas kernels: 49.1 us -> 36.5 us  [call(): pl.pallas_call(kernel, name=name, out_shape=[jax.ShapeDtypeStruct(shape,...]
  transfers between devices with their start and end apart: 12 -> 12, of which waited for: 8 -> 8; matrix products, arithmetic and copies ran while one was open for 1% -> 1% of each run, Pallas kernels for 9% -> 8%
where the time goes in v2:
time: 82 us; the launch traced here: 81.3 us
  Pallas kernels  36.5 us (45%)
  starting transfers between devices  17.4 us (21%)
  waiting for transfers between devices  14.4 us (18%)
  local copies, waits for them, and re-layouts  7.64 us (9%)
  between operations  3 us (4%)
  other arithmetic  2.3 us (3%)
    pallas_call x3, Pallas kernels, call(): pl.pallas_call(kernel, name=name, out_shape=[jax.ShapeDtypeStruct(shape,...  36.5 us
    ppermute x6, starting transfers between devices, body(): came = lax.ppermute(sent, axis, ring(axis, by))  8.93 us
    ppermute x3, starting transfers between devices, shifted_axes(): upper = lax.ppermute(first(rise, dim), axis, ring(axis, -1))  7.49 us
    ppermute x6, waiting for transfers between devices, body(): came = lax.ppermute(sent, axis, ring(axis, by))  6.63 us
    ppermute x3, waiting for transfers between devices, shifted_axes(): lower = lax.ppermute(last(fall, dim), axis, ring(axis, 1))  4.76 us
    unnamed x19, local copies, waits for them, and re-layouts  4.3 us
    ppermute x3, waiting for transfers between devices, shifted_axes(): upper = lax.ppermute(first(rise, dim), axis, ring(axis, -1))  3.05 us
  transfers between devices with their start and end apart: 12, of which 8 were waited for; matrix products, arithmetic and copies ran while one was open for 1% of the time, Pallas kernels for 8%

profile of v2, /device:TPU:6, one launch (start us, length us, event | category | flops | bytes accessed | tf_op | source)
XLA Modules:
  0.0 81.3 jit_solution(15822462021610108327)
XLA Ops:
  0.6 1.4 %fusion.27 = (s32[1,1]{1,0:T(1,128)}, s32[1,1]{1,0:T(1,128)}, s32[1,1]{1,0:T(1,128)}) fusion(s32[2,3]{1,0:T(2,128)} %param.12), kind=kLoop, calls=%fused_computation.96 | loop fusion | bytes 24 | tf_op jit(solution)/shard_map/slice | solution.py:285
  2.7 0.7 slice_select_fusion.1
  3.4 3.3 %collective-permute-start = (s32[1,8,128]{2,1,0:T(8,128)S(1)}, s32[1,8,128]{2,1,0:T(8,128)S(1)}, u32[]{:S(2)}, u32[]{:S(2)}) collective-permute-start(s32[1,8,128]{2,1,0:T(8,128)S(1)} %slice_bitcast_fusion.10), channel_id=1, source_target_pairs={{0,96},{32,0},{64,32},{96,64},{1,97},{33,1},{65,33},{97,65},{2,98}... | collective-permute-start | bytes 12296 | tf_op jit(solution)/shard_map/ppermute | solution.py:263
  6.7 0.7 copy-done.7
  8.1 3.1 %collective-permute-done.1 = s32[1,8,128]{2,1,0:T(8,128)S(1)} collective-permute-done((s32[1,8,128]{2,1,0:T(8,128)S(1)}, s32[1,8,128]{2,1,0:T(8,128)S(1)}, u32[]{:S(2)}, u32[]{:S(2)}) %collective-permute-start.1) | collective-permute-done | bytes 4128 | tf_op jit(solution)/shard_map/ppermute | solution.py:264
  11.3 3.1 %collective-permute-start.2 = (s32[4,1,128]{2,1,0:T(1,128)S(1)}, s32[4,1,128]{2,1,0:T(1,128)S(1)}, u32[]{:S(2)}, u32[]{:S(2)}) collective-permute-start(s32[4,1,128]{2,1,0:T(1,128)S(1)} %slice.404), channel_id=1, source_target_pairs={{0,24},{8,0},{16,8},{24,16},{1,25},{9,1},{17,9},{25,17},{2,26},{10... | collective-permute-start | bytes 6152 | tf_op jit(solution)/shard_map/ppermute | solution.py:263
  14.4 1.1 %copy-done = f32[3,40960]{1,0:T(4,128)S(1)} copy-done((f32[3,40960]{1,0:T(4,128)S(1)}, f32[3,40960]{1,0:T(4,128)}, u32[]{:S(2)}) %copy-start) | copy-done | bytes 491544
  15.5 1.0 %copy-done.1 = s32[2,40960]{1,0:T(2,128)S(1)} copy-done((s32[2,40960]{1,0:T(2,128)S(1)}, s32[2,40960]{1,0:T(2,128)}, u32[]{:S(2)}) %copy-start.1) | copy-done | bytes 327704
  16.4 6.5 %sums.1.mean_ref = f32[96,128]{1,0:T(8,128)S(1)} custom-call(f32[320,3,128]{2,1,0:T(4,128)S(1)} %bitcast.92, s32[320,2,128]{2,1,0:T(2,128)S(1)} %bitcast.94), custom_call_target="tpu_custom_call" | custom-call | flops 2348810240 | bytes 2097152 | tf_op jit(solution)/shard_map/sums/pallas_call | solution.py:225
  23.8 1.0 %collective-permute-start.5 = (s32[4,8,1]{2,1,0:T(8,128)S(1)}, s32[4,8,1]{2,1,0:T(8,128)S(1)}, u32[]{:S(2)}, u32[]{:S(2)}) collective-permute-start(s32[4,8,1]{2,1,0:T(8,128)S(1)} %slice.409), channel_id=1, source_target_pairs={{0,1},{1,2},{2,3},{3,4},{4,5},{5,6},{6,7},{7,0},{8,9},{9,10},{10,1... | collective-permute-start | bytes 392 | tf_op jit(solution)/shard_map/ppermute | solution.py:264
  24.7 1.1 %collective-permute-start.4 = (s32[4,8,1]{2,1,0:T(8,128)S(1)}, s32[4,8,1]{2,1,0:T(8,128)S(1)}, u32[]{:S(2)}, u32[]{:S(2)}) collective-permute-start(s32[4,8,1]{2,1,0:T(8,128)S(1)} %bitcast.102), channel_id=1, source_target_pairs={{0,7},{1,0},{2,1},{3,2},{4,3},{5,4},{6,5},{7,6},{8,15},{9,8},{10,9... | collective-permute-start | bytes 392 | tf_op jit(solution)/shard_map/ppermute | solution.py:263
  25.9 1.6 %collective-permute-done.5 = s32[4,8,1]{2,1,0:T(8,128)S(1)} collective-permute-done((s32[4,8,1]{2,1,0:T(8,128)S(1)}, s32[4,8,1]{2,1,0:T(8,128)S(1)}, u32[]{:S(2)}, u32[]{:S(2)}) %collective-permute-start.5) | collective-permute-done | bytes 160 | tf_op jit(solution)/shard_map/ppermute | solution.py:264
  27.5 3.0 %collective-permute-done.4 = s32[4,8,1]{2,1,0:T(8,128)S(1)} collective-permute-done((s32[4,8,1]{2,1,0:T(8,128)S(1)}, s32[4,8,1]{2,1,0:T(8,128)S(1)}, u32[]{:S(2)}, u32[]{:S(2)}) %collective-permute-start.4) | collective-permute-done | bytes 160 | tf_op jit(solution)/shard_map/ppermute | solution.py:263
  30.6 14.9 %turn.1 = (f32[3,320,128]{2,1,0:T(8,128)S(1)}, f32[96,128]{1,0:T(8,128)S(1)}) custom-call(f32[320,3,128]{2,1,0:T(4,128)S(1)} %bitcast.93, s32[320,2,128]{2,1,0:T(2,128)S(1)} %bitcast.95, f32[96,128]{1,0:T(8,128)S(1)} %sums.1.mean_ref, s32[32,128]{1,0:T(8,128)S(1)} %get-tuple-element.18.axis_ref), custom_call_target="tpu_custom_call" | custom-call | flops 4697620480 | bytes 2097152 | tf_op jit(solution)/shard_map/turn/pallas_call | solution.py:225
  45.6 0.8 %copy-done.3 = s32[40960]{0:T(1024)S(1)} copy-done((s32[40960]{0:T(1024)S(1)}, s32[40960]{0:T(1024)}, u32[]{:S(2)}) %copy-start.3) | copy-done | bytes 163864
  46.4 15.1 %last.1 = (f32[3,41920]{1,0:T(4,128)}, f32[48,128]{1,0:T(8,128)S(1)}, f32[64,128]{1,0:T(8,128)S(1)}) custom-call(f32[3,320,128]{2,1,0:T(8,128)S(1)} %get-tuple-element.9.v_ref, s32[320,2,128]{2,1,0:T(2,128)S(1)} %bitcast.96, f32[96,128]{1,0:T(8,128)S(1)} %get-tuple-element.8.mean_ref, s32[32,128]{1,0:T(8,128)S(1)} %get-tuple-element.17.axis_ref, ...), custom_call_target="tpu_custom_call" | custom-call | flops 4697620480 | bytes 2097152 | tf_op jit(solution)/shard_map/last/pallas_call | solution.py:225
  61.7 3.3 %collective-permute-start.6 = (f32[4864]{0:T(1024)S(1)}, f32[4864]{0:T(1024)S(1)}, u32[]{:S(2)}, u32[]{:S(2)}) collective-permute-start(f32[4864]{0:T(1024)S(1)} %pad_maximum_fusion), channel_id=1, source_target_pairs={{0,96},{32,0},{64,32},{96,64},{1,97},{33,1},{65,33},{97,65},{2,98}... | collective-permute-start | bytes 58376 | tf_op jit(solution)/shard_map/ppermute | solution.py:356
  65.0 1.3 %collective-permute-done.7 = f32[4864]{0:T(1024)S(1)} collective-permute-done((f32[4864]{0:T(1024)S(1)}, f32[4864]{0:T(1024)S(1)}, u32[]{:S(2)}, u32[]{:S(2)}) %collective-permute-start.7) | collective-permute-done | bytes 19488 | tf_op jit(solution)/shard_map/ppermute | solution.py:356
  67.2 2.7 %collective-permute-start.8 = (f32[3328]{0:T(1024)S(1)}, f32[3328]{0:T(1024)S(1)}, u32[]{:S(2)}, u32[]{:S(2)}) collective-permute-start(f32[3328]{0:T(1024)S(1)} %pad_maximum_fusion.2), channel_id=1, source_target_pairs={{0,24},{8,0},{16,8},{24,16},{1,25},{9,1},{17,9},{25,17},{2,26},{10... | collective-permute-start | bytes 39944 | tf_op jit(solution)/shard_map/ppermute | solution.py:356
  70.1 1.5 %collective-permute-done.9 = f32[3328]{0:T(1024)S(1)} collective-permute-done((f32[3328]{0:T(1024)S(1)}, f32[3328]{0:T(1024)S(1)}, u32[]{:S(2)}, u32[]{:S(2)}) %collective-permute-start.9) | collective-permute-done | bytes 13344 | tf_op jit(solution)/shard_map/ppermute | solution.py:356
  72.3 2.0 %collective-permute-start.10 = (f32[1888]{0:T(1024)S(1)}, f32[1888]{0:T(1024)S(1)}, u32[]{:S(2)}, u32[]{:S(2)}) collective-permute-start(f32[1888]{0:T(1024)S(1)} %pad_maximum_fusion.4), channel_id=1, source_target_pairs={{0,7},{1,0},{2,1},{3,2},{4,3},{5,4},{6,5},{7,6},{8,15},{9,8},{10,9... | collective-permute-start | bytes 22664 | tf_op jit(solution)/shard_map/ppermute | solution.py:356
  74.4 1.3 %collective-permute-done.11 = f32[1888]{0:T(1024)S(1)} collective-permute-done((f32[1888]{0:T(1024)S(1)}, f32[1888]{0:T(1024)S(1)}, u32[]{:S(2)}, u32[]{:S(2)}) %collective-permute-start.11) | collective-permute-done | bytes 7584 | tf_op jit(solution)/shard_map/ppermute | solution.py:356
  75.7 2.4 %collective-permute-done.10 = f32[1888]{0:T(1024)S(1)} collective-permute-done((f32[1888]{0:T(1024)S(1)}, f32[1888]{0:T(1024)S(1)}, u32[]{:S(2)}, u32[]{:S(2)}) %collective-permute-start.10) | collective-permute-done | bytes 7584 | tf_op jit(solution)/shard_map/ppermute | solution.py:356
  80.5 0.7 maximum_select_fusion.2
  (102 shorter events, 4.6 us)
Async XLA Ops:
  3.4 4.7 %collective-permute-start = (s32[1,8,128]{2,1,0:T(8,128)S(1)}, s32[1,8,128]{2,1,0:T(8,128)S(1)}, u32[]{:S(2)}, u32[]{:S(2)}) collective-permute-start(s32[1,8,128]{2,1,0:T(8,128)S(1)} %slice_bitcast_fusion.10), channel_id=1, source_target_pairs={{0,96},{32,0},{64,32},{96,64},{1,97},{33,1},{65,33},{97,65},{2,98}... | collective-permute-start | bytes 12296 | tf_op jit(solution)/shard_map/ppermute | solution.py:263
  6.7 4.5 %collective-permute-start.1 = (s32[1,8,128]{2,1,0:T(8,128)S(1)}, s32[1,8,128]{2,1,0:T(8,128)S(1)}, u32[]{:S(2)}, u32[]{:S(2)}) collective-permute-start(s32[1,8,128]{2,1,0:T(8,128)S(1)} %slice_bitcast_fusion.9), channel_id=1, source_target_pairs={{0,32},{32,64},{64,96},{96,0},{1,33},{33,65},{65,97},{97,1},{2,34}... | collective-permute-start | bytes 12296 | tf_op jit(solution)/shard_map/ppermute | solution.py:264
  6.7 0.7 copy-start.7
  11.3 12.4 %collective-permute-start.2 = (s32[4,1,128]{2,1,0:T(1,128)S(1)}, s32[4,1,128]{2,1,0:T(1,128)S(1)}, u32[]{:S(2)}, u32[]{:S(2)}) collective-permute-start(s32[4,1,128]{2,1,0:T(1,128)S(1)} %slice.404), channel_id=1, source_target_pairs={{0,24},{8,0},{16,8},{24,16},{1,25},{9,1},{17,9},{25,17},{2,26},{10... | collective-permute-start | bytes 6152 | tf_op jit(solution)/shard_map/ppermute | solution.py:263
  14.4 9.3 %collective-permute-start.3 = (s32[4,1,128]{2,1,0:T(1,128)S(1)}, s32[4,1,128]{2,1,0:T(1,128)S(1)}, u32[]{:S(2)}, u32[]{:S(2)}) collective-permute-start(s32[4,1,128]{2,1,0:T(1,128)S(1)} %slice.405), channel_id=1, source_target_pairs={{0,8},{8,16},{16,24},{24,0},{1,9},{9,17},{17,25},{25,1},{2,10},{10... | collective-permute-start | bytes 6152 | tf_op jit(solution)/shard_map/ppermute | solution.py:264
  14.4 1.1 %copy-start = (f32[3,40960]{1,0:T(4,128)S(1)}, f32[3,40960]{1,0:T(4,128)}, u32[]{:S(2)}) copy-start(f32[3,40960]{1,0:T(4,128)} %param.10) | copy-start | bytes 1474564
  15.5 1.0 %copy-start.1 = (s32[2,40960]{1,0:T(2,128)S(1)}, s32[2,40960]{1,0:T(2,128)}, u32[]{:S(2)}) copy-start(s32[2,40960]{1,0:T(2,128)} %param.11) | copy-start | bytes 983044
  23.8 3.8 %collective-permute-start.5 = (s32[4,8,1]{2,1,0:T(8,128)S(1)}, s32[4,8,1]{2,1,0:T(8,128)S(1)}, u32[]{:S(2)}, u32[]{:S(2)}) collective-permute-start(s32[4,8,1]{2,1,0:T(8,128)S(1)} %slice.409), channel_id=1, source_target_pairs={{0,1},{1,2},{2,3},{3,4},{4,5},{5,6},{6,7},{7,0},{8,9},{9,10},{10,1... | collective-permute-start | bytes 392 | tf_op jit(solution)/shard_map/ppermute | solution.py:264
  24.7 5.8 %collective-permute-start.4 = (s32[4,8,1]{2,1,0:T(8,128)S(1)}, s32[4,8,1]{2,1,0:T(8,128)S(1)}, u32[]{:S(2)}, u32[]{:S(2)}) collective-permute-start(s32[4,8,1]{2,1,0:T(8,128)S(1)} %bitcast.102), channel_id=1, source_target_pairs={{0,7},{1,0},{2,1},{3,2},{4,3},{5,4},{6,5},{7,6},{8,15},{9,8},{10,9... | collective-permute-start | bytes 392 | tf_op jit(solution)/shard_map/ppermute | solution.py:263
  30.6 14.9 %copy-start.2 = (s32[2,40960]{1,0:T(2,128)S(1)}, s32[2,40960]{1,0:T(2,128)}, u32[]{:S(2)}) copy-start(s32[2,40960]{1,0:T(2,128)} %param.11) | copy-start | bytes 983044
  30.6 15.0 %copy-start.4 = (s32[40960]{0:T(1024)S(1)}, s32[40960]{0:T(1024)}, u32[]{:S(2)}) copy-start(s32[40960]{0:T(1024)} %param.15) | copy-start | bytes 491524
  45.5 0.9 %copy-start.3 = (s32[40960]{0:T(1024)S(1)}, s32[40960]{0:T(1024)}, u32[]{:S(2)}) copy-start(s32[40960]{0:T(1024)} %param.14) | copy-start | bytes 491524
  45.5 0.9 %copy-start.6 = (f32[2048]{0:T(1024)S(1)}, f32[2048]{0:T(1024)}, u32[]{:S(2)}) copy-start(f32[2048]{0:T(1024)} %param.18) | copy-start | bytes 24580
  45.6 0.9 %copy-start.5 = (s32[2048]{0:T(1024)S(1)}, s32[2048]{0:T(1024)}, u32[]{:S(2)}) copy-start(s32[2048]{0:T(1024)} %param.17) | copy-start | bytes 24580
  61.6 4.8 %collective-permute-start.7 = (f32[4864]{0:T(1024)S(1)}, f32[4864]{0:T(1024)S(1)}, u32[]{:S(2)}, u32[]{:S(2)}) collective-permute-start(f32[4864]{0:T(1024)S(1)} %pad_maximum_fusion.1), channel_id=1, source_target_pairs={{0,32},{32,64},{64,96},{96,0},{1,33},{33,65},{65,97},{97,1},{2,34}... | collective-permute-start | bytes 58376 | tf_op jit(solution)/shard_map/ppermute | solution.py:356
  61.7 4.8 %collective-permute-start.6 = (f32[4864]{0:T(1024)S(1)}, f32[4864]{0:T(1024)S(1)}, u32[]{:S(2)}, u32[]{:S(2)}) collective-permute-start(f32[4864]{0:T(1024)S(1)} %pad_maximum_fusion), channel_id=1, source_target_pairs={{0,96},{32,0},{64,32},{96,64},{1,97},{33,1},{65,33},{97,65},{2,98}... | collective-permute-start | bytes 58376 | tf_op jit(solution)/shard_map/ppermute | solution.py:356
  66.6 5.0 %collective-permute-start.9 = (f32[3328]{0:T(1024)S(1)}, f32[3328]{0:T(1024)S(1)}, u32[]{:S(2)}, u32[]{:S(2)}) collective-permute-start(f32[3328]{0:T(1024)S(1)} %pad_maximum_fusion.3), channel_id=1, source_target_pairs={{0,8},{8,16},{16,24},{24,0},{1,9},{9,17},{17,25},{25,1},{2,10},{10... | collective-permute-start | bytes 39944 | tf_op jit(solution)/shard_map/ppermute | solution.py:356
  67.2 4.4 %collective-permute-start.8 = (f32[3328]{0:T(1024)S(1)}, f32[3328]{0:T(1024)S(1)}, u32[]{:S(2)}, u32[]{:S(2)}) collective-permute-start(f32[3328]{0:T(1024)S(1)} %pad_maximum_fusion.2), channel_id=1, source_target_pairs={{0,24},{8,0},{16,8},{24,16},{1,25},{9,1},{17,9},{25,17},{2,26},{10... | collective-permute-start | bytes 39944 | tf_op jit(solution)/shard_map/ppermute | solution.py:356
  71.9 3.7 %collective-permute-start.11 = (f32[1888]{0:T(1024)S(1)}, f32[1888]{0:T(1024)S(1)}, u32[]{:S(2)}, u32[]{:S(2)}) collective-permute-start(f32[1888]{0:T(1024)S(1)} %pad_maximum_fusion.5), channel_id=1, source_target_pairs={{0,1},{1,2},{2,3},{3,4},{4,5},{5,6},{6,7},{7,0},{8,9},{9,10},{10,1... | collective-permute-start | bytes 22664 | tf_op jit(solution)/shard_map/ppermute | solution.py:356
  72.3 5.8 %collective-permute-start.10 = (f32[1888]{0:T(1024)S(1)}, f32[1888]{0:T(1024)S(1)}, u32[]{:S(2)}, u32[]{:S(2)}) collective-permute-start(f32[1888]{0:T(1024)S(1)} %pad_maximum_fusion.4), channel_id=1, source_target_pairs={{0,7},{1,0},{2,1},{3,2},{4,3},{5,4},{6,5},{7,6},{8,15},{9,8},{10,9... | collective-permute-start | bytes 22664 | tf_op jit(solution)/shard_map/ppermute | solution.py:356
  79.2 0.7 copy-start.8

commit v3 on v2

--- a/solution.py
+++ b/solution.py
@@ -1,3 +1,4 @@
+import functools
 import math
 
 import jax
@@ -127,21 +128,21 @@
     return [turned[i] + picked[i] for i in range(3)]
 
 
-def sum_kernel(v_ref, cells_ref, mean_ref, total):
-    total[...] = jnp.zeros_like(total)
-
-    def step(i, carry):
+def sum_kernel(low, high, ends, v_ref, cells_ref, *refs):
+    done_ref, out_ref = (None, refs[-1]) if low == 0 else (refs[0], refs[-1])
+    shape = (224, LANES)
+
+    def step(i, total):
         lanes = places(LANES)
-        added = 0.0
         for part in range(UNROLL):
             at = pl.ds(pl.multiple_of((i * UNROLL + part) * 8, 8), 8)
             v = [v_ref[at, c, :] for c in range(3)]
-            added += scatter(v, cells_ref[at, 0, :], 32, True, lanes)
-        total[...] += added
-        return carry
-
-    lax.fori_loop(0, v_ref.shape[0] // (8 * UNROLL), step, 0)
-    mean_ref[...] = mean_of(total[...])
+            total += scatter(v, cells_ref[at, 0, :], 32, True, lanes)
+        return total
+
+    total = jnp.zeros(shape, jnp.float32) if done_ref is None else done_ref[...]
+    total = lax.fori_loop(low, high, step, total)
+    out_ref[...] = mean_of(total) if ends else total
 
 
 def turn_kernel(v_ref, cells_ref, mean_ref, axis_ref, out_ref, next_ref, total, table):
@@ -165,24 +166,7 @@
     next_ref[...] = mean_of(total[...])
 
 
-def last_kernel(
-    v_ref,
-    cells_ref,
-    mean_ref,
-    axis_ref,
-    dir_ref,
-    slot_ref,
-    particle_ref,
-    place_ref,
-    weight_ref,
-    kept_ref,
-    moved_ref,
-    force_ref,
-    moved,
-    table,
-    held,
-):
-    moved[...] = jnp.zeros_like(moved)
+def leave(low, high, v_ref, cells_ref, mean_ref, axis_ref, dir_ref, slot_ref, new_ref, first, moved, table):
     table[...] = cell_table(mean_ref[...], axis_ref[...])
 
     def step(i, carry):
@@ -193,23 +177,53 @@
             at = pl.ds(line, 8)
             v = [v_ref[c, at, :] for c in range(3)]
             new = collide(table[...], cells_ref[at, 1, :], v, lanes)
+            to = pl.ds(pl.multiple_of(line - first, 8), 8)
+            for c in range(3):
+                new_ref[c, to, :] = new[c]
             code = dir_ref[at, :]
-            for c in range(3):
-                held[c, at, :] = new[c]
-                kept = jnp.where(code > 0, 0.0, new[c])
-                for j in range(8):
-                    kept_ref[c : c + 1, pl.ds((line + j) * LANES, LANES)] = kept[j : j + 1]
             key = jnp.where(code > 0, (code - 1) * 256 + slot_ref[at, :], 4096)
             added += scatter(new, key, 16, False, lanes)
         moved[...] += added
         return carry
 
-    lax.fori_loop(0, v_ref.shape[1] // (8 * UNROLL), step, 0)
+    lax.fori_loop(low, high, step, 0)
+
+
+def part_kernel(low, high, *refs):
+    inputs, refs = refs[:6], refs[6:]
+    new_ref, moved_ref, table = refs[-3:]
+    moved_ref[...] = jnp.zeros_like(moved_ref) if low == 0 else refs[0][...]
+    leave(low, high, *inputs, new_ref, low * 8 * UNROLL, moved_ref, table)
+
+
+def last_kernel(low, high, *refs):
+    inputs, refs = refs[:6], refs[6:]
+    before_ref, parts, refs = refs[0], refs[1:3], refs[3:]
+    particle_ref, place_ref, weight_ref = refs[:3]
+    kept_ref, moved_ref, force_ref, moved, table, held = refs[-6:]
+    dir_ref = inputs[4]
+    moved[...] = before_ref[...]
+    start = 0
+    for part in parts:
+        held[:, start : start + part.shape[1], :] = part[...]
+        start += part.shape[1]
+    leave(low, high, *inputs, held, 0, moved, table)
     moved_ref[...] = moved[0:48] + moved[48:96]
 
+    def keep(i, carry):
+        line = pl.multiple_of(i * 8, 8)
+        at = pl.ds(line, 8)
+        stays = dir_ref[at, :] == 0
+        for c in range(3):
+            kept = jnp.where(stays, held[c, at, :], 0.0)
+            for j in range(8):
+                kept_ref[c : c + 1, pl.ds((line + j) * LANES, LANES)] = kept[j : j + 1]
+        return carry
+
     lines = held.shape[1]
-    high, low = split(held[...].reshape(3 * lines, LANES))
-    wide = jnp.concatenate([high, low], axis=1).astype(jnp.bfloat16)
+    lax.fori_loop(0, lines // 8, keep, 0, unroll=4)
+    high_part, low_part = split(held[...].reshape(3 * lines, LANES))
+    wide = jnp.concatenate([high_part, low_part], axis=1).astype(jnp.bfloat16)
     lanes = places(LANES)
     force = jnp.zeros((128, LANES), jnp.float32)
     for part in range(particle_ref.shape[0] // 8):
@@ -255,17 +269,22 @@
     return jnp.concatenate([rim, lax.slice_in_dim(x, 0, x.shape[dim] - 1, axis=dim)], axis=dim)
 
 
-def shifted_axes(axis_index, up):
-    at = axis_index
-    for dim, axis in enumerate(("gx", "gy", "gz")):
-        rise = jnp.where(up[dim], at[0], at[1])
-        fall = jnp.where(up[dim], at[1], at[0])
-        upper = lax.ppermute(first(rise, dim), axis, ring(axis, -1))
-        lower = lax.ppermute(last(fall, dim), axis, ring(axis, 1))
-        rise = ahead(rise, upper, dim)
-        fall = behind(fall, lower, dim)
-        at = jnp.stack([jnp.where(up[dim], rise, fall), jnp.where(up[dim], fall, rise)])
-    return at
+def axis_round(at, up, dim, axis):
+    rise = jnp.where(up, at[0], at[1])
+    fall = jnp.where(up, at[1], at[0])
+    upper = lax.ppermute(first(rise, dim), axis, ring(axis, -1))
+    lower = lax.ppermute(last(fall, dim), axis, ring(axis, 1))
+    rise = ahead(rise, upper, dim)
+    fall = behind(fall, lower, dim)
+    at = jnp.stack([jnp.where(up, rise, fall), jnp.where(up, fall, rise)])
+    return at, (upper, lower)
+
+
+def mean_round(mean, up, dim, axis):
+    lower = lax.ppermute(last(mean, dim + 1), axis, ring(axis, 1))
+    upper = lax.ppermute(first(mean, dim + 1), axis, ring(axis, -1))
+    mean = jnp.where(up, ahead(mean, upper, dim + 1), behind(mean, lower, dim + 1))
+    return mean, (upper, lower)
 
 
 def body(
@@ -296,16 +315,33 @@
     code = jnp.where(apart_x == 1, 1, jnp.where(apart_x == size_x - 1, 2, code))
     place = code * COLLOIDS_PER_UNIT + contact_colloid % COLLOIDS_PER_UNIT
 
-    axes = shifted_axes(axis_index, up).reshape(2, cells_x * cells_y, cells_z)
     lines = particles // LANES
+    steps = lines // (8 * UNROLL)
+    cuts = (0, steps * 3 // 10, steps * 6 // 10, steps)
+    spans = tuple(zip(cuts[:-1], cuts[1:]))
     velocity = velocities.reshape(3, lines, LANES).transpose(1, 0, 2)
     cells = particle_cells.reshape(2, lines, LANES).transpose(1, 0, 2)
     total = pltpu.VMEM((224, LANES), jnp.float32)
     table = pltpu.VMEM((128, 256), jnp.bfloat16)
     pair_flops = 2 * 224 * 128 * particles
-    (mean0,) = call(
-        sum_kernel, "sums", [(96, LANES)], [total], pair_flops, (velocity, cells)
-    )
+
+    axes = axis_index
+    summed = ()
+    for dim, axis in enumerate(("gx", "gy", "gz")):
+        axes, rims = axis_round(axes, up[dim], dim, axis)
+        low, high = spans[dim]
+        ends = dim == 2
+        (result,) = call(
+            functools.partial(sum_kernel, low, high, ends),
+            "sums_%d" % dim,
+            [(96 if ends else 224, LANES)],
+            [],
+            pair_flops // 3,
+            (velocity, cells) + summed,
+        )
+        summed = (result,) + rims
+    mean0 = result
+    axes = axes.reshape(2, cells_x * cells_y, cells_z)
     moving, mean1 = call(
         turn_kernel,
         "turn",
@@ -314,8 +350,33 @@
         2 * pair_flops,
         (velocity, cells, mean0, axes[0]),
     )
+    shared = (
+        moving,
+        cells,
+        mean1,
+        axes[1],
+        migrate_dir.reshape(lines, LANES),
+        migrate_slot.reshape(lines, LANES),
+    )
+    mean = mean1.reshape(3, cells_x, cells_y, cells_z)
+    tied = ()
+    parts = []
+    for dim, axis in enumerate(("gx", "gy")):
+        mean, rims = mean_round(mean, up[dim], dim, axis)
+        low, high = spans[dim]
+        part, moved = call(
+            functools.partial(part_kernel, low, high),
+            "part_%d" % dim,
+            [(3, (high - low) * 8 * UNROLL, LANES), (96, LANES)],
+            [table],
+            pair_flops // 2,
+            shared + tied,
+        )
+        parts.append(part)
+        tied = (moved,) + rims
+    low, high = spans[2]
     kept, moved, force = call(
-        last_kernel,
+        functools.partial(last_kernel, low, high),
         "last",
         [(3, particles + 6 * CAP), (48, LANES), (64, LANES)],
         [
@@ -323,41 +384,36 @@
             table,
             pltpu.VMEM((3, lines, LANES), jnp.float32),
         ],
-        2 * pair_flops,
-        (
-            moving,
-            cells,
-            mean1,
-            axes[1],
-            migrate_dir.reshape(lines, LANES),
-            migrate_slot.reshape(lines, LANES),
+        pair_flops,
+        shared
+        + (moved, *parts)
+        + (
             contact_particle.reshape(-1, LANES),
             place.reshape(-1, LANES),
             contact_weight.reshape(-1, LANES),
-        ),
+        )
+        + rims,
     )
     moved = moved.reshape(3, 16, LANES)
     force = force.reshape(4, 16, LANES)
-    mean = mean1.reshape(3, cells_x, cells_y, cells_z)
     sums = force[:, 0:2].reshape(4, COLLOIDS_PER_UNIT)
     arrivals = []
-    for dim, axis in enumerate(("gx", "gy", "gz")):
-        rims = (last(mean, dim + 1), first(mean, dim + 1))
-        got = []
-        for side, by in enumerate((1, -1)):
-            number = 2 * dim + side
-            sent = jnp.concatenate(
-                [
-                    moved[:, 2 * number : 2 * number + 2].reshape(-1),
-                    force[:, 2 * number + 2 : 2 * number + 4].reshape(-1),
-                    rims[side].reshape(-1),
-                ]
-            )
-            came = lax.ppermute(sent, axis, ring(axis, by))
-            arrivals.append(came[0:768].reshape(3, 256)[:, :CAP])
-            sums = sums + came[768:1792].reshape(4, COLLOIDS_PER_UNIT)
-            got.append(came[1792:].reshape(rims[side].shape))
-        mean = jnp.where(up[dim], ahead(mean, got[1], dim + 1), behind(mean, got[0], dim + 1))
+    faces = (last(mean, 3), first(mean, 3))
+    got = []
+    for number in range(6):
+        axis, by = ("gx", "gy", "gz")[number // 2], 1 - 2 * (number % 2)
+        sent = [
+            moved[:, 2 * number : 2 * number + 2].reshape(-1),
+            force[:, 2 * number + 2 : 2 * number + 4].reshape(-1),
+        ]
+        if axis == "gz":
+            sent.append(faces[number % 2].reshape(-1))
+        came = lax.ppermute(jnp.concatenate(sent), axis, ring(axis, by))
+        arrivals.append(came[0:768].reshape(3, 256)[:, :CAP])
+        sums = sums + came[768:1792].reshape(4, COLLOIDS_PER_UNIT)
+        if axis == "gz":
+            got.append(came[1792:].reshape(faces[0].shape))
+    mean = jnp.where(up[2], ahead(mean, got[1], 3), behind(mean, got[0], 3))
     migrated = lax.dynamic_update_slice(kept, jnp.concatenate(arrivals, axis=1), (0, particles))
     colloid_force = (sums[0:3] - sums[3:4] * colloid_velocity) / jnp.maximum(sums[3:4], 1.0)
     return (mean, migrated, colloid_force)

time: 82 us -> 79.1 us (0.965)
  waiting for transfers between devices: 14.4 us -> 10.4 us
  starting transfers between devices: 17.4 us -> 18.4 us
    ppermute x12 -> x16, waiting for transfers between devices: 14.4 us -> 10.4 us  [the longest x6 4.67 us: body(): came = lax.ppermute(jnp.concatenate(sent), axis, ring(axis, by))]
    ppermute x12 -> x16, starting transfers between devices: 17.4 us -> 18.4 us  [the longest x3 7.49 us: axis_round(): upper = lax.ppermute(first(rise, dim), axis, ring(axis, -1))]
    pallas_call x3 -> x7, Pallas kernels: 36.5 us -> 37 us  [call(): pl.pallas_call(kernel, name=name, out_shape=[jax.ShapeDtypeStruct(shape,...]
  transfers between devices with their start and end apart: 12 -> 16, of which waited for: 8 -> 6; matrix products, arithmetic and copies ran while one was open for 1% -> 1% of each run, Pallas kernels for 8% -> 18%
where the time goes in v3:
time: 79.1 us; the launch traced here: 78.6 us
  Pallas kernels  37 us (47%)
  starting transfers between devices  18.4 us (23%)
  waiting for transfers between devices  10.4 us (13%)
  local copies, waits for them, and re-layouts  7.37 us (9%)
  between operations  3.04 us (4%)
  other arithmetic  2.3 us (3%)
    pallas_call x7, Pallas kernels, call(): pl.pallas_call(kernel, name=name, out_shape=[jax.ShapeDtypeStruct(shape,...  37 us
    ppermute x3, starting transfers between devices, axis_round(): upper = lax.ppermute(first(rise, dim), axis, ring(axis, -1))  7.49 us
    ppermute x6, starting transfers between devices, body(): came = lax.ppermute(jnp.concatenate(sent), axis, ring(axis, by))  6.42 us
    ppermute x6, waiting for transfers between devices, body(): came = lax.ppermute(jnp.concatenate(sent), axis, ring(axis, by))  4.67 us
    unnamed x19, local copies, waits for them, and re-layouts  4.12 us
    ppermute x3, waiting for transfers between devices, axis_round(): lower = lax.ppermute(last(fall, dim), axis, ring(axis, 1))  2.83 us
    ppermute x2, starting transfers between devices, mean_round(): upper = lax.ppermute(first(mean, dim + 1), axis, ring(axis, -1))  2.43 us
    ppermute x3, waiting for transfers between devices, axis_round(): upper = lax.ppermute(first(rise, dim), axis, ring(axis, -1))  2.16 us
  transfers between devices with their start and end apart: 16, of which 6 were waited for; matrix products, arithmetic and copies ran while one was open for 1% of the time, Pallas kernels for 18%

profile of v3, /device:TPU:6, one launch (start us, length us, event | category | flops | bytes accessed | tf_op | source)
XLA Modules:
  0.0 78.6 jit_solution(6941593335185777948)
XLA Ops:
  0.6 1.4 %fusion.29 = (s32[1,1]{1,0:T(1,128)}, s32[1,1]{1,0:T(1,128)}, s32[1,1]{1,0:T(1,128)}) fusion(s32[2,3]{1,0:T(2,128)} %param.12), kind=kLoop, calls=%fused_computation.92 | loop fusion | bytes 24 | tf_op jit(solution)/shard_map/slice | solution.py:304
  3.4 3.3 %collective-permute-start = (s32[1,8,128]{2,1,0:T(8,128)S(1)}, s32[1,8,128]{2,1,0:T(8,128)S(1)}, u32[]{:S(2)}, u32[]{:S(2)}) collective-permute-start(s32[1,8,128]{2,1,0:T(8,128)S(1)} %slice_bitcast_fusion.6), channel_id=1, source_target_pairs={{0,96},{32,0},{64,32},{96,64},{1,97},{33,1},{65,33},{97,65},{2,98}... | collective-permute-start | bytes 12296 | tf_op jit(solution)/shard_map/ppermute | solution.py:275
  7.5 1.1 %copy-done = f32[3,40960]{1,0:T(4,128)S(1)} copy-done((f32[3,40960]{1,0:T(4,128)S(1)}, f32[3,40960]{1,0:T(4,128)}, u32[]{:S(2)}) %copy-start) | copy-done | bytes 491544
  8.6 1.0 %copy-done.1 = s32[2,40960]{1,0:T(2,128)S(1)} copy-done((s32[2,40960]{1,0:T(2,128)S(1)}, s32[2,40960]{1,0:T(2,128)}, u32[]{:S(2)}) %copy-start.1) | copy-done | bytes 327704
  9.5 1.9 %sums_0.1.refs_0_ = f32[224,128]{1,0:T(8,128)S(1)} custom-call(f32[320,3,128]{2,1,0:T(4,128)S(1)} %bitcast.78, s32[320,2,128]{2,1,0:T(2,128)S(1)} %bitcast.82), custom_call_target="tpu_custom_call" | custom-call | flops 782936768 | bytes 2097152 | tf_op jit(solution)/shard_map/sums_0/pallas_call | solution.py:239
  12.8 3.1 %collective-permute-start.2 = (s32[4,1,128]{2,1,0:T(1,128)S(1)}, s32[4,1,128]{2,1,0:T(1,128)S(1)}, u32[]{:S(2)}, u32[]{:S(2)}) collective-permute-start(s32[4,1,128]{2,1,0:T(1,128)S(1)} %slice.387), channel_id=1, source_target_pairs={{0,24},{8,0},{16,8},{24,16},{1,25},{9,1},{17,9},{25,17},{2,26},{10... | collective-permute-start | bytes 6152 | tf_op jit(solution)/shard_map/ppermute | solution.py:275
  15.9 1.9 %sums_1.1.refs_0_ = f32[224,128]{1,0:T(8,128)S(1)} custom-call(f32[320,3,128]{2,1,0:T(4,128)S(1)} %bitcast.79, s32[320,2,128]{2,1,0:T(2,128)S(1)} %bitcast.83, f32[224,128]{1,0:T(8,128)S(1)} %sums_0.1.refs_0_, s32[1,8,128]{2,1,0:T(8,128)S(1)} %collective-permute-done.refs_1_, s32[1,8,128]{2,1,0:T(8,128)S(1)} %collective-permute-done.1.refs_2_), custom_call_target="tpu_custom_call" | custom-call | flops 782936768 | bytes 2097152 | tf_op jit(solution)/shard_map/sums_1/pallas_call | solution.py:239
  17.9 2.8 %collective-permute-done.3.refs_2_ = s32[4,1,128]{2,1,0:T(1,128)S(1)} collective-permute-done((s32[4,1,128]{2,1,0:T(1,128)S(1)}, s32[4,1,128]{2,1,0:T(1,128)S(1)}, u32[]{:S(2)}, u32[]{:S(2)}) %collective-permute-start.3) | collective-permute-done | bytes 2080 | tf_op jit(solution)/shard_map/ppermute | solution.py:276
  20.8 1.0 %collective-permute-start.5 = (s32[4,8,1]{2,1,0:T(8,128)S(1)}, s32[4,8,1]{2,1,0:T(8,128)S(1)}, u32[]{:S(2)}, u32[]{:S(2)}) collective-permute-start(s32[4,8,1]{2,1,0:T(8,128)S(1)} %slice.393), channel_id=1, source_target_pairs={{0,1},{1,2},{2,3},{3,4},{4,5},{5,6},{6,7},{7,0},{8,9},{9,10},{10,1... | collective-permute-start | bytes 392 | tf_op jit(solution)/shard_map/ppermute | solution.py:276
  21.8 1.1 %collective-permute-start.4 = (s32[4,8,1]{2,1,0:T(8,128)S(1)}, s32[4,8,1]{2,1,0:T(8,128)S(1)}, u32[]{:S(2)}, u32[]{:S(2)}) collective-permute-start(s32[4,8,1]{2,1,0:T(8,128)S(1)} %bitcast.98), channel_id=1, source_target_pairs={{0,7},{1,0},{2,1},{3,2},{4,3},{5,4},{6,5},{7,6},{8,15},{9,8},{10,9... | collective-permute-start | bytes 392 | tf_op jit(solution)/shard_map/ppermute | solution.py:275
  22.9 2.6 %sums_2.1.mean_ref = f32[96,128]{1,0:T(8,128)S(1)} custom-call(f32[320,3,128]{2,1,0:T(4,128)S(1)} %bitcast.80, s32[320,2,128]{2,1,0:T(2,128)S(1)} %bitcast.84, f32[224,128]{1,0:T(8,128)S(1)} %sums_1.1.refs_0_, s32[4,1,128]{2,1,0:T(1,128)S(1)} %collective-permute-done.2.refs_1_, s32[4,1,128]{2,1,0:T(1,128)S(1)} %collective-permute-done.3.refs_2_), custom_call_target="tpu_custom_call" | custom-call | flops 782936768 | bytes 2097152 | tf_op jit(solution)/shard_map/sums_2/pallas_call | solution.py:239
  25.5 2.2 %collective-permute-done.4 = s32[4,8,1]{2,1,0:T(8,128)S(1)} collective-permute-done((s32[4,8,1]{2,1,0:T(8,128)S(1)}, s32[4,8,1]{2,1,0:T(8,128)S(1)}, u32[]{:S(2)}, u32[]{:S(2)}) %collective-permute-start.4) | collective-permute-done | bytes 160 | tf_op jit(solution)/shard_map/ppermute | solution.py:275
  27.8 14.9 %turn.1 = (f32[3,320,128]{2,1,0:T(8,128)S(1)}, f32[96,128]{1,0:T(8,128)S(1)}) custom-call(f32[320,3,128]{2,1,0:T(4,128)S(1)} %bitcast.81, s32[320,2,128]{2,1,0:T(2,128)S(1)} %bitcast.85, f32[96,128]{1,0:T(8,128)S(1)} %sums_2.1.mean_ref, s32[32,128]{1,0:T(8,128)S(1)} %get-tuple-element.24.axis_ref), custom_call_target="tpu_custom_call" | custom-call | flops 4697620480 | bytes 2097152 | tf_op jit(solution)/shard_map/turn/pallas_call | solution.py:239
  42.7 1.4 %collective-permute-start.6 = (f32[3,1,8,128]{3,2,1,0:T(8,128)S(1)}, f32[3,1,8,128]{3,2,1,0:T(8,128)S(1)}, u32[]{:S(2)}, u32[]{:S(2)}) collective-permute-start(f32[3,1,8,128]{3,2,1,0:T(8,128)S(1)} %get-tuple-element.32), channel_id=1, source_target_pairs={{0,96},{32,0},{64,32},{96,64},{1,97},{33,1},{65,33},{97,65},{2,98}... | collective-permute-start | bytes 36872 | tf_op jit(solution)/shard_map/ppermute | solution.py:285
  44.1 3.8 %part_0.1 = (f32[3,96,128]{2,1,0:T(8,128)S(1)}, f32[96,128]{1,0:T(8,128)S(1)}) custom-call(f32[3,320,128]{2,1,0:T(8,128)S(1)} %get-tuple-element.13.refs_0_, s32[320,2,128]{2,1,0:T(2,128)S(1)} %bitcast.86, f32[96,128]{1,0:T(8,128)S(1)} %get-tuple-element.12.refs_2_, s32[32,128]{1,0:T(8,128)S(1)} %get-tuple-element.23.refs_3_, s32[320,128]{1,0:T(8,128)S(1)} %bitcast.89, ...), custom_call_target="tpu_custom_call" | custom-call | flops 1174405120 | bytes 2097152 | tf_op jit(solution)/shard_map/part_0/pallas_call | solution.py:239
  48.7 1.0 %collective-permute-start.8 = (f32[3,4,1,128]{3,2,1,0:T(1,128)S(1)}, f32[3,4,1,128]{3,2,1,0:T(1,128)S(1)}, u32[]{:S(2)}, u32[]{:S(2)}) collective-permute-start(f32[3,4,1,128]{3,2,1,0:T(1,128)S(1)} %get-tuple-element.28), channel_id=1, source_target_pairs={{0,24},{8,0},{16,8},{24,16},{1,25},{9,1},{17,9},{25,17},{2,26},{10... | collective-permute-start | bytes 18440 | tf_op jit(solution)/shard_map/ppermute | solution.py:285
  49.8 1.1 %collective-permute-start.9 = (f32[3,4,1,128]{3,2,1,0:T(1,128)S(1)}, f32[3,4,1,128]{3,2,1,0:T(1,128)S(1)}, u32[]{:S(2)}, u32[]{:S(2)}) collective-permute-start(f32[3,4,1,128]{3,2,1,0:T(1,128)S(1)} %get-tuple-element.27), channel_id=1, source_target_pairs={{0,8},{8,16},{16,24},{24,0},{1,9},{9,17},{17,25},{25,1},{2,10},{10... | collective-permute-start | bytes 18440 | tf_op jit(solution)/shard_map/ppermute | solution.py:284
  50.8 3.8 %part_1.1 = (f32[3,96,128]{2,1,0:T(8,128)S(1)}, f32[96,128]{1,0:T(8,128)S(1)}) custom-call(f32[3,320,128]{2,1,0:T(8,128)S(1)} %get-tuple-element.13.refs_0_, s32[320,2,128]{2,1,0:T(2,128)S(1)} %bitcast.87, f32[96,128]{1,0:T(8,128)S(1)} %get-tuple-element.12.refs_2_, s32[32,128]{1,0:T(8,128)S(1)} %get-tuple-element.23.refs_3_, s32[320,128]{1,0:T(8,128)S(1)} %bitcast.90, ...), custom_call_target="tpu_custom_call" | custom-call | flops 1174405120 | bytes 2097152 | tf_op jit(solution)/shard_map/part_1/pallas_call | solution.py:239
  55.3 8.1 %last.1 = (f32[3,41920]{1,0:T(4,128)}, f32[48,128]{1,0:T(8,128)S(1)}, f32[64,128]{1,0:T(8,128)S(1)}) custom-call(f32[3,320,128]{2,1,0:T(8,128)S(1)} %get-tuple-element.13.refs_0_, s32[320,2,128]{2,1,0:T(2,128)S(1)} %bitcast.88, f32[96,128]{1,0:T(8,128)S(1)} %get-tuple-element.12.refs_2_, s32[32,128]{1,0:T(8,128)S(1)} %get-tuple-element.23.refs_3_, ...), custom_call_target="tpu_custom_call" | custom-call | flops 2348810240 | bytes 2097152 | tf_op jit(solution)/shard_map/last/pallas_call | solution.py:239
  63.5 2.4 %collective-permute-start.15 = (f32[1792]{0:T(1024)S(1)}, f32[1792]{0:T(1024)S(1)}, u32[]{:S(2)}, u32[]{:S(2)}) collective-permute-start(f32[1792]{0:T(1024)S(1)} %pad_maximum_fusion.5), channel_id=1, source_target_pairs={{0,24},{8,0},{16,8},{24,16},{1,25},{9,1},{17,9},{25,17},{2,26},{10... | collective-permute-start | bytes 21512 | tf_op jit(solution)/shard_map/ppermute | solution.py:411
  66.1 1.7 %collective-permute-start.13 = (f32[1792]{0:T(1024)S(1)}, f32[1792]{0:T(1024)S(1)}, u32[]{:S(2)}, u32[]{:S(2)}) collective-permute-start(f32[1792]{0:T(1024)S(1)} %pad_maximum_fusion.3), channel_id=1, source_target_pairs={{0,96},{32,0},{64,32},{96,64},{1,97},{33,1},{65,33},{97,65},{2,98}... | collective-permute-start | bytes 21512 | tf_op jit(solution)/shard_map/ppermute | solution.py:411
  68.2 1.3 %collective-permute-start.11 = (f32[1888]{0:T(1024)S(1)}, f32[1888]{0:T(1024)S(1)}, u32[]{:S(2)}, u32[]{:S(2)}) collective-permute-start(f32[1888]{0:T(1024)S(1)} %pad_maximum_fusion.1), channel_id=1, source_target_pairs={{0,1},{1,2},{2,3},{3,4},{4,5},{5,6},{6,7},{7,0},{8,9},{9,10},{10,1... | collective-permute-start | bytes 22664 | tf_op jit(solution)/shard_map/ppermute | solution.py:411
  70.9 1.5 %collective-permute-done.12 = f32[1792]{0:T(1024)S(1)} collective-permute-done((f32[1792]{0:T(1024)S(1)}, f32[1792]{0:T(1024)S(1)}, u32[]{:S(2)}, u32[]{:S(2)}) %collective-permute-start.12) | collective-permute-done | bytes 7200 | tf_op jit(solution)/shard_map/ppermute | solution.py:411
  72.6 2.8 %collective-permute-done.10 = f32[1888]{0:T(1024)S(1)} collective-permute-done((f32[1888]{0:T(1024)S(1)}, f32[1888]{0:T(1024)S(1)}, u32[]{:S(2)}, u32[]{:S(2)}) %collective-permute-start.10) | collective-permute-done | bytes 7584 | tf_op jit(solution)/shard_map/ppermute | solution.py:411
  (106 shorter events, 8.4 us)
Async XLA Ops:
  3.4 9.4 %collective-permute-start = (s32[1,8,128]{2,1,0:T(8,128)S(1)}, s32[1,8,128]{2,1,0:T(8,128)S(1)}, u32[]{:S(2)}, u32[]{:S(2)}) collective-permute-start(s32[1,8,128]{2,1,0:T(8,128)S(1)} %slice_bitcast_fusion.6), channel_id=1, source_target_pairs={{0,96},{32,0},{64,32},{96,64},{1,97},{33,1},{65,33},{97,65},{2,98}... | collective-permute-start | bytes 12296 | tf_op jit(solution)/shard_map/ppermute | solution.py:275
  6.7 6.1 %collective-permute-start.1 = (s32[1,8,128]{2,1,0:T(8,128)S(1)}, s32[1,8,128]{2,1,0:T(8,128)S(1)}, u32[]{:S(2)}, u32[]{:S(2)}) collective-permute-start(s32[1,8,128]{2,1,0:T(8,128)S(1)} %slice_bitcast_fusion.5), channel_id=1, source_target_pairs={{0,32},{32,64},{64,96},{96,0},{1,33},{33,65},{65,97},{97,1},{2,34}... | collective-permute-start | bytes 12296 | tf_op jit(solution)/shard_map/ppermute | solution.py:276
  6.7 0.7 copy-start.7
  7.5 1.1 %copy-start = (f32[3,40960]{1,0:T(4,128)S(1)}, f32[3,40960]{1,0:T(4,128)}, u32[]{:S(2)}) copy-start(f32[3,40960]{1,0:T(4,128)} %param.10) | copy-start | bytes 1474564
  8.6 1.0 %copy-start.1 = (s32[2,40960]{1,0:T(2,128)S(1)}, s32[2,40960]{1,0:T(2,128)}, u32[]{:S(2)}) copy-start(s32[2,40960]{1,0:T(2,128)} %param.11) | copy-start | bytes 983044
  12.8 5.0 %collective-permute-start.2 = (s32[4,1,128]{2,1,0:T(1,128)S(1)}, s32[4,1,128]{2,1,0:T(1,128)S(1)}, u32[]{:S(2)}, u32[]{:S(2)}) collective-permute-start(s32[4,1,128]{2,1,0:T(1,128)S(1)} %slice.387), channel_id=1, source_target_pairs={{0,24},{8,0},{16,8},{24,16},{1,25},{9,1},{17,9},{25,17},{2,26},{10... | collective-permute-start | bytes 6152 | tf_op jit(solution)/shard_map/ppermute | solution.py:275
  15.9 4.8 %collective-permute-start.3 = (s32[4,1,128]{2,1,0:T(1,128)S(1)}, s32[4,1,128]{2,1,0:T(1,128)S(1)}, u32[]{:S(2)}, u32[]{:S(2)}) collective-permute-start(s32[4,1,128]{2,1,0:T(1,128)S(1)} %slice.388), channel_id=1, source_target_pairs={{0,8},{8,16},{16,24},{24,0},{1,9},{9,17},{17,25},{25,1},{2,10},{10... | collective-permute-start | bytes 6152 | tf_op jit(solution)/shard_map/ppermute | solution.py:276
  20.8 4.7 %collective-permute-start.5 = (s32[4,8,1]{2,1,0:T(8,128)S(1)}, s32[4,8,1]{2,1,0:T(8,128)S(1)}, u32[]{:S(2)}, u32[]{:S(2)}) collective-permute-start(s32[4,8,1]{2,1,0:T(8,128)S(1)} %slice.393), channel_id=1, source_target_pairs={{0,1},{1,2},{2,3},{3,4},{4,5},{5,6},{6,7},{7,0},{8,9},{9,10},{10,1... | collective-permute-start | bytes 392 | tf_op jit(solution)/shard_map/ppermute | solution.py:276
  21.8 5.8 %collective-permute-start.4 = (s32[4,8,1]{2,1,0:T(8,128)S(1)}, s32[4,8,1]{2,1,0:T(8,128)S(1)}, u32[]{:S(2)}, u32[]{:S(2)}) collective-permute-start(s32[4,8,1]{2,1,0:T(8,128)S(1)} %bitcast.98), channel_id=1, source_target_pairs={{0,7},{1,0},{2,1},{3,2},{4,3},{5,4},{6,5},{7,6},{8,15},{9,8},{10,9... | collective-permute-start | bytes 392 | tf_op jit(solution)/shard_map/ppermute | solution.py:275
  27.8 16.3 %copy-start.2 = (s32[2,40960]{1,0:T(2,128)S(1)}, s32[2,40960]{1,0:T(2,128)}, u32[]{:S(2)}) copy-start(s32[2,40960]{1,0:T(2,128)} %param.11) | copy-start | bytes 983044
  27.8 16.3 %copy-start.4 = (s32[40960]{0:T(1024)S(1)}, s32[40960]{0:T(1024)}, u32[]{:S(2)}) copy-start(s32[40960]{0:T(1024)} %param.15) | copy-start | bytes 491524
  42.6 1.5 %copy-start.3 = (s32[40960]{0:T(1024)S(1)}, s32[40960]{0:T(1024)}, u32[]{:S(2)}) copy-start(s32[40960]{0:T(1024)} %param.14) | copy-start | bytes 491524
  42.7 5.2 %collective-permute-start.6 = (f32[3,1,8,128]{3,2,1,0:T(8,128)S(1)}, f32[3,1,8,128]{3,2,1,0:T(8,128)S(1)}, u32[]{:S(2)}, u32[]{:S(2)}) collective-permute-start(f32[3,1,8,128]{3,2,1,0:T(8,128)S(1)} %get-tuple-element.32), channel_id=1, source_target_pairs={{0,96},{32,0},{64,32},{96,64},{1,97},{33,1},{65,33},{97,65},{2,98}... | collective-permute-start | bytes 36872 | tf_op jit(solution)/shard_map/ppermute | solution.py:285
  44.1 4.6 %collective-permute-start.7 = (f32[3,1,8,128]{3,2,1,0:T(8,128)S(1)}, f32[3,1,8,128]{3,2,1,0:T(8,128)S(1)}, u32[]{:S(2)}, u32[]{:S(2)}) collective-permute-start(f32[3,1,8,128]{3,2,1,0:T(8,128)S(1)} %get-tuple-element.31), channel_id=1, source_target_pairs={{0,32},{32,64},{64,96},{96,0},{1,33},{33,65},{65,97},{97,1},{2,34}... | collective-permute-start | bytes 36872 | tf_op jit(solution)/shard_map/ppermute | solution.py:284
  48.7 5.9 %collective-permute-start.8 = (f32[3,4,1,128]{3,2,1,0:T(1,128)S(1)}, f32[3,4,1,128]{3,2,1,0:T(1,128)S(1)}, u32[]{:S(2)}, u32[]{:S(2)}) collective-permute-start(f32[3,4,1,128]{3,2,1,0:T(1,128)S(1)} %get-tuple-element.28), channel_id=1, source_target_pairs={{0,24},{8,0},{16,8},{24,16},{1,25},{9,1},{17,9},{25,17},{2,26},{10... | collective-permute-start | bytes 18440 | tf_op jit(solution)/shard_map/ppermute | solution.py:285
  49.8 4.9 %collective-permute-start.9 = (f32[3,4,1,128]{3,2,1,0:T(1,128)S(1)}, f32[3,4,1,128]{3,2,1,0:T(1,128)S(1)}, u32[]{:S(2)}, u32[]{:S(2)}) collective-permute-start(f32[3,4,1,128]{3,2,1,0:T(1,128)S(1)} %get-tuple-element.27), channel_id=1, source_target_pairs={{0,8},{8,16},{16,24},{24,0},{1,9},{9,17},{17,25},{25,1},{2,10},{10... | collective-permute-start | bytes 18440 | tf_op jit(solution)/shard_map/ppermute | solution.py:284
  50.8 3.8 %copy-start.6 = (f32[2048]{0:T(1024)S(1)}, f32[2048]{0:T(1024)}, u32[]{:S(2)}) copy-start(f32[2048]{0:T(1024)} %param.18) | copy-start | bytes 24580
  54.6 0.7 copy-start.5
  63.5 6.0 %collective-permute-start.15 = (f32[1792]{0:T(1024)S(1)}, f32[1792]{0:T(1024)S(1)}, u32[]{:S(2)}, u32[]{:S(2)}) collective-permute-start(f32[1792]{0:T(1024)S(1)} %pad_maximum_fusion.5), channel_id=1, source_target_pairs={{0,24},{8,0},{16,8},{24,16},{1,25},{9,1},{17,9},{25,17},{2,26},{10... | collective-permute-start | bytes 21512 | tf_op jit(solution)/shard_map/ppermute | solution.py:411
  66.0 4.9 %collective-permute-start.14 = (f32[1792]{0:T(1024)S(1)}, f32[1792]{0:T(1024)S(1)}, u32[]{:S(2)}, u32[]{:S(2)}) collective-permute-start(f32[1792]{0:T(1024)S(1)} %pad_maximum_fusion.4), channel_id=1, source_target_pairs={{0,8},{8,16},{16,24},{24,0},{1,9},{9,17},{17,25},{25,1},{2,10},{10... | collective-permute-start | bytes 21512 | tf_op jit(solution)/shard_map/ppermute | solution.py:411
  66.1 4.8 %collective-permute-start.13 = (f32[1792]{0:T(1024)S(1)}, f32[1792]{0:T(1024)S(1)}, u32[]{:S(2)}, u32[]{:S(2)}) collective-permute-start(f32[1792]{0:T(1024)S(1)} %pad_maximum_fusion.3), channel_id=1, source_target_pairs={{0,96},{32,0},{64,32},{96,64},{1,97},{33,1},{65,33},{97,65},{2,98}... | collective-permute-start | bytes 21512 | tf_op jit(solution)/shard_map/ppermute | solution.py:411
  67.8 4.6 %collective-permute-start.12 = (f32[1792]{0:T(1024)S(1)}, f32[1792]{0:T(1024)S(1)}, u32[]{:S(2)}, u32[]{:S(2)}) collective-permute-start(f32[1792]{0:T(1024)S(1)} %pad_maximum_fusion.2), channel_id=1, source_target_pairs={{0,32},{32,64},{64,96},{96,0},{1,33},{33,65},{65,97},{97,1},{2,34}... | collective-permute-start | bytes 21512 | tf_op jit(solution)/shard_map/ppermute | solution.py:411
  68.2 4.3 %collective-permute-start.11 = (f32[1888]{0:T(1024)S(1)}, f32[1888]{0:T(1024)S(1)}, u32[]{:S(2)}, u32[]{:S(2)}) collective-permute-start(f32[1888]{0:T(1024)S(1)} %pad_maximum_fusion.1), channel_id=1, source_target_pairs={{0,1},{1,2},{2,3},{3,4},{4,5},{5,6},{6,7},{7,0},{8,9},{9,10},{10,1... | collective-permute-start | bytes 22664 | tf_op jit(solution)/shard_map/ppermute | solution.py:411
  69.6 5.8 %collective-permute-start.10 = (f32[1888]{0:T(1024)S(1)}, f32[1888]{0:T(1024)S(1)}, u32[]{:S(2)}, u32[]{:S(2)}) collective-permute-start(f32[1888]{0:T(1024)S(1)} %pad_maximum_fusion), channel_id=1, source_target_pairs={{0,7},{1,0},{2,1},{3,2},{4,3},{5,4},{6,5},{7,6},{8,15},{9,8},{10,9... | collective-permute-start | bytes 22664 | tf_op jit(solution)/shard_map/ppermute | solution.py:411
  (1 other events, 0.7 us)

commit v4 on v3

--- a/solution.py
+++ b/solution.py
@@ -46,14 +46,14 @@
 
 def fold(parts):
     rows = lax.broadcasted_iota(jnp.int32, parts[0].shape, 0)
-    step = len(parts) // 2
-    while step:
+    step = 1
+    while len(parts) > 1:
         low = (rows & step) == 0
         parts = [
-            jnp.where(low, p + pltpu.roll(p, 8 - step, 0), q + pltpu.roll(q, step, 0))
-            for p, q in zip(parts[:step], parts[step:])
+            jnp.where(low, p, q) + pltpu.roll(jnp.where(low, q, p), step, 0)
+            for p, q in zip(parts[0::2], parts[1::2])
         ]
-        step //= 2
+        step *= 2
     return parts[0]
 
 
@@ -116,9 +116,13 @@
         for k in range(2):
             mask = spots == jnp.broadcast_to(line[j + k : j + k + 1], (rows, LANES))
             for f in range(count):
-                found = wide[rows * f : rows * f + rows, k * LANES : (k + 1) * LANES]
-                found = jnp.where(mask, found, 0.0)
-                parts[f].append(jnp.sum(found.reshape(rows // 8, 8, LANES), axis=0))
+                found = jnp.zeros((8, LANES), jnp.float32)
+                for row in range(0, rows, 8):
+                    at = slice(rows * f + row, rows * f + row + 8)
+                    found = jnp.where(
+                        mask[row : row + 8], wide[at, k * LANES : (k + 1) * LANES], found
+                    )
+                parts[f].append(found)
     return [fold(p) for p in parts]
 
 
@@ -196,11 +200,25 @@
     leave(low, high, *inputs, new_ref, low * 8 * UNROLL, moved_ref, table)
 
 
+def places_of(colloid):
+    owner = colloid // COLLOIDS_PER_UNIT
+    code = jnp.zeros_like(colloid)
+    stride = 1
+    for axis, up in (("gz", 5), ("gy", 3), ("gx", 1)):
+        size = lax.axis_size(axis)
+        apart = (owner // stride - lax.axis_index(axis) + size) % size
+        code = jnp.where(apart == 1, up, jnp.where(apart == size - 1, up + 1, code))
+        stride *= size
+    return code * COLLOIDS_PER_UNIT + colloid % COLLOIDS_PER_UNIT
+
+
 def last_kernel(low, high, *refs):
     inputs, refs = refs[:6], refs[6:]
     before_ref, parts, refs = refs[0], refs[1:3], refs[3:]
-    particle_ref, place_ref, weight_ref = refs[:3]
-    kept_ref, moved_ref, force_ref, moved, table, held = refs[-6:]
+    particle_ref, colloid_ref, weight_ref = refs[:3]
+    faces = refs[3:5]
+    kept_ref, own_ref, *outs = refs[-11:-3]
+    moved, table, held = refs[-3:]
     dir_ref = inputs[4]
     moved[...] = before_ref[...]
     start = 0
@@ -208,7 +226,10 @@
         held[:, start : start + part.shape[1], :] = part[...]
         start += part.shape[1]
     leave(low, high, *inputs, held, 0, moved, table)
-    moved_ref[...] = moved[0:48] + moved[48:96]
+    for number, out in enumerate(outs):
+        for c in range(3):
+            at = 16 * c + 2 * number
+            out[2 * c : 2 * c + 2, :] = moved[at : at + 2, :] + moved[48 + at : 50 + at, :]
 
     def keep(i, carry):
         line = pl.multiple_of(i * 8, 8)
@@ -230,17 +251,64 @@
         at = slice(8 * part, 8 * part + 8)
         weight = weight_ref[at, :]
         terms = [weight * x for x in pick(wide, particle_ref[at, :], lines, lanes)] + [weight]
-        force = force + scatter(terms, place_ref[at, :], 16, False, lanes)
-    force_ref[...] = force[0:64] + force[64:128]
-
-
-def call(kernel, name, outs, scratch, flops, args):
+        force = force + scatter(terms, places_of(colloid_ref[at, :]), 16, False, lanes)
+    force = force[0:64] + force[64:128]
+    for f in range(4):
+        own_ref[2 * f : 2 * f + 2, :] = force[16 * f : 16 * f + 2]
+        for number, out in enumerate(outs):
+            at = 16 * f + 2 * number + 2
+            out[6 + 2 * f : 8 + 2 * f, :] = force[at : at + 2]
+    for out, face in zip(outs[4:], faces):
+        out[14:15, :] = face[...]
+
+
+def prepare_kernel(shift_ref, axis_ref, sign_ref, first_ref, last_ref, rise_ref, fall_ref):
+    rows = lax.broadcasted_iota(jnp.int32, (8, LANES), 0)
+    sign = jnp.zeros((8, LANES), jnp.int32)
+    for dim in range(3):
+        sign = jnp.where(rows == dim, shift_ref[0, dim], sign)
+    sign_ref[...] = sign
+    up = jnp.full(rise_ref.shape, shift_ref[0, 0], jnp.int32) > 0
+    rise_ref[...] = jnp.where(up, axis_ref[0], axis_ref[1])
+    fall_ref[...] = jnp.where(up, axis_ref[1], axis_ref[0])
+    first_ref[...] = rise_ref[0 : first_ref.shape[0], :]
+    last_ref[...] = fall_ref[fall_ref.shape[0] - last_ref.shape[0] :, :]
+
+
+def finish_kernel(sign_ref, mean_ref, own_ref, speed_ref, *refs):
+    came, (mean_out, moved_out, force_out) = refs[:6], refs[6:]
+    mean = mean_ref[...]
+    rows = mean.shape[0]
+    sides = [jnp.broadcast_to(x[14:15, :], (8, LANES)).T[:rows, 0:1] for x in came[4:]]
+    lane = lax.broadcasted_iota(jnp.int32, mean.shape, 1)
+    ahead_mean = jnp.where(lane == LANES - 1, sides[1], pltpu.roll(mean, LANES - 1, 1))
+    behind_mean = jnp.where(lane == 0, sides[0], pltpu.roll(mean, 1, 1))
+    up = jnp.broadcast_to(sign_ref[2:3, :], mean.shape) > 0
+    mean_out[...] = jnp.where(up, ahead_mean, behind_mean)
+    total = own_ref[...]
+    for x in came:
+        total = total + x[6:14, :]
+    for c in range(3):
+        pieces = []
+        for x in came:
+            pieces += [x[2 * c : 2 * c + 1, :], x[2 * c + 1 : 2 * c + 2, : CAP - LANES]]
+        moved_out[c : c + 1, :] = jnp.concatenate(pieces, axis=1)
+        for half in range(2):
+            at = slice(half * LANES, half * LANES + LANES)
+            weight = total[6 + half : 7 + half]
+            rest = total[2 * c + half : 2 * c + half + 1] - weight * speed_ref[c : c + 1, at]
+            force_out[c : c + 1, at] = rest / jnp.maximum(weight, 1.0)
+
+
+def call(kernel, name, outs, scratch, flops, args, scalars=0):
     vmem = pl.BlockSpec(memory_space=pltpu.VMEM)
+    smem = pl.BlockSpec(memory_space=pltpu.SMEM)
+    outs = [out if hasattr(out, "dtype") else jax.ShapeDtypeStruct(out, jnp.float32) for out in outs]
     return pl.pallas_call(
         kernel,
         name=name,
-        out_shape=[jax.ShapeDtypeStruct(shape, jnp.float32) for shape in outs],
-        in_specs=[vmem] * len(args),
+        out_shape=outs,
+        in_specs=[smem] * scalars + [vmem] * (len(args) - scalars),
         out_specs=[vmem] * len(outs),
         scratch_shapes=scratch,
         compiler_params=pltpu.CompilerParams(vmem_limit_bytes=VMEM_LIMIT),
@@ -269,15 +337,10 @@
     return jnp.concatenate([rim, lax.slice_in_dim(x, 0, x.shape[dim] - 1, axis=dim)], axis=dim)
 
 
-def axis_round(at, up, dim, axis):
-    rise = jnp.where(up, at[0], at[1])
-    fall = jnp.where(up, at[1], at[0])
-    upper = lax.ppermute(first(rise, dim), axis, ring(axis, -1))
-    lower = lax.ppermute(last(fall, dim), axis, ring(axis, 1))
-    rise = ahead(rise, upper, dim)
-    fall = behind(fall, lower, dim)
-    at = jnp.stack([jnp.where(up, rise, fall), jnp.where(up, fall, rise)])
-    return at, (upper, lower)
+def axis_round(rise, fall, sent, dim, axis):
+    upper = lax.ppermute(sent[0], axis, ring(axis, -1))
+    lower = lax.ppermute(sent[1], axis, ring(axis, 1))
+    return ahead(rise, upper, dim), behind(fall, lower, dim), (upper, lower)
 
 
 def mean_round(mean, up, dim, axis):
@@ -301,20 +364,6 @@
 ):
     particles = velocities.shape[1]
     cells_x, cells_y, cells_z = axis_index.shape[1:]
-    up = [grid_shift[0, dim] > 0 for dim in range(3)]
-
-    size_x = lax.axis_size("gx")
-    size_y = lax.axis_size("gy")
-    size_z = lax.axis_size("gz")
-    owner = contact_colloid // COLLOIDS_PER_UNIT
-    apart_x = (owner // (size_y * size_z) - lax.axis_index("gx")) % size_x
-    apart_y = (owner // size_z % size_y - lax.axis_index("gy")) % size_y
-    apart_z = (owner % size_z - lax.axis_index("gz")) % size_z
-    code = jnp.where(apart_z == 1, 5, jnp.where(apart_z == size_z - 1, 6, 0))
-    code = jnp.where(apart_y == 1, 3, jnp.where(apart_y == size_y - 1, 4, code))
-    code = jnp.where(apart_x == 1, 1, jnp.where(apart_x == size_x - 1, 2, code))
-    place = code * COLLOIDS_PER_UNIT + contact_colloid % COLLOIDS_PER_UNIT
-
     lines = particles // LANES
     steps = lines // (8 * UNROLL)
     cuts = (0, steps * 3 // 10, steps * 6 // 10, steps)
@@ -325,10 +374,30 @@
     table = pltpu.VMEM((128, 256), jnp.bfloat16)
     pair_flops = 2 * 224 * 128 * particles
 
-    axes = axis_index
+    plane, cells_all = cells_y, cells_x * cells_y
+    whole = jax.ShapeDtypeStruct((cells_all, cells_z), jnp.int32)
+    rim = jax.ShapeDtypeStruct((plane, cells_z), jnp.int32)
+    sign, first_rim, last_rim, rise, fall = call(
+        prepare_kernel,
+        "prepare",
+        [jax.ShapeDtypeStruct((8, LANES), jnp.int32), rim, rim, whole, whole],
+        [],
+        1 << 16,
+        (grid_shift, axis_index.reshape(2, cells_all, cells_z)),
+        scalars=1,
+    )
+    up = [sign[dim, 0] > 0 for dim in range(3)]
+    rise = rise.reshape(cells_x, cells_y, cells_z)
+    fall = fall.reshape(cells_x, cells_y, cells_z)
+    sent = (first_rim[None], last_rim[None])
     summed = ()
     for dim, axis in enumerate(("gx", "gy", "gz")):
-        axes, rims = axis_round(axes, up[dim], dim, axis)
+        rise, fall, rims = axis_round(rise, fall, sent, dim, axis)
+        axes = (jnp.where(up[dim], rise, fall), jnp.where(up[dim], fall, rise))
+        if dim < 2:
+            rise = jnp.where(up[dim + 1], axes[0], axes[1])
+            fall = jnp.where(up[dim + 1], axes[1], axes[0])
+            sent = (first(rise, dim + 1), last(fall, dim + 1))
         low, high = spans[dim]
         ends = dim == 2
         (result,) = call(
@@ -341,7 +410,7 @@
         )
         summed = (result,) + rims
     mean0 = result
-    axes = axes.reshape(2, cells_x * cells_y, cells_z)
+    axes = [x.reshape(cells_all, cells_z) for x in axes]
     moving, mean1 = call(
         turn_kernel,
         "turn",
@@ -374,11 +443,15 @@
         )
         parts.append(part)
         tied = (moved,) + rims
+    faces = [
+        jnp.pad(x.reshape(1, -1), ((0, 0), (0, LANES - 3 * cells_all)))
+        for x in (last(mean, 3), first(mean, 3))
+    ]
     low, high = spans[2]
-    kept, moved, force = call(
+    kept, own, *blocks = call(
         functools.partial(last_kernel, low, high),
         "last",
-        [(3, particles + 6 * CAP), (48, LANES), (64, LANES)],
+        [(3, particles + 6 * CAP), (8, LANES)] + [(14, LANES)] * 4 + [(15, LANES)] * 2,
         [
             pltpu.VMEM((96, LANES), jnp.float32),
             table,
@@ -389,33 +462,26 @@
         + (moved, *parts)
         + (
             contact_particle.reshape(-1, LANES),
-            place.reshape(-1, LANES),
+            contact_colloid.reshape(-1, LANES),
             contact_weight.reshape(-1, LANES),
+            *faces,
         )
         + rims,
     )
-    moved = moved.reshape(3, 16, LANES)
-    force = force.reshape(4, 16, LANES)
-    sums = force[:, 0:2].reshape(4, COLLOIDS_PER_UNIT)
-    arrivals = []
-    faces = (last(mean, 3), first(mean, 3))
-    got = []
-    for number in range(6):
+    came = []
+    for number, block in enumerate(blocks):
         axis, by = ("gx", "gy", "gz")[number // 2], 1 - 2 * (number % 2)
-        sent = [
-            moved[:, 2 * number : 2 * number + 2].reshape(-1),
-            force[:, 2 * number + 2 : 2 * number + 4].reshape(-1),
-        ]
-        if axis == "gz":
-            sent.append(faces[number % 2].reshape(-1))
-        came = lax.ppermute(jnp.concatenate(sent), axis, ring(axis, by))
-        arrivals.append(came[0:768].reshape(3, 256)[:, :CAP])
-        sums = sums + came[768:1792].reshape(4, COLLOIDS_PER_UNIT)
-        if axis == "gz":
-            got.append(came[1792:].reshape(faces[0].shape))
-    mean = jnp.where(up[2], ahead(mean, got[1], 3), behind(mean, got[0], 3))
-    migrated = lax.dynamic_update_slice(kept, jnp.concatenate(arrivals, axis=1), (0, particles))
-    colloid_force = (sums[0:3] - sums[3:4] * colloid_velocity) / jnp.maximum(sums[3:4], 1.0)
+        came.append(lax.ppermute(block, axis, ring(axis, by)))
+    mean, arrivals, colloid_force = call(
+        finish_kernel,
+        "finish",
+        [(3 * cells_all, cells_z), (3, 6 * CAP), colloid_velocity.shape],
+        [],
+        1 << 20,
+        (sign, mean.reshape(3 * cells_all, cells_z), own, colloid_velocity, *came),
+    )
+    mean = mean.reshape(3, cells_x, cells_y, cells_z)
+    migrated = lax.dynamic_update_slice(kept, arrivals, (0, particles))
     return (mean, migrated, colloid_force)
 
 

time: 79.1 us -> 79.7 us (level)
  the two profiles are of different devices: /device:TPU:6 before, /device:TPU:1 now
where the time goes in v4:
time: 79.7 us; the launch traced here: 79.3 us
  Pallas kernels  37.3 us (47%)
  starting transfers between devices  28.7 us (36%)
  local copies, waits for them, and re-layouts  5.85 us (7%)
  waiting for transfers between devices  4.43 us (6%)
  between operations  2.89 us (4%)
    pallas_call x9, Pallas kernels, call(): pl.pallas_call(kernel, name=name, out_shape=outs, in_specs=[smem] * scala...  37.3 us
    ppermute x6, starting transfers between devices, body(): came.append(lax.ppermute(block, axis, ring(axis, by)))  9.23 us
    ppermute x3, starting transfers between devices, axis_round(): lower = lax.ppermute(sent[1], axis, ring(axis, 1))  6.28 us
    ppermute x2, starting transfers between devices, mean_round(): lower = lax.ppermute(last(mean, dim + 1), axis, ring(axis, 1))  5.38 us
    ppermute x3, starting transfers between devices, axis_round(): upper = lax.ppermute(sent[0], axis, ring(axis, -1))  5.16 us
    unnamed x22, local copies, waits for them, and re-layouts  4.18 us
    ppermute x2, starting transfers between devices, mean_round(): upper = lax.ppermute(first(mean, dim + 1), axis, ring(axis, -1))  2.67 us
    ppermute x6, waiting for transfers between devices, body(): came.append(lax.ppermute(block, axis, ring(axis, by)))  1.91 us
  transfers between devices with their start and end apart: 16, of which 3 were waited for; matrix products, arithmetic and copies ran while one was open for 1% of the time, Pallas kernels for 18%

profile of v4, /device:TPU:1, one launch (start us, length us, event | category | flops | bytes accessed | tf_op | source)
XLA Modules:
  0.0 79.3 jit_solution(12331283499887397970)
XLA Ops:
  0.6 0.7 copy-done.2
  1.3 0.8 copy-done
  2.6 5.1 %collective-permute-start.1 = (s32[1,8,128]{2,1,0:T(8,128)S(1)}, s32[1,8,128]{2,1,0:T(8,128)S(1)}, u32[]{:S(2)}, u32[]{:S(2)}) collective-permute-start(s32[1,8,128]{2,1,0:T(8,128)S(1)} %bitcast.57), channel_id=1, source_target_pairs={{0,32},{32,64},{64,96},{96,0},{1,33},{33,65},{65,97},{97,1},{2,34}... | collective-permute-start | bytes 12296 | tf_op jit(solution)/shard_map/ppermute | solution.py:342
  8.2 1.1 %copy-done.3 = f32[3,40960]{1,0:T(4,128)S(1)} copy-done((f32[3,40960]{1,0:T(4,128)S(1)}, f32[3,40960]{1,0:T(4,128)}, u32[]{:S(2)}) %copy-start.3) | copy-done | bytes 491544
  9.3 1.0 %copy-done.4 = s32[2,40960]{1,0:T(2,128)S(1)} copy-done((s32[2,40960]{1,0:T(2,128)S(1)}, s32[2,40960]{1,0:T(2,128)}, u32[]{:S(2)}) %copy-start.4) | copy-done | bytes 327704
  10.3 1.9 %sums_0.1.refs_0_ = f32[224,128]{1,0:T(8,128)S(1)} custom-call(f32[320,3,128]{2,1,0:T(4,128)S(1)} %bitcast.36, s32[320,2,128]{2,1,0:T(2,128)S(1)} %bitcast.40), custom_call_target="tpu_custom_call" | custom-call | flops 782936768 | bytes 2097152 | tf_op jit(solution)/shard_map/sums_0/pallas_call | solution.py:307
  14.2 2.8 %collective-permute-start.2 = (s32[4,1,128]{2,1,0:T(1,128)S(1)}, s32[4,1,128]{2,1,0:T(1,128)S(1)}, u32[]{:S(2)}, u32[]{:S(2)}) collective-permute-start(s32[4,1,128]{2,1,0:T(1,128)S(1)} %slice.100), channel_id=1, source_target_pairs={{0,24},{8,0},{16,8},{24,16},{1,25},{9,1},{17,9},{25,17},{2,26},{10... | collective-permute-start | bytes 6152 | tf_op jit(solution)/shard_map/ppermute | solution.py:341
  17.0 1.9 %sums_1.1.refs_0_ = f32[224,128]{1,0:T(8,128)S(1)} custom-call(f32[320,3,128]{2,1,0:T(4,128)S(1)} %bitcast.37, s32[320,2,128]{2,1,0:T(2,128)S(1)} %bitcast.41, f32[224,128]{1,0:T(8,128)S(1)} %sums_0.1.refs_0_, s32[1,8,128]{2,1,0:T(8,128)S(1)} %collective-permute-done.refs_1_, s32[1,8,128]{2,1,0:T(8,128)S(1)} %collective-permute-done.1.refs_2_), custom_call_target="tpu_custom_call" | custom-call | flops 782936768 | bytes 2097152 | tf_op jit(solution)/shard_map/sums_1/pallas_call | solution.py:307
  19.0 1.7 %collective-permute-done.3.refs_2_ = s32[4,1,128]{2,1,0:T(1,128)S(1)} collective-permute-done((s32[4,1,128]{2,1,0:T(1,128)S(1)}, s32[4,1,128]{2,1,0:T(1,128)S(1)}, u32[]{:S(2)}, u32[]{:S(2)}) %collective-permute-start.3) | collective-permute-done | bytes 2080 | tf_op jit(solution)/shard_map/ppermute | solution.py:342
  20.8 1.2 %collective-permute-start.5 = (s32[4,8,1]{2,1,0:T(8,128)S(1)}, s32[4,8,1]{2,1,0:T(8,128)S(1)}, u32[]{:S(2)}, u32[]{:S(2)}) collective-permute-start(s32[4,8,1]{2,1,0:T(8,128)S(1)} %slice.106), channel_id=1, source_target_pairs={{0,1},{1,2},{2,3},{3,4},{4,5},{5,6},{6,7},{7,0},{8,9},{9,10},{10,1... | collective-permute-start | bytes 392 | tf_op jit(solution)/shard_map/ppermute | solution.py:342
  22.1 2.4 %collective-permute-start.4 = (s32[4,8,1]{2,1,0:T(8,128)S(1)}, s32[4,8,1]{2,1,0:T(8,128)S(1)}, u32[]{:S(2)}, u32[]{:S(2)}) collective-permute-start(s32[4,8,1]{2,1,0:T(8,128)S(1)} %bitcast.59), channel_id=1, source_target_pairs={{0,7},{1,0},{2,1},{3,2},{4,3},{5,4},{6,5},{7,6},{8,15},{9,8},{10,9... | collective-permute-start | bytes 392 | tf_op jit(solution)/shard_map/ppermute | solution.py:341
  24.4 2.6 %sums_2.1.mean_ref = f32[96,128]{1,0:T(8,128)S(1)} custom-call(f32[320,3,128]{2,1,0:T(4,128)S(1)} %bitcast.38, s32[320,2,128]{2,1,0:T(2,128)S(1)} %bitcast.42, f32[224,128]{1,0:T(8,128)S(1)} %sums_1.1.refs_0_, s32[4,1,128]{2,1,0:T(1,128)S(1)} %collective-permute-done.2.refs_1_, s32[4,1,128]{2,1,0:T(1,128)S(1)} %collective-permute-done.3.refs_2_), custom_call_target="tpu_custom_call" | custom-call | flops 782936768 | bytes 2097152 | tf_op jit(solution)/shard_map/sums_2/pallas_call | solution.py:307
  27.1 14.3 %turn.1 = (f32[3,320,128]{2,1,0:T(8,128)S(1)}, f32[96,128]{1,0:T(8,128)S(1)}) custom-call(f32[320,3,128]{2,1,0:T(4,128)S(1)} %bitcast.39, s32[320,2,128]{2,1,0:T(2,128)S(1)} %bitcast.43, f32[96,128]{1,0:T(8,128)S(1)} %sums_2.1.mean_ref, s32[32,128]{1,0:T(8,128)S(1)} %get-tuple-element.50.axis_ref), custom_call_target="tpu_custom_call" | custom-call | flops 4697620480 | bytes 2097152 | tf_op jit(solution)/shard_map/turn/pallas_call | solution.py:307
  41.5 5.3 %collective-permute-start.7 = (f32[3,1,8,128]{3,2,1,0:T(8,128)S(1)}, f32[3,1,8,128]{3,2,1,0:T(8,128)S(1)}, u32[]{:S(2)}, u32[]{:S(2)}) collective-permute-start(f32[3,1,8,128]{3,2,1,0:T(8,128)S(1)} %get-tuple-element.55), channel_id=1, source_target_pairs={{0,32},{32,64},{64,96},{96,0},{1,33},{33,65},{65,97},{97,1},{2,34}... | collective-permute-start | bytes 36872 | tf_op jit(solution)/shard_map/ppermute | solution.py:347
  46.8 3.8 %part_0.1 = (f32[3,96,128]{2,1,0:T(8,128)S(1)}, f32[96,128]{1,0:T(8,128)S(1)}) custom-call(f32[3,320,128]{2,1,0:T(8,128)S(1)} %get-tuple-element.31.refs_0_, s32[320,2,128]{2,1,0:T(2,128)S(1)} %bitcast.44, f32[96,128]{1,0:T(8,128)S(1)} %get-tuple-element.30.refs_2_, s32[32,128]{1,0:T(8,128)S(1)} %get-tuple-element.49.refs_3_, s32[320,128]{1,0:T(8,128)S(1)} %bitcast.47, ...), custom_call_target="tpu_custom_call" | custom-call | flops 1174405120 | bytes 2097152 | tf_op jit(solution)/shard_map/part_0/pallas_call | solution.py:307
  50.6 0.8 %collective-permute-done.6.refs_7_ = f32[3,1,8,128]{3,2,1,0:T(8,128)S(1)} collective-permute-done((f32[3,1,8,128]{3,2,1,0:T(8,128)S(1)}, f32[3,1,8,128]{3,2,1,0:T(8,128)S(1)}, u32[]{:S(2)}, u32[]{:S(2)}) %collective-permute-start.6) | collective-permute-done | bytes 12320 | tf_op jit(solution)/shard_map/ppermute | solution.py:348
  51.6 2.7 %collective-permute-start.8 = (f32[3,4,1,128]{3,2,1,0:T(1,128)S(1)}, f32[3,4,1,128]{3,2,1,0:T(1,128)S(1)}, u32[]{:S(2)}, u32[]{:S(2)}) collective-permute-start(f32[3,4,1,128]{3,2,1,0:T(1,128)S(1)} %get-tuple-element.52), channel_id=1, source_target_pairs={{0,24},{8,0},{16,8},{24,16},{1,25},{9,1},{17,9},{25,17},{2,26},{10... | collective-permute-start | bytes 18440 | tf_op jit(solution)/shard_map/ppermute | solution.py:348
  54.2 3.7 %part_1.1 = (f32[3,96,128]{2,1,0:T(8,128)S(1)}, f32[96,128]{1,0:T(8,128)S(1)}) custom-call(f32[3,320,128]{2,1,0:T(8,128)S(1)} %get-tuple-element.31.refs_0_, s32[320,2,128]{2,1,0:T(2,128)S(1)} %bitcast.45, f32[96,128]{1,0:T(8,128)S(1)} %get-tuple-element.30.refs_2_, s32[32,128]{1,0:T(8,128)S(1)} %get-tuple-element.49.refs_3_, s32[320,128]{1,0:T(8,128)S(1)} %bitcast.48, ...), custom_call_target="tpu_custom_call" | custom-call | flops 1174405120 | bytes 2097152 | tf_op jit(solution)/shard_map/part_1/pallas_call | solution.py:307
  59.1 7.6 %last.1 = (f32[3,41920]{1,0:T(4,128)}, f32[8,128]{1,0:T(8,128)S(1)}, f32[14,128]{1,0:T(8,128)S(1)}, f32[14,128]{1,0:T(8,128)S(1)}, f32[14,128]{1,0:T(8,128)S(1)}...) custom-call(f32[3,320,128]{2,1,0:T(8,128)S(1)} %get-tuple-element.31.refs_0_, ...), custom_call_target="tpu_custom_call" | custom-call | flops 2348810240 | bytes 2097152 | tf_op jit(solution)/shard_map/last/pallas_call | solution.py:307
  66.6 3.0 %collective-permute-start.10 = (f32[14,128]{1,0:T(8,128)S(1)}, f32[14,128]{1,0:T(8,128)S(1)}, u32[]{:S(2)}, u32[]{:S(2)}) collective-permute-start(f32[14,128]{1,0:T(8,128)S(1)} %get-tuple-element.37), channel_id=1, source_target_pairs={{0,32},{32,64},{64,96},{96,0},{1,33},{33,65},{65,97},{97,1},{2,34}... | collective-permute-start | bytes 21512 | tf_op jit(solution)/shard_map/ppermute | solution.py:474
  69.6 3.6 %collective-permute-start.15 = (f32[15,128]{1,0:T(8,128)S(1)}, f32[15,128]{1,0:T(8,128)S(1)}, u32[]{:S(2)}, u32[]{:S(2)}) collective-permute-start(f32[15,128]{1,0:T(8,128)S(1)} %get-tuple-element.42), channel_id=1, source_target_pairs={{0,7},{1,0},{2,1},{3,2},{4,3},{5,4},{6,5},{7,6},{8,15},{9,8},{10,9... | collective-permute-start | bytes 23048 | tf_op jit(solution)/shard_map/ppermute | solution.py:474
  73.2 2.7 %collective-permute-start.13 = (f32[14,128]{1,0:T(8,128)S(1)}, f32[14,128]{1,0:T(8,128)S(1)}, u32[]{:S(2)}, u32[]{:S(2)}) collective-permute-start(f32[14,128]{1,0:T(8,128)S(1)} %get-tuple-element.40), channel_id=1, source_target_pairs={{0,24},{8,0},{16,8},{24,16},{1,25},{9,1},{17,9},{25,17},{2,26},{10... | collective-permute-start | bytes 21512 | tf_op jit(solution)/shard_map/ppermute | solution.py:474
  75.9 1.9 %collective-permute-done.11.refs_1_ = f32[14,128]{1,0:T(8,128)S(1)} collective-permute-done((f32[14,128]{1,0:T(8,128)S(1)}, f32[14,128]{1,0:T(8,128)S(1)}, u32[]{:S(2)}, u32[]{:S(2)}) %collective-permute-start.11) | collective-permute-done | bytes 7200 | tf_op jit(solution)/shard_map/ppermute | solution.py:474
  77.8 0.9 %finish.1 = (f32[96,128]{1,0:T(8,128)}, f32[3,960]{1,0:T(4,128)S(1)}, f32[3,256]{1,0:T(4,128)}) custom-call(s32[8,128]{1,0:T(8,128)S(1)} %get-tuple-element.25.sign_ref, f32[96,128]{1,0:T(8,128)S(1)} %bitcast.32, f32[8,128]{1,0:T(8,128)S(1)} %get-tuple-element.36.own_ref, f32[3,256]{1,0:T(4,128)S(1)} %copy-done.1, ...), custom_call_target="tpu_custom_call" | custom-call | flops 1048576 | bytes 2097152 | tf_op jit(solution)/shard_map/finish/pallas_call | solution.py:307
  (62 shorter events, 3.2 us)
Async XLA Ops:
  1.3 0.8 copy-start
  2.6 11.5 %collective-permute-start.1 = (s32[1,8,128]{2,1,0:T(8,128)S(1)}, s32[1,8,128]{2,1,0:T(8,128)S(1)}, u32[]{:S(2)}, u32[]{:S(2)}) collective-permute-start(s32[1,8,128]{2,1,0:T(8,128)S(1)} %bitcast.57), channel_id=1, source_target_pairs={{0,32},{32,64},{64,96},{96,0},{1,33},{33,65},{65,97},{97,1},{2,34}... | collective-permute-start | bytes 12296 | tf_op jit(solution)/shard_map/ppermute | solution.py:342
  7.7 6.5 %collective-permute-start = (s32[1,8,128]{2,1,0:T(8,128)S(1)}, s32[1,8,128]{2,1,0:T(8,128)S(1)}, u32[]{:S(2)}, u32[]{:S(2)}) collective-permute-start(s32[1,8,128]{2,1,0:T(8,128)S(1)} %bitcast.56), channel_id=1, source_target_pairs={{0,96},{32,0},{64,32},{96,64},{1,97},{33,1},{65,33},{97,65},{2,98}... | collective-permute-start | bytes 12296 | tf_op jit(solution)/shard_map/ppermute | solution.py:341
  8.2 1.1 %copy-start.3 = (f32[3,40960]{1,0:T(4,128)S(1)}, f32[3,40960]{1,0:T(4,128)}, u32[]{:S(2)}) copy-start(f32[3,40960]{1,0:T(4,128)} %param.10) | copy-start | bytes 1474564
  9.3 1.0 %copy-start.4 = (s32[2,40960]{1,0:T(2,128)S(1)}, s32[2,40960]{1,0:T(2,128)}, u32[]{:S(2)}) copy-start(s32[2,40960]{1,0:T(2,128)} %param.11) | copy-start | bytes 983044
  14.2 4.8 %collective-permute-start.2 = (s32[4,1,128]{2,1,0:T(1,128)S(1)}, s32[4,1,128]{2,1,0:T(1,128)S(1)}, u32[]{:S(2)}, u32[]{:S(2)}) collective-permute-start(s32[4,1,128]{2,1,0:T(1,128)S(1)} %slice.100), channel_id=1, source_target_pairs={{0,24},{8,0},{16,8},{24,16},{1,25},{9,1},{17,9},{25,17},{2,26},{10... | collective-permute-start | bytes 6152 | tf_op jit(solution)/shard_map/ppermute | solution.py:341
  17.0 3.6 %collective-permute-start.3 = (s32[4,1,128]{2,1,0:T(1,128)S(1)}, s32[4,1,128]{2,1,0:T(1,128)S(1)}, u32[]{:S(2)}, u32[]{:S(2)}) collective-permute-start(s32[4,1,128]{2,1,0:T(1,128)S(1)} %slice.101), channel_id=1, source_target_pairs={{0,8},{8,16},{16,24},{24,0},{1,9},{9,17},{17,25},{25,1},{2,10},{10... | collective-permute-start | bytes 6152 | tf_op jit(solution)/shard_map/ppermute | solution.py:342
  20.8 6.2 %collective-permute-start.5 = (s32[4,8,1]{2,1,0:T(8,128)S(1)}, s32[4,8,1]{2,1,0:T(8,128)S(1)}, u32[]{:S(2)}, u32[]{:S(2)}) collective-permute-start(s32[4,8,1]{2,1,0:T(8,128)S(1)} %slice.106), channel_id=1, source_target_pairs={{0,1},{1,2},{2,3},{3,4},{4,5},{5,6},{6,7},{7,0},{8,9},{9,10},{10,1... | collective-permute-start | bytes 392 | tf_op jit(solution)/shard_map/ppermute | solution.py:342
  22.1 5.0 %collective-permute-start.4 = (s32[4,8,1]{2,1,0:T(8,128)S(1)}, s32[4,8,1]{2,1,0:T(8,128)S(1)}, u32[]{:S(2)}, u32[]{:S(2)}) collective-permute-start(s32[4,8,1]{2,1,0:T(8,128)S(1)} %bitcast.59), channel_id=1, source_target_pairs={{0,7},{1,0},{2,1},{3,2},{4,3},{5,4},{6,5},{7,6},{8,15},{9,8},{10,9... | collective-permute-start | bytes 392 | tf_op jit(solution)/shard_map/ppermute | solution.py:341
  27.1 19.7 %copy-start.5 = (s32[2,40960]{1,0:T(2,128)S(1)}, s32[2,40960]{1,0:T(2,128)}, u32[]{:S(2)}) copy-start(s32[2,40960]{1,0:T(2,128)} %param.11) | copy-start | bytes 983044
  27.1 19.7 %copy-start.7 = (s32[40960]{0:T(1024)S(1)}, s32[40960]{0:T(1024)}, u32[]{:S(2)}) copy-start(s32[40960]{0:T(1024)} %param.15) | copy-start | bytes 491524
  41.5 5.4 %copy-start.6 = (s32[40960]{0:T(1024)S(1)}, s32[40960]{0:T(1024)}, u32[]{:S(2)}) copy-start(s32[40960]{0:T(1024)} %param.14) | copy-start | bytes 491524
  41.5 9.1 %collective-permute-start.7 = (f32[3,1,8,128]{3,2,1,0:T(8,128)S(1)}, f32[3,1,8,128]{3,2,1,0:T(8,128)S(1)}, u32[]{:S(2)}, u32[]{:S(2)}) collective-permute-start(f32[3,1,8,128]{3,2,1,0:T(8,128)S(1)} %get-tuple-element.55), channel_id=1, source_target_pairs={{0,32},{32,64},{64,96},{96,0},{1,33},{33,65},{65,97},{97,1},{2,34}... | collective-permute-start | bytes 36872 | tf_op jit(solution)/shard_map/ppermute | solution.py:347
  46.8 4.6 %collective-permute-start.6 = (f32[3,1,8,128]{3,2,1,0:T(8,128)S(1)}, f32[3,1,8,128]{3,2,1,0:T(8,128)S(1)}, u32[]{:S(2)}, u32[]{:S(2)}) collective-permute-start(f32[3,1,8,128]{3,2,1,0:T(8,128)S(1)} %get-tuple-element.56), channel_id=1, source_target_pairs={{0,96},{32,0},{64,32},{96,64},{1,97},{33,1},{65,33},{97,65},{2,98}... | collective-permute-start | bytes 36872 | tf_op jit(solution)/shard_map/ppermute | solution.py:348
  51.5 6.5 %collective-permute-start.9 = (f32[3,4,1,128]{3,2,1,0:T(1,128)S(1)}, f32[3,4,1,128]{3,2,1,0:T(1,128)S(1)}, u32[]{:S(2)}, u32[]{:S(2)}) collective-permute-start(f32[3,4,1,128]{3,2,1,0:T(1,128)S(1)} %get-tuple-element.51), channel_id=1, source_target_pairs={{0,8},{8,16},{16,24},{24,0},{1,9},{9,17},{17,25},{25,1},{2,10},{10... | collective-permute-start | bytes 18440 | tf_op jit(solution)/shard_map/ppermute | solution.py:347
  51.6 6.4 %collective-permute-start.8 = (f32[3,4,1,128]{3,2,1,0:T(1,128)S(1)}, f32[3,4,1,128]{3,2,1,0:T(1,128)S(1)}, u32[]{:S(2)}, u32[]{:S(2)}) collective-permute-start(f32[3,4,1,128]{3,2,1,0:T(1,128)S(1)} %get-tuple-element.52), channel_id=1, source_target_pairs={{0,24},{8,0},{16,8},{24,16},{1,25},{9,1},{17,9},{25,17},{2,26},{10... | collective-permute-start | bytes 18440 | tf_op jit(solution)/shard_map/ppermute | solution.py:348
  58.2 0.7 copy-start.10
  66.6 6.6 %collective-permute-start.10 = (f32[14,128]{1,0:T(8,128)S(1)}, f32[14,128]{1,0:T(8,128)S(1)}, u32[]{:S(2)}, u32[]{:S(2)}) collective-permute-start(f32[14,128]{1,0:T(8,128)S(1)} %get-tuple-element.37), channel_id=1, source_target_pairs={{0,32},{32,64},{64,96},{96,0},{1,33},{33,65},{65,97},{97,1},{2,34}... | collective-permute-start | bytes 21512 | tf_op jit(solution)/shard_map/ppermute | solution.py:474
  69.6 8.2 %collective-permute-start.14 = (f32[15,128]{1,0:T(8,128)S(1)}, f32[15,128]{1,0:T(8,128)S(1)}, u32[]{:S(2)}, u32[]{:S(2)}) collective-permute-start(f32[15,128]{1,0:T(8,128)S(1)} %get-tuple-element.41), channel_id=1, source_target_pairs={{0,1},{1,2},{2,3},{3,4},{4,5},{5,6},{6,7},{7,0},{8,9},{9,10},{10,1... | collective-permute-start | bytes 23048 | tf_op jit(solution)/shard_map/ppermute | solution.py:474
  69.6 8.2 %collective-permute-start.15 = (f32[15,128]{1,0:T(8,128)S(1)}, f32[15,128]{1,0:T(8,128)S(1)}, u32[]{:S(2)}, u32[]{:S(2)}) collective-permute-start(f32[15,128]{1,0:T(8,128)S(1)} %get-tuple-element.42), channel_id=1, source_target_pairs={{0,7},{1,0},{2,1},{3,2},{4,3},{5,4},{6,5},{7,6},{8,15},{9,8},{10,9... | collective-permute-start | bytes 23048 | tf_op jit(solution)/shard_map/ppermute | solution.py:474
  73.2 4.6 %copy-start.1 = (f32[3,256]{1,0:T(4,128)S(1)}, f32[3,256]{1,0:T(4,128)}, u32[]{:S(2)}) copy-start(f32[3,256]{1,0:T(4,128)} %speed_ref.1) | copy-start | bytes 9220
  73.2 4.6 %collective-permute-start.11 = (f32[14,128]{1,0:T(8,128)S(1)}, f32[14,128]{1,0:T(8,128)S(1)}, u32[]{:S(2)}, u32[]{:S(2)}) collective-permute-start(f32[14,128]{1,0:T(8,128)S(1)} %get-tuple-element.38), channel_id=1, source_target_pairs={{0,96},{32,0},{64,32},{96,64},{1,97},{33,1},{65,33},{97,65},{2,98}... | collective-permute-start | bytes 21512 | tf_op jit(solution)/shard_map/ppermute | solution.py:474
  73.2 4.6 %collective-permute-start.12 = (f32[14,128]{1,0:T(8,128)S(1)}, f32[14,128]{1,0:T(8,128)S(1)}, u32[]{:S(2)}, u32[]{:S(2)}) collective-permute-start(f32[14,128]{1,0:T(8,128)S(1)} %get-tuple-element.39), channel_id=1, source_target_pairs={{0,8},{8,16},{16,24},{24,0},{1,9},{9,17},{17,25},{25,1},{2,10},{10... | collective-permute-start | bytes 21512 | tf_op jit(solution)/shard_map/ppermute | solution.py:474
  73.2 4.6 %collective-permute-start.13 = (f32[14,128]{1,0:T(8,128)S(1)}, f32[14,128]{1,0:T(8,128)S(1)}, u32[]{:S(2)}, u32[]{:S(2)}) collective-permute-start(f32[14,128]{1,0:T(8,128)S(1)} %get-tuple-element.40), channel_id=1, source_target_pairs={{0,24},{8,0},{16,8},{24,16},{1,25},{9,1},{17,9},{25,17},{2,26},{10... | collective-permute-start | bytes 21512 | tf_op jit(solution)/shard_map/ppermute | solution.py:474
  (3 other events, 2.1 us)

commit v5 on v4

--- a/solution.py
+++ b/solution.py
@@ -386,7 +386,7 @@
         (grid_shift, axis_index.reshape(2, cells_all, cells_z)),
         scalars=1,
     )
-    up = [sign[dim, 0] > 0 for dim in range(3)]
+    up = [sign[dim] > 0 for dim in range(3)]
     rise = rise.reshape(cells_x, cells_y, cells_z)
     fall = fall.reshape(cells_x, cells_y, cells_z)
     sent = (first_rim[None], last_rim[None])

time: 79.7 us -> 78.1 us (0.980)
  the two profiles are of different devices: /device:TPU:1 before, /device:TPU:6 now
where the time goes in v5:
time: 78.1 us; the launch traced here: 77.8 us
  Pallas kernels  37.3 us (48%)
  starting transfers between devices  23.7 us (30%)
  waiting for transfers between devices  10.4 us (13%)
  local copies, waits for them, and re-layouts  5.33 us (7%)
  between operations  0.97 us (1%)
    pallas_call x9, Pallas kernels, call(): pl.pallas_call(kernel, name=name, out_shape=outs, in_specs=[smem] * scala...  37.3 us
    ppermute x6, starting transfers between devices, body(): came.append(lax.ppermute(block, axis, ring(axis, by)))  8.51 us
    ppermute x3, starting transfers between devices, axis_round(): upper = lax.ppermute(sent[0], axis, ring(axis, -1))  6.8 us
    ppermute x2, starting transfers between devices, mean_round(): upper = lax.ppermute(first(mean, dim + 1), axis, ring(axis, -1))  6.46 us
    ppermute x6, waiting for transfers between devices, body(): came.append(lax.ppermute(block, axis, ring(axis, by)))  4.63 us
    unnamed x22, local copies, waits for them, and re-layouts  4.18 us
    ppermute x3, waiting for transfers between devices, axis_round(): upper = lax.ppermute(sent[0], axis, ring(axis, -1))  2.9 us
    ppermute x3, waiting for transfers between devices, axis_round(): lower = lax.ppermute(sent[1], axis, ring(axis, 1))  2.83 us
  transfers between devices with their start and end apart: 16, of which 4 were waited for; matrix products, arithmetic and copies ran while one was open for 0% of the time, Pallas kernels for 18%

profile of v5, /device:TPU:6, one launch (start us, length us, event | category | flops | bytes accessed | tf_op | source)
XLA Modules:
  0.0 77.8 jit_solution(1573238952926951849)
XLA Ops:
  1.3 0.8 copy-done
  2.7 3.4 %collective-permute-start = (s32[1,8,128]{2,1,0:T(8,128)S(1)}, s32[1,8,128]{2,1,0:T(8,128)S(1)}, u32[]{:S(2)}, u32[]{:S(2)}) collective-permute-start(s32[1,8,128]{2,1,0:T(8,128)S(1)} %bitcast.61), channel_id=1, source_target_pairs={{0,96},{32,0},{64,32},{96,64},{1,97},{33,1},{65,33},{97,65},{2,98}... | collective-permute-start | bytes 12296 | tf_op jit(solution)/shard_map/ppermute | solution.py:341
  6.1 1.1 %copy-done.3 = f32[3,40960]{1,0:T(4,128)S(1)} copy-done((f32[3,40960]{1,0:T(4,128)S(1)}, f32[3,40960]{1,0:T(4,128)}, u32[]{:S(2)}) %copy-start.3) | copy-done | bytes 491544
  7.2 1.0 %copy-done.4 = s32[2,40960]{1,0:T(2,128)S(1)} copy-done((s32[2,40960]{1,0:T(2,128)S(1)}, s32[2,40960]{1,0:T(2,128)}, u32[]{:S(2)}) %copy-start.4) | copy-done | bytes 327704
  8.2 1.9 %sums_0.1.refs_0_ = f32[224,128]{1,0:T(8,128)S(1)} custom-call(f32[320,3,128]{2,1,0:T(4,128)S(1)} %bitcast.41, s32[320,2,128]{2,1,0:T(2,128)S(1)} %bitcast.45), custom_call_target="tpu_custom_call" | custom-call | flops 782936768 | bytes 2097152 | tf_op jit(solution)/shard_map/sums_0/pallas_call | solution.py:307
  10.2 3.1 %collective-permute-start.2 = (s32[4,1,128]{2,1,0:T(1,128)S(1)}, s32[4,1,128]{2,1,0:T(1,128)S(1)}, u32[]{:S(2)}, u32[]{:S(2)}) collective-permute-start(s32[4,1,128]{2,1,0:T(1,128)S(1)} %slice.100), channel_id=1, source_target_pairs={{0,24},{8,0},{16,8},{24,16},{1,25},{9,1},{17,9},{25,17},{2,26},{10... | collective-permute-start | bytes 6152 | tf_op jit(solution)/shard_map/ppermute | solution.py:341
  13.3 1.9 %sums_1.1.refs_0_ = f32[224,128]{1,0:T(8,128)S(1)} custom-call(f32[320,3,128]{2,1,0:T(4,128)S(1)} %bitcast.42, s32[320,2,128]{2,1,0:T(2,128)S(1)} %bitcast.46, f32[224,128]{1,0:T(8,128)S(1)} %sums_0.1.refs_0_, s32[1,8,128]{2,1,0:T(8,128)S(1)} %collective-permute-done.refs_1_, s32[1,8,128]{2,1,0:T(8,128)S(1)} %collective-permute-done.1.refs_2_), custom_call_target="tpu_custom_call" | custom-call | flops 782936768 | bytes 2097152 | tf_op jit(solution)/shard_map/sums_1/pallas_call | solution.py:307
  15.2 2.8 %collective-permute-done.3.refs_2_ = s32[4,1,128]{2,1,0:T(1,128)S(1)} collective-permute-done((s32[4,1,128]{2,1,0:T(1,128)S(1)}, s32[4,1,128]{2,1,0:T(1,128)S(1)}, u32[]{:S(2)}, u32[]{:S(2)}) %collective-permute-start.3) | collective-permute-done | bytes 2080 | tf_op jit(solution)/shard_map/ppermute | solution.py:342
  18.2 1.7 %collective-permute-start.5 = (s32[4,8,1]{2,1,0:T(8,128)S(1)}, s32[4,8,1]{2,1,0:T(8,128)S(1)}, u32[]{:S(2)}, u32[]{:S(2)}) collective-permute-start(s32[4,8,1]{2,1,0:T(8,128)S(1)} %slice.106), channel_id=1, source_target_pairs={{0,1},{1,2},{2,3},{3,4},{4,5},{5,6},{6,7},{7,0},{8,9},{9,10},{10,1... | collective-permute-start | bytes 392 | tf_op jit(solution)/shard_map/ppermute | solution.py:342
  20.3 2.6 %sums_2.1.mean_ref = f32[96,128]{1,0:T(8,128)S(1)} custom-call(f32[320,3,128]{2,1,0:T(4,128)S(1)} %bitcast.43, s32[320,2,128]{2,1,0:T(2,128)S(1)} %bitcast.47, f32[224,128]{1,0:T(8,128)S(1)} %sums_1.1.refs_0_, s32[4,1,128]{2,1,0:T(1,128)S(1)} %collective-permute-done.2.refs_1_, s32[4,1,128]{2,1,0:T(1,128)S(1)} %collective-permute-done.3.refs_2_), custom_call_target="tpu_custom_call" | custom-call | flops 782936768 | bytes 2097152 | tf_op jit(solution)/shard_map/sums_2/pallas_call | solution.py:307
  22.9 2.9 %collective-permute-done.4 = s32[4,8,1]{2,1,0:T(8,128)S(1)} collective-permute-done((s32[4,8,1]{2,1,0:T(8,128)S(1)}, s32[4,8,1]{2,1,0:T(8,128)S(1)}, u32[]{:S(2)}, u32[]{:S(2)}) %collective-permute-start.4) | collective-permute-done | bytes 160 | tf_op jit(solution)/shard_map/ppermute | solution.py:341
  25.9 14.3 %turn.1 = (f32[3,320,128]{2,1,0:T(8,128)S(1)}, f32[96,128]{1,0:T(8,128)S(1)}) custom-call(f32[320,3,128]{2,1,0:T(4,128)S(1)} %bitcast.44, s32[320,2,128]{2,1,0:T(2,128)S(1)} %bitcast.48, f32[96,128]{1,0:T(8,128)S(1)} %sums_2.1.mean_ref, s32[32,128]{1,0:T(8,128)S(1)} %get-tuple-element.53.axis_ref), custom_call_target="tpu_custom_call" | custom-call | flops 4697620480 | bytes 2097152 | tf_op jit(solution)/shard_map/turn/pallas_call | solution.py:307
  40.3 3.2 %collective-permute-start.6 = (f32[3,1,8,128]{3,2,1,0:T(8,128)S(1)}, f32[3,1,8,128]{3,2,1,0:T(8,128)S(1)}, u32[]{:S(2)}, u32[]{:S(2)}) collective-permute-start(f32[3,1,8,128]{3,2,1,0:T(8,128)S(1)} %get-tuple-element.59), channel_id=1, source_target_pairs={{0,96},{32,0},{64,32},{96,64},{1,97},{33,1},{65,33},{97,65},{2,98}... | collective-permute-start | bytes 36872 | tf_op jit(solution)/shard_map/ppermute | solution.py:348
  43.6 3.8 %part_0.1 = (f32[3,96,128]{2,1,0:T(8,128)S(1)}, f32[96,128]{1,0:T(8,128)S(1)}) custom-call(f32[3,320,128]{2,1,0:T(8,128)S(1)} %get-tuple-element.31.refs_0_, s32[320,2,128]{2,1,0:T(2,128)S(1)} %bitcast.49, f32[96,128]{1,0:T(8,128)S(1)} %get-tuple-element.30.refs_2_, s32[32,128]{1,0:T(8,128)S(1)} %get-tuple-element.52.refs_3_, s32[320,128]{1,0:T(8,128)S(1)} %bitcast.52, ...), custom_call_target="tpu_custom_call" | custom-call | flops 1174405120 | bytes 2097152 | tf_op jit(solution)/shard_map/part_0/pallas_call | solution.py:307
  47.5 3.2 %collective-permute-start.8 = (f32[3,4,1,128]{3,2,1,0:T(1,128)S(1)}, f32[3,4,1,128]{3,2,1,0:T(1,128)S(1)}, u32[]{:S(2)}, u32[]{:S(2)}) collective-permute-start(f32[3,4,1,128]{3,2,1,0:T(1,128)S(1)} %get-tuple-element.55), channel_id=1, source_target_pairs={{0,24},{8,0},{16,8},{24,16},{1,25},{9,1},{17,9},{25,17},{2,26},{10... | collective-permute-start | bytes 18440 | tf_op jit(solution)/shard_map/ppermute | solution.py:348
  50.7 3.7 %part_1.1 = (f32[3,96,128]{2,1,0:T(8,128)S(1)}, f32[96,128]{1,0:T(8,128)S(1)}) custom-call(f32[3,320,128]{2,1,0:T(8,128)S(1)} %get-tuple-element.31.refs_0_, s32[320,2,128]{2,1,0:T(2,128)S(1)} %bitcast.50, f32[96,128]{1,0:T(8,128)S(1)} %get-tuple-element.30.refs_2_, s32[32,128]{1,0:T(8,128)S(1)} %get-tuple-element.52.refs_3_, s32[320,128]{1,0:T(8,128)S(1)} %bitcast.53, ...), custom_call_target="tpu_custom_call" | custom-call | flops 1174405120 | bytes 2097152 | tf_op jit(solution)/shard_map/part_1/pallas_call | solution.py:307
  55.6 7.6 %last.1 = (f32[3,41920]{1,0:T(4,128)}, f32[8,128]{1,0:T(8,128)S(1)}, f32[14,128]{1,0:T(8,128)S(1)}, f32[14,128]{1,0:T(8,128)S(1)}, f32[14,128]{1,0:T(8,128)S(1)}...) custom-call(f32[3,320,128]{2,1,0:T(8,128)S(1)} %get-tuple-element.31.refs_0_, ...), custom_call_target="tpu_custom_call" | custom-call | flops 2348810240 | bytes 2097152 | tf_op jit(solution)/shard_map/last/pallas_call | solution.py:307
  63.8 2.6 %collective-permute-start.11 = (f32[14,128]{1,0:T(8,128)S(1)}, f32[14,128]{1,0:T(8,128)S(1)}, u32[]{:S(2)}, u32[]{:S(2)}) collective-permute-start(f32[14,128]{1,0:T(8,128)S(1)} %get-tuple-element.38), channel_id=1, source_target_pairs={{0,96},{32,0},{64,32},{96,64},{1,97},{33,1},{65,33},{97,65},{2,98}... | collective-permute-start | bytes 21512 | tf_op jit(solution)/shard_map/ppermute | solution.py:474
  66.4 3.2 %collective-permute-start.13 = (f32[14,128]{1,0:T(8,128)S(1)}, f32[14,128]{1,0:T(8,128)S(1)}, u32[]{:S(2)}, u32[]{:S(2)}) collective-permute-start(f32[14,128]{1,0:T(8,128)S(1)} %get-tuple-element.40), channel_id=1, source_target_pairs={{0,24},{8,0},{16,8},{24,16},{1,25},{9,1},{17,9},{25,17},{2,26},{10... | collective-permute-start | bytes 21512 | tf_op jit(solution)/shard_map/ppermute | solution.py:474
  69.6 0.9 %collective-permute-start.14 = (f32[15,128]{1,0:T(8,128)S(1)}, f32[15,128]{1,0:T(8,128)S(1)}, u32[]{:S(2)}, u32[]{:S(2)}) collective-permute-start(f32[15,128]{1,0:T(8,128)S(1)} %get-tuple-element.41), channel_id=1, source_target_pairs={{0,1},{1,2},{2,3},{3,4},{4,5},{5,6},{6,7},{7,0},{8,9},{9,10},{10,1... | collective-permute-start | bytes 23048 | tf_op jit(solution)/shard_map/ppermute | solution.py:474
  70.5 1.1 %collective-permute-start.15 = (f32[15,128]{1,0:T(8,128)S(1)}, f32[15,128]{1,0:T(8,128)S(1)}, u32[]{:S(2)}, u32[]{:S(2)}) collective-permute-start(f32[15,128]{1,0:T(8,128)S(1)} %get-tuple-element.42), channel_id=1, source_target_pairs={{0,7},{1,0},{2,1},{3,2},{4,3},{5,4},{6,5},{7,6},{8,15},{9,8},{10,9... | collective-permute-start | bytes 23048 | tf_op jit(solution)/shard_map/ppermute | solution.py:474
  71.7 1.6 %collective-permute-done.14.refs_4_ = f32[15,128]{1,0:T(8,128)S(1)} collective-permute-done((f32[15,128]{1,0:T(8,128)S(1)}, f32[15,128]{1,0:T(8,128)S(1)}, u32[]{:S(2)}, u32[]{:S(2)}) %collective-permute-start.14) | collective-permute-done | bytes 7712 | tf_op jit(solution)/shard_map/ppermute | solution.py:474
  73.3 3.0 %collective-permute-done.15.refs_5_ = f32[15,128]{1,0:T(8,128)S(1)} collective-permute-done((f32[15,128]{1,0:T(8,128)S(1)}, f32[15,128]{1,0:T(8,128)S(1)}, u32[]{:S(2)}, u32[]{:S(2)}) %collective-permute-start.15) | collective-permute-done | bytes 7712 | tf_op jit(solution)/shard_map/ppermute | solution.py:474
  76.3 0.9 %finish.1 = (f32[96,128]{1,0:T(8,128)}, f32[3,960]{1,0:T(4,128)S(1)}, f32[3,256]{1,0:T(4,128)}) custom-call(s32[8,128]{1,0:T(8,128)S(1)} %get-tuple-element.25.sign_ref, f32[96,128]{1,0:T(8,128)S(1)} %bitcast_select_fusion.mean_ref, f32[8,128]{1,0:T(8,128)S(1)} %get-tuple-element.36.own_ref, f32[3,256]{1,0:T(4,128)S(1)} %copy-done.1, ...), custom_call_target="tpu_custom_call" | custom-call | flops 1048576 | bytes 2097152 | tf_op jit(solution)/shard_map/finish/pallas_call | solution.py:307
  (63 shorter events, 4.5 us)
Async XLA Ops:
  1.3 0.8 copy-start
  2.6 7.5 %collective-permute-start.1 = (s32[1,8,128]{2,1,0:T(8,128)S(1)}, s32[1,8,128]{2,1,0:T(8,128)S(1)}, u32[]{:S(2)}, u32[]{:S(2)}) collective-permute-start(s32[1,8,128]{2,1,0:T(8,128)S(1)} %bitcast.62), channel_id=1, source_target_pairs={{0,32},{32,64},{64,96},{96,0},{1,33},{33,65},{65,97},{97,1},{2,34}... | collective-permute-start | bytes 12296 | tf_op jit(solution)/shard_map/ppermute | solution.py:342
  2.7 7.4 %collective-permute-start = (s32[1,8,128]{2,1,0:T(8,128)S(1)}, s32[1,8,128]{2,1,0:T(8,128)S(1)}, u32[]{:S(2)}, u32[]{:S(2)}) collective-permute-start(s32[1,8,128]{2,1,0:T(8,128)S(1)} %bitcast.61), channel_id=1, source_target_pairs={{0,96},{32,0},{64,32},{96,64},{1,97},{33,1},{65,33},{97,65},{2,98}... | collective-permute-start | bytes 12296 | tf_op jit(solution)/shard_map/ppermute | solution.py:341
  6.1 1.1 %copy-start.3 = (f32[3,40960]{1,0:T(4,128)S(1)}, f32[3,40960]{1,0:T(4,128)}, u32[]{:S(2)}) copy-start(f32[3,40960]{1,0:T(4,128)} %param.10) | copy-start | bytes 1474564
  7.2 1.0 %copy-start.4 = (s32[2,40960]{1,0:T(2,128)S(1)}, s32[2,40960]{1,0:T(2,128)}, u32[]{:S(2)}) copy-start(s32[2,40960]{1,0:T(2,128)} %param.11) | copy-start | bytes 983044
  10.2 5.0 %collective-permute-start.2 = (s32[4,1,128]{2,1,0:T(1,128)S(1)}, s32[4,1,128]{2,1,0:T(1,128)S(1)}, u32[]{:S(2)}, u32[]{:S(2)}) collective-permute-start(s32[4,1,128]{2,1,0:T(1,128)S(1)} %slice.100), channel_id=1, source_target_pairs={{0,24},{8,0},{16,8},{24,16},{1,25},{9,1},{17,9},{25,17},{2,26},{10... | collective-permute-start | bytes 6152 | tf_op jit(solution)/shard_map/ppermute | solution.py:341
  13.3 4.8 %collective-permute-start.3 = (s32[4,1,128]{2,1,0:T(1,128)S(1)}, s32[4,1,128]{2,1,0:T(1,128)S(1)}, u32[]{:S(2)}, u32[]{:S(2)}) collective-permute-start(s32[4,1,128]{2,1,0:T(1,128)S(1)} %slice.101), channel_id=1, source_target_pairs={{0,8},{8,16},{16,24},{24,0},{1,9},{9,17},{17,25},{25,1},{2,10},{10... | collective-permute-start | bytes 6152 | tf_op jit(solution)/shard_map/ppermute | solution.py:342
  18.2 4.6 %collective-permute-start.5 = (s32[4,8,1]{2,1,0:T(8,128)S(1)}, s32[4,8,1]{2,1,0:T(8,128)S(1)}, u32[]{:S(2)}, u32[]{:S(2)}) collective-permute-start(s32[4,8,1]{2,1,0:T(8,128)S(1)} %slice.106), channel_id=1, source_target_pairs={{0,1},{1,2},{2,3},{3,4},{4,5},{5,6},{6,7},{7,0},{8,9},{9,10},{10,1... | collective-permute-start | bytes 392 | tf_op jit(solution)/shard_map/ppermute | solution.py:342
  19.9 5.8 %collective-permute-start.4 = (s32[4,8,1]{2,1,0:T(8,128)S(1)}, s32[4,8,1]{2,1,0:T(8,128)S(1)}, u32[]{:S(2)}, u32[]{:S(2)}) collective-permute-start(s32[4,8,1]{2,1,0:T(8,128)S(1)} %bitcast.64), channel_id=1, source_target_pairs={{0,7},{1,0},{2,1},{3,2},{4,3},{5,4},{6,5},{7,6},{8,15},{9,8},{10,9... | collective-permute-start | bytes 392 | tf_op jit(solution)/shard_map/ppermute | solution.py:341
  25.9 17.7 %copy-start.5 = (s32[2,40960]{1,0:T(2,128)S(1)}, s32[2,40960]{1,0:T(2,128)}, u32[]{:S(2)}) copy-start(s32[2,40960]{1,0:T(2,128)} %param.11) | copy-start | bytes 983044
  25.9 17.7 %copy-start.7 = (s32[40960]{0:T(1024)S(1)}, s32[40960]{0:T(1024)}, u32[]{:S(2)}) copy-start(s32[40960]{0:T(1024)} %param.15) | copy-start | bytes 491524
  40.2 3.4 %copy-start.6 = (s32[40960]{0:T(1024)S(1)}, s32[40960]{0:T(1024)}, u32[]{:S(2)}) copy-start(s32[40960]{0:T(1024)} %param.14) | copy-start | bytes 491524
  40.2 7.1 %collective-permute-start.7 = (f32[3,1,8,128]{3,2,1,0:T(8,128)S(1)}, f32[3,1,8,128]{3,2,1,0:T(8,128)S(1)}, u32[]{:S(2)}, u32[]{:S(2)}) collective-permute-start(f32[3,1,8,128]{3,2,1,0:T(8,128)S(1)} %get-tuple-element.58), channel_id=1, source_target_pairs={{0,32},{32,64},{64,96},{96,0},{1,33},{33,65},{65,97},{97,1},{2,34}... | collective-permute-start | bytes 36872 | tf_op jit(solution)/shard_map/ppermute | solution.py:347
  40.3 7.0 %collective-permute-start.6 = (f32[3,1,8,128]{3,2,1,0:T(8,128)S(1)}, f32[3,1,8,128]{3,2,1,0:T(8,128)S(1)}, u32[]{:S(2)}, u32[]{:S(2)}) collective-permute-start(f32[3,1,8,128]{3,2,1,0:T(8,128)S(1)} %get-tuple-element.59), channel_id=1, source_target_pairs={{0,96},{32,0},{64,32},{96,64},{1,97},{33,1},{65,33},{97,65},{2,98}... | collective-permute-start | bytes 36872 | tf_op jit(solution)/shard_map/ppermute | solution.py:348
  47.4 7.0 %collective-permute-start.9 = (f32[3,4,1,128]{3,2,1,0:T(1,128)S(1)}, f32[3,4,1,128]{3,2,1,0:T(1,128)S(1)}, u32[]{:S(2)}, u32[]{:S(2)}) collective-permute-start(f32[3,4,1,128]{3,2,1,0:T(1,128)S(1)} %get-tuple-element.54), channel_id=1, source_target_pairs={{0,8},{8,16},{16,24},{24,0},{1,9},{9,17},{17,25},{25,1},{2,10},{10... | collective-permute-start | bytes 18440 | tf_op jit(solution)/shard_map/ppermute | solution.py:347
  47.5 7.0 %collective-permute-start.8 = (f32[3,4,1,128]{3,2,1,0:T(1,128)S(1)}, f32[3,4,1,128]{3,2,1,0:T(1,128)S(1)}, u32[]{:S(2)}, u32[]{:S(2)}) collective-permute-start(f32[3,4,1,128]{3,2,1,0:T(1,128)S(1)} %get-tuple-element.55), channel_id=1, source_target_pairs={{0,24},{8,0},{16,8},{24,16},{1,25},{9,1},{17,9},{25,17},{2,26},{10... | collective-permute-start | bytes 18440 | tf_op jit(solution)/shard_map/ppermute | solution.py:348
  54.7 0.7 copy-start.10
  63.1 7.4 %collective-permute-start.10 = (f32[14,128]{1,0:T(8,128)S(1)}, f32[14,128]{1,0:T(8,128)S(1)}, u32[]{:S(2)}, u32[]{:S(2)}) collective-permute-start(f32[14,128]{1,0:T(8,128)S(1)} %get-tuple-element.37), channel_id=1, source_target_pairs={{0,32},{32,64},{64,96},{96,0},{1,33},{33,65},{65,97},{97,1},{2,34}... | collective-permute-start | bytes 21512 | tf_op jit(solution)/shard_map/ppermute | solution.py:474
  63.8 7.8 %collective-permute-start.11 = (f32[14,128]{1,0:T(8,128)S(1)}, f32[14,128]{1,0:T(8,128)S(1)}, u32[]{:S(2)}, u32[]{:S(2)}) collective-permute-start(f32[14,128]{1,0:T(8,128)S(1)} %get-tuple-element.38), channel_id=1, source_target_pairs={{0,96},{32,0},{64,32},{96,64},{1,97},{33,1},{65,33},{97,65},{2,98}... | collective-permute-start | bytes 21512 | tf_op jit(solution)/shard_map/ppermute | solution.py:474
  66.4 5.3 %collective-permute-start.12 = (f32[14,128]{1,0:T(8,128)S(1)}, f32[14,128]{1,0:T(8,128)S(1)}, u32[]{:S(2)}, u32[]{:S(2)}) collective-permute-start(f32[14,128]{1,0:T(8,128)S(1)} %get-tuple-element.39), channel_id=1, source_target_pairs={{0,8},{8,16},{16,24},{24,0},{1,9},{9,17},{17,25},{25,1},{2,10},{10... | collective-permute-start | bytes 21512 | tf_op jit(solution)/shard_map/ppermute | solution.py:474
  66.4 5.3 %collective-permute-start.13 = (f32[14,128]{1,0:T(8,128)S(1)}, f32[14,128]{1,0:T(8,128)S(1)}, u32[]{:S(2)}, u32[]{:S(2)}) collective-permute-start(f32[14,128]{1,0:T(8,128)S(1)} %get-tuple-element.40), channel_id=1, source_target_pairs={{0,24},{8,0},{16,8},{24,16},{1,25},{9,1},{17,9},{25,17},{2,26},{10... | collective-permute-start | bytes 21512 | tf_op jit(solution)/shard_map/ppermute | solution.py:474
  69.6 3.7 %collective-permute-start.14 = (f32[15,128]{1,0:T(8,128)S(1)}, f32[15,128]{1,0:T(8,128)S(1)}, u32[]{:S(2)}, u32[]{:S(2)}) collective-permute-start(f32[15,128]{1,0:T(8,128)S(1)} %get-tuple-element.41), channel_id=1, source_target_pairs={{0,1},{1,2},{2,3},{3,4},{4,5},{5,6},{6,7},{7,0},{8,9},{9,10},{10,1... | collective-permute-start | bytes 23048 | tf_op jit(solution)/shard_map/ppermute | solution.py:474
  70.5 5.8 %collective-permute-start.15 = (f32[15,128]{1,0:T(8,128)S(1)}, f32[15,128]{1,0:T(8,128)S(1)}, u32[]{:S(2)}, u32[]{:S(2)}) collective-permute-start(f32[15,128]{1,0:T(8,128)S(1)} %get-tuple-element.42), channel_id=1, source_target_pairs={{0,7},{1,0},{2,1},{3,2},{4,3},{5,4},{6,5},{7,6},{8,15},{9,8},{10,9... | collective-permute-start | bytes 23048 | tf_op jit(solution)/shard_map/ppermute | solution.py:474
  71.6 4.7 %copy-start.1 = (f32[3,256]{1,0:T(4,128)S(1)}, f32[3,256]{1,0:T(4,128)}, u32[]{:S(2)}) copy-start(f32[3,256]{1,0:T(4,128)} %speed_ref.1) | copy-start | bytes 9220
  (3 other events, 2.1 us)

commit v6 on v5

--- a/solution.py
+++ b/solution.py
@@ -11,7 +11,7 @@
 COLLOIDS_PER_UNIT = 256
 CAP = 160
 LANES = 128
-UNROLL = 4
+UNROLL = 20
 ANGLE = 130.0 * math.pi / 180.0
 COS = math.cos(ANGLE)
 ALONG = (1.0 - math.cos(ANGLE)) / 3.0
@@ -132,72 +132,89 @@
     return [turned[i] + picked[i] for i in range(3)]
 
 
+def sweep(low, high, total, pick_block, add_block):
+    count = high - low
+    unroll = max(u for u in range(1, UNROLL + 1) if count % u == 0)
+
+    def step(i, carry):
+        lanes = places(LANES)
+        added, held = 0.0, None
+        for part in range(unroll + 1):
+            line = pl.multiple_of((low + i * unroll + part) * 8, 8)
+            new = pick_block(line, lanes) if part < unroll else None
+            if part:
+                added += add_block(line - 8, held, lanes)
+            held = new
+        total[...] += added
+        return carry
+
+    lax.fori_loop(0, count // unroll, step, 0)
+
+
+def rows_at(line):
+    return pl.ds(pl.multiple_of(line, 8), 8)
+
+
 def sum_kernel(low, high, ends, v_ref, cells_ref, *refs):
-    done_ref, out_ref = (None, refs[-1]) if low == 0 else (refs[0], refs[-1])
-    shape = (224, LANES)
-
-    def step(i, total):
-        lanes = places(LANES)
-        for part in range(UNROLL):
-            at = pl.ds(pl.multiple_of((i * UNROLL + part) * 8, 8), 8)
-            v = [v_ref[at, c, :] for c in range(3)]
-            total += scatter(v, cells_ref[at, 0, :], 32, True, lanes)
-        return total
-
-    total = jnp.zeros(shape, jnp.float32) if done_ref is None else done_ref[...]
-    total = lax.fori_loop(low, high, step, total)
-    out_ref[...] = mean_of(total) if ends else total
+    out_ref, total = refs[-2:]
+    total[...] = jnp.zeros_like(total) if low == 0 else refs[0][...]
+
+    def load(line, lanes):
+        return [v_ref[rows_at(line), c, :] for c in range(3)]
+
+    def add(line, v, lanes):
+        return scatter(v, cells_ref[rows_at(line), 0, :], 32, True, lanes)
+
+    sweep(low, high, total, load, add)
+    out_ref[...] = mean_of(total[...]) if ends else total[...]
 
 
 def turn_kernel(v_ref, cells_ref, mean_ref, axis_ref, out_ref, next_ref, total, table):
     total[...] = jnp.zeros_like(total)
     table[...] = cell_table(mean_ref[...], axis_ref[...])
 
-    def step(i, carry):
-        lanes = places(LANES)
-        added = 0.0
-        for part in range(UNROLL):
-            at = pl.ds(pl.multiple_of((i * UNROLL + part) * 8, 8), 8)
-            v = [v_ref[at, c, :] for c in range(3)]
-            new = collide(table[...], cells_ref[at, 0, :], v, lanes)
-            for c in range(3):
-                out_ref[c, at, :] = new[c]
-            added += scatter(new, cells_ref[at, 1, :], 32, True, lanes)
-        total[...] += added
-        return carry
-
-    lax.fori_loop(0, v_ref.shape[0] // (8 * UNROLL), step, 0)
+    def turn(line, lanes):
+        at = rows_at(line)
+        v = [v_ref[at, c, :] for c in range(3)]
+        new = collide(table[...], cells_ref[at, 0, :], v, lanes)
+        for c in range(3):
+            out_ref[c, at, :] = new[c]
+        return new
+
+    def add(line, v, lanes):
+        return scatter(v, cells_ref[rows_at(line), 1, :], 32, True, lanes)
+
+    sweep(0, v_ref.shape[0] // 8, total, turn, add)
     next_ref[...] = mean_of(total[...])
 
 
-def leave(low, high, v_ref, cells_ref, mean_ref, axis_ref, dir_ref, slot_ref, new_ref, first, moved, table):
+def leave(
+    low, high, v_ref, cells_ref, mean_ref, axis_ref, dir_ref, slot_ref, new_ref, first, moved, table
+):
     table[...] = cell_table(mean_ref[...], axis_ref[...])
 
-    def step(i, carry):
-        lanes = places(LANES)
-        added = 0.0
-        for part in range(UNROLL):
-            line = pl.multiple_of((i * UNROLL + part) * 8, 8)
-            at = pl.ds(line, 8)
-            v = [v_ref[c, at, :] for c in range(3)]
-            new = collide(table[...], cells_ref[at, 1, :], v, lanes)
-            to = pl.ds(pl.multiple_of(line - first, 8), 8)
-            for c in range(3):
-                new_ref[c, to, :] = new[c]
-            code = dir_ref[at, :]
-            key = jnp.where(code > 0, (code - 1) * 256 + slot_ref[at, :], 4096)
-            added += scatter(new, key, 16, False, lanes)
-        moved[...] += added
-        return carry
-
-    lax.fori_loop(low, high, step, 0)
+    def turn(line, lanes):
+        at = rows_at(line)
+        v = [v_ref[c, at, :] for c in range(3)]
+        new = collide(table[...], cells_ref[at, 1, :], v, lanes)
+        for c in range(3):
+            new_ref[c, rows_at(line - first), :] = new[c]
+        return new
+
+    def add(line, v, lanes):
+        at = rows_at(line)
+        code = dir_ref[at, :]
+        key = jnp.where(code > 0, (code - 1) * 256 + slot_ref[at, :], 4096)
+        return scatter(v, key, 16, False, lanes)
+
+    sweep(low, high, moved, turn, add)
 
 
 def part_kernel(low, high, *refs):
     inputs, refs = refs[:6], refs[6:]
     new_ref, moved_ref, table = refs[-3:]
     moved_ref[...] = jnp.zeros_like(moved_ref) if low == 0 else refs[0][...]
-    leave(low, high, *inputs, new_ref, low * 8 * UNROLL, moved_ref, table)
+    leave(low, high, *inputs, new_ref, low * 8, moved_ref, table)
 
 
 def places_of(colloid):
@@ -246,12 +263,15 @@
     high_part, low_part = split(held[...].reshape(3 * lines, LANES))
     wide = jnp.concatenate([high_part, low_part], axis=1).astype(jnp.bfloat16)
     lanes = places(LANES)
+    slots = [slice(8 * part, 8 * part + 8) for part in range(particle_ref.shape[0] // 8)]
+    terms = []
+    for at in slots:
+        weight = weight_ref[at, :]
+        found = pick(wide, particle_ref[at, :], lines, lanes)
+        terms.append([weight * x for x in found] + [weight])
     force = jnp.zeros((128, LANES), jnp.float32)
-    for part in range(particle_ref.shape[0] // 8):
-        at = slice(8 * part, 8 * part + 8)
-        weight = weight_ref[at, :]
-        terms = [weight * x for x in pick(wide, particle_ref[at, :], lines, lanes)] + [weight]
-        force = force + scatter(terms, places_of(colloid_ref[at, :]), 16, False, lanes)
+    for at, values in zip(slots, terms):
+        force = force + scatter(values, places_of(colloid_ref[at, :]), 16, False, lanes)
     force = force[0:64] + force[64:128]
     for f in range(4):
         own_ref[2 * f : 2 * f + 2, :] = force[16 * f : 16 * f + 2]
@@ -365,7 +385,7 @@
     particles = velocities.shape[1]
     cells_x, cells_y, cells_z = axis_index.shape[1:]
     lines = particles // LANES
-    steps = lines // (8 * UNROLL)
+    steps = lines // 8
     cuts = (0, steps * 3 // 10, steps * 6 // 10, steps)
     spans = tuple(zip(cuts[:-1], cuts[1:]))
     velocity = velocities.reshape(3, lines, LANES).transpose(1, 0, 2)
@@ -404,7 +424,7 @@
             functools.partial(sum_kernel, low, high, ends),
             "sums_%d" % dim,
             [(96 if ends else 224, LANES)],
-            [],
+            [total],
             pair_flops // 3,
             (velocity, cells) + summed,
         )
@@ -436,7 +456,7 @@
         part, moved = call(
             functools.partial(part_kernel, low, high),
             "part_%d" % dim,
-            [(3, (high - low) * 8 * UNROLL, LANES), (96, LANES)],
+            [(3, (high - low) * 8, LANES), (96, LANES)],
             [table],
             pair_flops // 2,
             shared + tied,

time: 78.1 us -> 67.7 us (0.87)
  Pallas kernels: 37.3 us -> 26.3 us
    pallas_call x9, Pallas kernels: 37.3 us -> 26.3 us  [call(): pl.pallas_call(kernel, name=name, out_shape=outs, in_specs=[smem] * scala...]
  transfers between devices with their start and end apart: 16 -> 16, of which waited for: 4 -> 4; matrix products, arithmetic and copies ran while one was open for 0% -> 0% of each run, Pallas kernels for 18% -> 15%
where the time goes in v6:
time: 67.7 us; the launch traced here: 67.3 us
  Pallas kernels  26.3 us (39%)
  starting transfers between devices  23.9 us (35%)
  waiting for transfers between devices  10.7 us (16%)
  local copies, waits for them, and re-layouts  5.33 us (8%)
  between operations  0.96 us (1%)
    pallas_call x9, Pallas kernels, call(): pl.pallas_call(kernel, name=name, out_shape=outs, in_specs=[smem] * scala...  26.3 us
    ppermute x6, starting transfers between devices, body(): came.append(lax.ppermute(block, axis, ring(axis, by)))  8.51 us
    ppermute x3, starting transfers between devices, axis_round(): upper = lax.ppermute(sent[0], axis, ring(axis, -1))  6.78 us
    ppermute x2, starting transfers between devices, mean_round(): upper = lax.ppermute(first(mean, dim + 1), axis, ring(axis, -1))  6.46 us
    unnamed x22, local copies, waits for them, and re-layouts  4.18 us
    ppermute x6, waiting for transfers between devices, body(): came.append(lax.ppermute(block, axis, ring(axis, by)))  4.14 us
    ppermute x3, waiting for transfers between devices, axis_round(): upper = lax.ppermute(sent[0], axis, ring(axis, -1))  3.42 us
    ppermute x3, waiting for transfers between devices, axis_round(): lower = lax.ppermute(sent[1], axis, ring(axis, 1))  3.14 us
  transfers between devices with their start and end apart: 16, of which 4 were waited for; matrix products, arithmetic and copies ran while one was open for 0% of the time, Pallas kernels for 15%

profile of v6, /device:TPU:6, one launch (start us, length us, event | category | flops | bytes accessed | tf_op | source)
XLA Modules:
  0.0 67.3 jit_solution(13995538515990193916)
XLA Ops:
  1.3 0.8 %copy-done = s32[2,4,8,128]{3,2,1,0:T(8,128)S(1)} copy-done((s32[2,4,8,128]{3,2,1,0:T(8,128)S(1)}, s32[2,4,8,128]{3,2,1,0:T(8,128)}, u32[]{:S(2)}) %copy-start) | copy-done | bytes 32792
  2.7 3.4 %collective-permute-start = (s32[1,8,128]{2,1,0:T(8,128)S(1)}, s32[1,8,128]{2,1,0:T(8,128)S(1)}, u32[]{:S(2)}, u32[]{:S(2)}) collective-permute-start(s32[1,8,128]{2,1,0:T(8,128)S(1)} %bitcast.61), channel_id=1, source_target_pairs={{0,96},{32,0},{64,32},{96,64},{1,97},{33,1},{65,33},{97,65},{2,98}... | collective-permute-start | bytes 12296 | tf_op jit(solution)/shard_map/ppermute | solution.py:361
  6.1 1.1 %copy-done.3 = f32[3,40960]{1,0:T(4,128)S(1)} copy-done((f32[3,40960]{1,0:T(4,128)S(1)}, f32[3,40960]{1,0:T(4,128)}, u32[]{:S(2)}) %copy-start.3) | copy-done | bytes 491544
  7.2 1.0 %copy-done.4 = s32[2,40960]{1,0:T(2,128)S(1)} copy-done((s32[2,40960]{1,0:T(2,128)S(1)}, s32[2,40960]{1,0:T(2,128)}, u32[]{:S(2)}) %copy-start.4) | copy-done | bytes 327704
  8.2 1.6 %sums_0.1.refs_0_ = f32[224,128]{1,0:T(8,128)S(1)} custom-call(f32[320,3,128]{2,1,0:T(4,128)S(1)} %bitcast.41, s32[320,2,128]{2,1,0:T(2,128)S(1)} %bitcast.45), custom_call_target="tpu_custom_call" | custom-call | flops 782936768 | bytes 2097152 | tf_op jit(solution)/shard_map/sums_0/pallas_call | solution.py:327
  9.8 3.1 %collective-permute-start.2 = (s32[4,1,128]{2,1,0:T(1,128)S(1)}, s32[4,1,128]{2,1,0:T(1,128)S(1)}, u32[]{:S(2)}, u32[]{:S(2)}) collective-permute-start(s32[4,1,128]{2,1,0:T(1,128)S(1)} %slice.100), channel_id=1, source_target_pairs={{0,24},{8,0},{16,8},{24,16},{1,25},{9,1},{17,9},{25,17},{2,26},{10... | collective-permute-start | bytes 6152 | tf_op jit(solution)/shard_map/ppermute | solution.py:361
  12.9 1.6 %sums_1.1.refs_0_ = f32[224,128]{1,0:T(8,128)S(1)} custom-call(f32[320,3,128]{2,1,0:T(4,128)S(1)} %bitcast.42, s32[320,2,128]{2,1,0:T(2,128)S(1)} %bitcast.46, f32[224,128]{1,0:T(8,128)S(1)} %sums_0.1.refs_0_, s32[1,8,128]{2,1,0:T(8,128)S(1)} %collective-permute-done.refs_1_, s32[1,8,128]{2,1,0:T(8,128)S(1)} %collective-permute-done.1.refs_2_), custom_call_target="tpu_custom_call" | custom-call | flops 782936768 | bytes 2097152 | tf_op jit(solution)/shard_map/sums_1/pallas_call | solution.py:327
  14.6 3.1 %collective-permute-done.3.refs_2_ = s32[4,1,128]{2,1,0:T(1,128)S(1)} collective-permute-done((s32[4,1,128]{2,1,0:T(1,128)S(1)}, s32[4,1,128]{2,1,0:T(1,128)S(1)}, u32[]{:S(2)}, u32[]{:S(2)}) %collective-permute-start.3) | collective-permute-done | bytes 2080 | tf_op jit(solution)/shard_map/ppermute | solution.py:362
  17.9 1.7 %collective-permute-start.5 = (s32[4,8,1]{2,1,0:T(8,128)S(1)}, s32[4,8,1]{2,1,0:T(8,128)S(1)}, u32[]{:S(2)}, u32[]{:S(2)}) collective-permute-start(s32[4,8,1]{2,1,0:T(8,128)S(1)} %slice.106), channel_id=1, source_target_pairs={{0,1},{1,2},{2,3},{3,4},{4,5},{5,6},{6,7},{7,0},{8,9},{9,10},{10,1... | collective-permute-start | bytes 392 | tf_op jit(solution)/shard_map/ppermute | solution.py:362
  19.9 2.1 %sums_2.1.mean_ref = f32[96,128]{1,0:T(8,128)S(1)} custom-call(f32[320,3,128]{2,1,0:T(4,128)S(1)} %bitcast.43, s32[320,2,128]{2,1,0:T(2,128)S(1)} %bitcast.47, f32[224,128]{1,0:T(8,128)S(1)} %sums_1.1.refs_0_, s32[4,1,128]{2,1,0:T(1,128)S(1)} %collective-permute-done.2.refs_1_, s32[4,1,128]{2,1,0:T(1,128)S(1)} %collective-permute-done.3.refs_2_), custom_call_target="tpu_custom_call" | custom-call | flops 782936768 | bytes 2097152 | tf_op jit(solution)/shard_map/sums_2/pallas_call | solution.py:327
  22.0 3.4 %collective-permute-done.4 = s32[4,8,1]{2,1,0:T(8,128)S(1)} collective-permute-done((s32[4,8,1]{2,1,0:T(8,128)S(1)}, s32[4,8,1]{2,1,0:T(8,128)S(1)}, u32[]{:S(2)}, u32[]{:S(2)}) %collective-permute-start.4) | collective-permute-done | bytes 160 | tf_op jit(solution)/shard_map/ppermute | solution.py:361
  25.5 9.5 %turn.1 = (f32[3,320,128]{2,1,0:T(8,128)S(1)}, f32[96,128]{1,0:T(8,128)S(1)}) custom-call(f32[320,3,128]{2,1,0:T(4,128)S(1)} %bitcast.44, s32[320,2,128]{2,1,0:T(2,128)S(1)} %bitcast.48, f32[96,128]{1,0:T(8,128)S(1)} %sums_2.1.mean_ref, s32[32,128]{1,0:T(8,128)S(1)} %get-tuple-element.53.axis_ref), custom_call_target="tpu_custom_call" | custom-call | flops 4697620480 | bytes 2097152 | tf_op jit(solution)/shard_map/turn/pallas_call | solution.py:327
  35.3 3.2 %collective-permute-start.6 = (f32[3,1,8,128]{3,2,1,0:T(8,128)S(1)}, f32[3,1,8,128]{3,2,1,0:T(8,128)S(1)}, u32[]{:S(2)}, u32[]{:S(2)}) collective-permute-start(f32[3,1,8,128]{3,2,1,0:T(8,128)S(1)} %get-tuple-element.59), channel_id=1, source_target_pairs={{0,96},{32,0},{64,32},{96,64},{1,97},{33,1},{65,33},{97,65},{2,98}... | collective-permute-start | bytes 36872 | tf_op jit(solution)/shard_map/ppermute | solution.py:368
  38.6 2.3 %part_0.1 = (f32[3,96,128]{2,1,0:T(8,128)S(1)}, f32[96,128]{1,0:T(8,128)S(1)}) custom-call(f32[3,320,128]{2,1,0:T(8,128)S(1)} %get-tuple-element.31.refs_0_, s32[320,2,128]{2,1,0:T(2,128)S(1)} %bitcast.49, f32[96,128]{1,0:T(8,128)S(1)} %get-tuple-element.30.refs_2_, s32[32,128]{1,0:T(8,128)S(1)} %get-tuple-element.52.refs_3_, s32[320,128]{1,0:T(8,128)S(1)} %bitcast.52, ...), custom_call_target="tpu_custom_call" | custom-call | flops 1174405120 | bytes 2097152 | tf_op jit(solution)/shard_map/part_0/pallas_call | solution.py:327
  41.0 3.2 %collective-permute-start.8 = (f32[3,4,1,128]{3,2,1,0:T(1,128)S(1)}, f32[3,4,1,128]{3,2,1,0:T(1,128)S(1)}, u32[]{:S(2)}, u32[]{:S(2)}) collective-permute-start(f32[3,4,1,128]{3,2,1,0:T(1,128)S(1)} %get-tuple-element.55), channel_id=1, source_target_pairs={{0,24},{8,0},{16,8},{24,16},{1,25},{9,1},{17,9},{25,17},{2,26},{10... | collective-permute-start | bytes 18440 | tf_op jit(solution)/shard_map/ppermute | solution.py:368
  44.2 2.3 %part_1.1 = (f32[3,96,128]{2,1,0:T(8,128)S(1)}, f32[96,128]{1,0:T(8,128)S(1)}) custom-call(f32[3,320,128]{2,1,0:T(8,128)S(1)} %get-tuple-element.31.refs_0_, s32[320,2,128]{2,1,0:T(2,128)S(1)} %bitcast.50, f32[96,128]{1,0:T(8,128)S(1)} %get-tuple-element.30.refs_2_, s32[32,128]{1,0:T(8,128)S(1)} %get-tuple-element.52.refs_3_, s32[320,128]{1,0:T(8,128)S(1)} %bitcast.53, ...), custom_call_target="tpu_custom_call" | custom-call | flops 1174405120 | bytes 2097152 | tf_op jit(solution)/shard_map/part_1/pallas_call | solution.py:327
  47.6 5.5 %last.1 = (f32[3,41920]{1,0:T(4,128)}, f32[8,128]{1,0:T(8,128)S(1)}, f32[14,128]{1,0:T(8,128)S(1)}, f32[14,128]{1,0:T(8,128)S(1)}, f32[14,128]{1,0:T(8,128)S(1)}...) custom-call(f32[3,320,128]{2,1,0:T(8,128)S(1)} %get-tuple-element.31.refs_0_, ...), custom_call_target="tpu_custom_call" | custom-call | flops 2348810240 | bytes 2097152 | tf_op jit(solution)/shard_map/last/pallas_call | solution.py:327
  53.2 2.2 %collective-permute-start.10 = (f32[14,128]{1,0:T(8,128)S(1)}, f32[14,128]{1,0:T(8,128)S(1)}, u32[]{:S(2)}, u32[]{:S(2)}) collective-permute-start(f32[14,128]{1,0:T(8,128)S(1)} %get-tuple-element.37), channel_id=1, source_target_pairs={{0,32},{32,64},{64,96},{96,0},{1,33},{33,65},{65,97},{97,1},{2,34}... | collective-permute-start | bytes 21512 | tf_op jit(solution)/shard_map/ppermute | solution.py:494
  55.3 1.1 %collective-permute-start.11 = (f32[14,128]{1,0:T(8,128)S(1)}, f32[14,128]{1,0:T(8,128)S(1)}, u32[]{:S(2)}, u32[]{:S(2)}) collective-permute-start(f32[14,128]{1,0:T(8,128)S(1)} %get-tuple-element.38), channel_id=1, source_target_pairs={{0,96},{32,0},{64,32},{96,64},{1,97},{33,1},{65,33},{97,65},{2,98}... | collective-permute-start | bytes 21512 | tf_op jit(solution)/shard_map/ppermute | solution.py:494
  56.4 3.2 %collective-permute-start.13 = (f32[14,128]{1,0:T(8,128)S(1)}, f32[14,128]{1,0:T(8,128)S(1)}, u32[]{:S(2)}, u32[]{:S(2)}) collective-permute-start(f32[14,128]{1,0:T(8,128)S(1)} %get-tuple-element.40), channel_id=1, source_target_pairs={{0,24},{8,0},{16,8},{24,16},{1,25},{9,1},{17,9},{25,17},{2,26},{10... | collective-permute-start | bytes 21512 | tf_op jit(solution)/shard_map/ppermute | solution.py:494
  60.1 1.6 %collective-permute-start.15 = (f32[15,128]{1,0:T(8,128)S(1)}, f32[15,128]{1,0:T(8,128)S(1)}, u32[]{:S(2)}, u32[]{:S(2)}) collective-permute-start(f32[15,128]{1,0:T(8,128)S(1)} %get-tuple-element.42), channel_id=1, source_target_pairs={{0,7},{1,0},{2,1},{3,2},{4,3},{5,4},{6,5},{7,6},{8,15},{9,8},{10,9... | collective-permute-start | bytes 23048 | tf_op jit(solution)/shard_map/ppermute | solution.py:494
  61.7 1.6 %collective-permute-done.14.refs_4_ = f32[15,128]{1,0:T(8,128)S(1)} collective-permute-done((f32[15,128]{1,0:T(8,128)S(1)}, f32[15,128]{1,0:T(8,128)S(1)}, u32[]{:S(2)}, u32[]{:S(2)}) %collective-permute-start.14) | collective-permute-done | bytes 7712 | tf_op jit(solution)/shard_map/ppermute | solution.py:494
  63.3 2.6 %collective-permute-done.15.refs_5_ = f32[15,128]{1,0:T(8,128)S(1)} collective-permute-done((f32[15,128]{1,0:T(8,128)S(1)}, f32[15,128]{1,0:T(8,128)S(1)}, u32[]{:S(2)}, u32[]{:S(2)}) %collective-permute-start.15) | collective-permute-done | bytes 7712 | tf_op jit(solution)/shard_map/ppermute | solution.py:494
  65.9 0.9 %finish.1 = (f32[96,128]{1,0:T(8,128)}, f32[3,960]{1,0:T(4,128)S(1)}, f32[3,256]{1,0:T(4,128)}) custom-call(s32[8,128]{1,0:T(8,128)S(1)} %get-tuple-element.25.sign_ref, f32[96,128]{1,0:T(8,128)S(1)} %bitcast_select_fusion.mean_ref, f32[8,128]{1,0:T(8,128)S(1)} %get-tuple-element.36.own_ref, f32[3,256]{1,0:T(4,128)S(1)} %copy-done.1, ...), custom_call_target="tpu_custom_call" | custom-call | flops 1048576 | bytes 2097152 | tf_op jit(solution)/shard_map/finish/pallas_call | solution.py:327
  (63 shorter events, 4.4 us)
Async XLA Ops:
  1.3 0.8 %copy-start = (s32[2,4,8,128]{3,2,1,0:T(8,128)S(1)}, s32[2,4,8,128]{3,2,1,0:T(8,128)}, u32[]{:S(2)}) copy-start(s32[2,4,8,128]{3,2,1,0:T(8,128)} %param.13) | copy-start | bytes 98308
  2.6 7.1 %collective-permute-start.1 = (s32[1,8,128]{2,1,0:T(8,128)S(1)}, s32[1,8,128]{2,1,0:T(8,128)S(1)}, u32[]{:S(2)}, u32[]{:S(2)}) collective-permute-start(s32[1,8,128]{2,1,0:T(8,128)S(1)} %bitcast.62), channel_id=1, source_target_pairs={{0,32},{32,64},{64,96},{96,0},{1,33},{33,65},{65,97},{97,1},{2,34}... | collective-permute-start | bytes 12296 | tf_op jit(solution)/shard_map/ppermute | solution.py:362
  2.7 7.1 %collective-permute-start = (s32[1,8,128]{2,1,0:T(8,128)S(1)}, s32[1,8,128]{2,1,0:T(8,128)S(1)}, u32[]{:S(2)}, u32[]{:S(2)}) collective-permute-start(s32[1,8,128]{2,1,0:T(8,128)S(1)} %bitcast.61), channel_id=1, source_target_pairs={{0,96},{32,0},{64,32},{96,64},{1,97},{33,1},{65,33},{97,65},{2,98}... | collective-permute-start | bytes 12296 | tf_op jit(solution)/shard_map/ppermute | solution.py:361
  6.1 1.1 %copy-start.3 = (f32[3,40960]{1,0:T(4,128)S(1)}, f32[3,40960]{1,0:T(4,128)}, u32[]{:S(2)}) copy-start(f32[3,40960]{1,0:T(4,128)} %param.10) | copy-start | bytes 1474564
  7.2 1.0 %copy-start.4 = (s32[2,40960]{1,0:T(2,128)S(1)}, s32[2,40960]{1,0:T(2,128)}, u32[]{:S(2)}) copy-start(s32[2,40960]{1,0:T(2,128)} %param.11) | copy-start | bytes 983044
  9.8 4.7 %collective-permute-start.2 = (s32[4,1,128]{2,1,0:T(1,128)S(1)}, s32[4,1,128]{2,1,0:T(1,128)S(1)}, u32[]{:S(2)}, u32[]{:S(2)}) collective-permute-start(s32[4,1,128]{2,1,0:T(1,128)S(1)} %slice.100), channel_id=1, source_target_pairs={{0,24},{8,0},{16,8},{24,16},{1,25},{9,1},{17,9},{25,17},{2,26},{10... | collective-permute-start | bytes 6152 | tf_op jit(solution)/shard_map/ppermute | solution.py:361
  12.9 4.8 %collective-permute-start.3 = (s32[4,1,128]{2,1,0:T(1,128)S(1)}, s32[4,1,128]{2,1,0:T(1,128)S(1)}, u32[]{:S(2)}, u32[]{:S(2)}) collective-permute-start(s32[4,1,128]{2,1,0:T(1,128)S(1)} %slice.101), channel_id=1, source_target_pairs={{0,8},{8,16},{16,24},{24,0},{1,9},{9,17},{17,25},{25,1},{2,10},{10... | collective-permute-start | bytes 6152 | tf_op jit(solution)/shard_map/ppermute | solution.py:362
  17.9 4.1 %collective-permute-start.5 = (s32[4,8,1]{2,1,0:T(8,128)S(1)}, s32[4,8,1]{2,1,0:T(8,128)S(1)}, u32[]{:S(2)}, u32[]{:S(2)}) collective-permute-start(s32[4,8,1]{2,1,0:T(8,128)S(1)} %slice.106), channel_id=1, source_target_pairs={{0,1},{1,2},{2,3},{3,4},{4,5},{5,6},{6,7},{7,0},{8,9},{9,10},{10,1... | collective-permute-start | bytes 392 | tf_op jit(solution)/shard_map/ppermute | solution.py:362
  19.6 5.8 %collective-permute-start.4 = (s32[4,8,1]{2,1,0:T(8,128)S(1)}, s32[4,8,1]{2,1,0:T(8,128)S(1)}, u32[]{:S(2)}, u32[]{:S(2)}) collective-permute-start(s32[4,8,1]{2,1,0:T(8,128)S(1)} %bitcast.64), channel_id=1, source_target_pairs={{0,7},{1,0},{2,1},{3,2},{4,3},{5,4},{6,5},{7,6},{8,15},{9,8},{10,9... | collective-permute-start | bytes 392 | tf_op jit(solution)/shard_map/ppermute | solution.py:361
  25.5 13.0 %copy-start.5 = (s32[2,40960]{1,0:T(2,128)S(1)}, s32[2,40960]{1,0:T(2,128)}, u32[]{:S(2)}) copy-start(s32[2,40960]{1,0:T(2,128)} %param.11) | copy-start | bytes 983044
  25.5 13.0 %copy-start.7 = (s32[40960]{0:T(1024)S(1)}, s32[40960]{0:T(1024)}, u32[]{:S(2)}) copy-start(s32[40960]{0:T(1024)} %param.15) | copy-start | bytes 491524
  35.0 3.5 %copy-start.6 = (s32[40960]{0:T(1024)S(1)}, s32[40960]{0:T(1024)}, u32[]{:S(2)}) copy-start(s32[40960]{0:T(1024)} %param.14) | copy-start | bytes 491524
  35.1 5.8 %collective-permute-start.7 = (f32[3,1,8,128]{3,2,1,0:T(8,128)S(1)}, f32[3,1,8,128]{3,2,1,0:T(8,128)S(1)}, u32[]{:S(2)}, u32[]{:S(2)}) collective-permute-start(f32[3,1,8,128]{3,2,1,0:T(8,128)S(1)} %get-tuple-element.58), channel_id=1, source_target_pairs={{0,32},{32,64},{64,96},{96,0},{1,33},{33,65},{65,97},{97,1},{2,34}... | collective-permute-start | bytes 36872 | tf_op jit(solution)/shard_map/ppermute | solution.py:367
  35.3 5.5 %collective-permute-start.6 = (f32[3,1,8,128]{3,2,1,0:T(8,128)S(1)}, f32[3,1,8,128]{3,2,1,0:T(8,128)S(1)}, u32[]{:S(2)}, u32[]{:S(2)}) collective-permute-start(f32[3,1,8,128]{3,2,1,0:T(8,128)S(1)} %get-tuple-element.59), channel_id=1, source_target_pairs={{0,96},{32,0},{64,32},{96,64},{1,97},{33,1},{65,33},{97,65},{2,98}... | collective-permute-start | bytes 36872 | tf_op jit(solution)/shard_map/ppermute | solution.py:368
  40.9 5.6 %collective-permute-start.9 = (f32[3,4,1,128]{3,2,1,0:T(1,128)S(1)}, f32[3,4,1,128]{3,2,1,0:T(1,128)S(1)}, u32[]{:S(2)}, u32[]{:S(2)}) collective-permute-start(f32[3,4,1,128]{3,2,1,0:T(1,128)S(1)} %get-tuple-element.54), channel_id=1, source_target_pairs={{0,8},{8,16},{16,24},{24,0},{1,9},{9,17},{17,25},{25,1},{2,10},{10... | collective-permute-start | bytes 18440 | tf_op jit(solution)/shard_map/ppermute | solution.py:367
  41.0 5.5 %collective-permute-start.8 = (f32[3,4,1,128]{3,2,1,0:T(1,128)S(1)}, f32[3,4,1,128]{3,2,1,0:T(1,128)S(1)}, u32[]{:S(2)}, u32[]{:S(2)}) collective-permute-start(f32[3,4,1,128]{3,2,1,0:T(1,128)S(1)} %get-tuple-element.55), channel_id=1, source_target_pairs={{0,24},{8,0},{16,8},{24,16},{1,25},{9,1},{17,9},{25,17},{2,26},{10... | collective-permute-start | bytes 18440 | tf_op jit(solution)/shard_map/ppermute | solution.py:368
  46.7 0.7 %copy-start.10 = (f32[2048]{0:T(1024)S(1)}, f32[2048]{0:T(1024)}, u32[]{:S(2)}) copy-start(f32[2048]{0:T(1024)} %param.18) | copy-start | bytes 24580
  53.2 6.9 %collective-permute-start.10 = (f32[14,128]{1,0:T(8,128)S(1)}, f32[14,128]{1,0:T(8,128)S(1)}, u32[]{:S(2)}, u32[]{:S(2)}) collective-permute-start(f32[14,128]{1,0:T(8,128)S(1)} %get-tuple-element.37), channel_id=1, source_target_pairs={{0,32},{32,64},{64,96},{96,0},{1,33},{33,65},{65,97},{97,1},{2,34}... | collective-permute-start | bytes 21512 | tf_op jit(solution)/shard_map/ppermute | solution.py:494
  55.3 6.4 %collective-permute-start.11 = (f32[14,128]{1,0:T(8,128)S(1)}, f32[14,128]{1,0:T(8,128)S(1)}, u32[]{:S(2)}, u32[]{:S(2)}) collective-permute-start(f32[14,128]{1,0:T(8,128)S(1)} %get-tuple-element.38), channel_id=1, source_target_pairs={{0,96},{32,0},{64,32},{96,64},{1,97},{33,1},{65,33},{97,65},{2,98}... | collective-permute-start | bytes 21512 | tf_op jit(solution)/shard_map/ppermute | solution.py:494
  56.4 5.3 %collective-permute-start.12 = (f32[14,128]{1,0:T(8,128)S(1)}, f32[14,128]{1,0:T(8,128)S(1)}, u32[]{:S(2)}, u32[]{:S(2)}) collective-permute-start(f32[14,128]{1,0:T(8,128)S(1)} %get-tuple-element.39), channel_id=1, source_target_pairs={{0,8},{8,16},{16,24},{24,0},{1,9},{9,17},{17,25},{25,1},{2,10},{10... | collective-permute-start | bytes 21512 | tf_op jit(solution)/shard_map/ppermute | solution.py:494
  56.4 5.3 %collective-permute-start.13 = (f32[14,128]{1,0:T(8,128)S(1)}, f32[14,128]{1,0:T(8,128)S(1)}, u32[]{:S(2)}, u32[]{:S(2)}) collective-permute-start(f32[14,128]{1,0:T(8,128)S(1)} %get-tuple-element.40), channel_id=1, source_target_pairs={{0,24},{8,0},{16,8},{24,16},{1,25},{9,1},{17,9},{25,17},{2,26},{10... | collective-permute-start | bytes 21512 | tf_op jit(solution)/shard_map/ppermute | solution.py:494
  59.7 3.7 %collective-permute-start.14 = (f32[15,128]{1,0:T(8,128)S(1)}, f32[15,128]{1,0:T(8,128)S(1)}, u32[]{:S(2)}, u32[]{:S(2)}) collective-permute-start(f32[15,128]{1,0:T(8,128)S(1)} %get-tuple-element.41), channel_id=1, source_target_pairs={{0,1},{1,2},{2,3},{3,4},{4,5},{5,6},{6,7},{7,0},{8,9},{9,10},{10,1... | collective-permute-start | bytes 23048 | tf_op jit(solution)/shard_map/ppermute | solution.py:494
  60.1 5.8 %collective-permute-start.15 = (f32[15,128]{1,0:T(8,128)S(1)}, f32[15,128]{1,0:T(8,128)S(1)}, u32[]{:S(2)}, u32[]{:S(2)}) collective-permute-start(f32[15,128]{1,0:T(8,128)S(1)} %get-tuple-element.42), channel_id=1, source_target_pairs={{0,7},{1,0},{2,1},{3,2},{4,3},{5,4},{6,5},{7,6},{8,15},{9,8},{10,9... | collective-permute-start | bytes 23048 | tf_op jit(solution)/shard_map/ppermute | solution.py:494
  61.7 4.2 %copy-start.1 = (f32[3,256]{1,0:T(4,128)S(1)}, f32[3,256]{1,0:T(4,128)}, u32[]{:S(2)}) copy-start(f32[3,256]{1,0:T(4,128)} %speed_ref.1) | copy-start | bytes 9220
  (3 other events, 2.1 us)

commit v7 on v6

--- a/solution.py
+++ b/solution.py
@@ -231,9 +231,8 @@
 
 def last_kernel(low, high, *refs):
     inputs, refs = refs[:6], refs[6:]
-    before_ref, parts, refs = refs[0], refs[1:3], refs[3:]
+    before_ref, parts, refs = refs[0], refs[1:2], refs[2:]
     particle_ref, colloid_ref, weight_ref = refs[:3]
-    faces = refs[3:5]
     kept_ref, own_ref, *outs = refs[-11:-3]
     moved, table, held = refs[-3:]
     dir_ref = inputs[4]
@@ -278,19 +277,17 @@
         for number, out in enumerate(outs):
             at = 16 * f + 2 * number + 2
             out[6 + 2 * f : 8 + 2 * f, :] = force[at : at + 2]
-    for out, face in zip(outs[4:], faces):
-        out[14:15, :] = face[...]
-
-
-def prepare_kernel(shift_ref, axis_ref, sign_ref, first_ref, last_ref, rise_ref, fall_ref):
-    rows = lax.broadcasted_iota(jnp.int32, (8, LANES), 0)
-    sign = jnp.zeros((8, LANES), jnp.int32)
-    for dim in range(3):
-        sign = jnp.where(rows == dim, shift_ref[0, dim], sign)
-    sign_ref[...] = sign
-    up = jnp.full(rise_ref.shape, shift_ref[0, 0], jnp.int32) > 0
-    rise_ref[...] = jnp.where(up, axis_ref[0], axis_ref[1])
-    fall_ref[...] = jnp.where(up, axis_ref[1], axis_ref[0])
+    for out in outs:
+        out[14:16, :] = jnp.zeros((2, LANES), jnp.float32)
+
+
+def prepare_kernel(all_ref, sign_ref, first_ref, last_ref, rise_ref, fall_ref):
+    rows = rise_ref.shape[0]
+    sign_ref[...] = all_ref[2 * rows :, :]
+    up = jnp.broadcast_to(all_ref[2 * rows : 2 * rows + 1, :], rise_ref.shape) > 0
+    axes = [all_ref[0:rows, :], all_ref[rows : 2 * rows, :]]
+    rise_ref[...] = jnp.where(up, axes[0], axes[1])
+    fall_ref[...] = jnp.where(up, axes[1], axes[0])
     first_ref[...] = rise_ref[0 : first_ref.shape[0], :]
     last_ref[...] = fall_ref[fall_ref.shape[0] - last_ref.shape[0] :, :]
 
@@ -299,7 +296,7 @@
     came, (mean_out, moved_out, force_out) = refs[:6], refs[6:]
     mean = mean_ref[...]
     rows = mean.shape[0]
-    sides = [jnp.broadcast_to(x[14:15, :], (8, LANES)).T[:rows, 0:1] for x in came[4:]]
+    sides = [jnp.broadcast_to(x[16:17, :], (8, LANES)).T[:rows, 0:1] for x in came[4:]]
     lane = lax.broadcasted_iota(jnp.int32, mean.shape, 1)
     ahead_mean = jnp.where(lane == LANES - 1, sides[1], pltpu.roll(mean, LANES - 1, 1))
     behind_mean = jnp.where(lane == 0, sides[0], pltpu.roll(mean, 1, 1))
@@ -320,15 +317,14 @@
             force_out[c : c + 1, at] = rest / jnp.maximum(weight, 1.0)
 
 
-def call(kernel, name, outs, scratch, flops, args, scalars=0):
+def call(kernel, name, outs, scratch, flops, args):
     vmem = pl.BlockSpec(memory_space=pltpu.VMEM)
-    smem = pl.BlockSpec(memory_space=pltpu.SMEM)
     outs = [out if hasattr(out, "dtype") else jax.ShapeDtypeStruct(out, jnp.float32) for out in outs]
     return pl.pallas_call(
         kernel,
         name=name,
         out_shape=outs,
-        in_specs=[smem] * scalars + [vmem] * (len(args) - scalars),
+        in_specs=[vmem] * len(args),
         out_specs=[vmem] * len(outs),
         scratch_shapes=scratch,
         compiler_params=pltpu.CompilerParams(vmem_limit_bytes=VMEM_LIMIT),
@@ -397,14 +393,14 @@
     plane, cells_all = cells_y, cells_x * cells_y
     whole = jax.ShapeDtypeStruct((cells_all, cells_z), jnp.int32)
     rim = jax.ShapeDtypeStruct((plane, cells_z), jnp.int32)
+    shifts = jnp.broadcast_to(jnp.pad(grid_shift[0], (0, 5))[:, None], (8, LANES))
     sign, first_rim, last_rim, rise, fall = call(
         prepare_kernel,
         "prepare",
         [jax.ShapeDtypeStruct((8, LANES), jnp.int32), rim, rim, whole, whole],
         [],
         1 << 16,
-        (grid_shift, axis_index.reshape(2, cells_all, cells_z)),
-        scalars=1,
+        (jnp.concatenate([axis_index.reshape(2 * cells_all, cells_z), shifts], axis=0),),
     )
     up = [sign[dim] > 0 for dim in range(3)]
     rise = rise.reshape(cells_x, cells_y, cells_z)
@@ -450,9 +446,9 @@
     mean = mean1.reshape(3, cells_x, cells_y, cells_z)
     tied = ()
     parts = []
-    for dim, axis in enumerate(("gx", "gy")):
+    for dim, axis in enumerate(("gx",)):
         mean, rims = mean_round(mean, up[dim], dim, axis)
-        low, high = spans[dim]
+        low, high = 0, steps // 2
         part, moved = call(
             functools.partial(part_kernel, low, high),
             "part_%d" % dim,
@@ -463,15 +459,11 @@
         )
         parts.append(part)
         tied = (moved,) + rims
-    faces = [
-        jnp.pad(x.reshape(1, -1), ((0, 0), (0, LANES - 3 * cells_all)))
-        for x in (last(mean, 3), first(mean, 3))
-    ]
-    low, high = spans[2]
+    low, high = steps // 2, steps
     kept, own, *blocks = call(
         functools.partial(last_kernel, low, high),
         "last",
-        [(3, particles + 6 * CAP), (8, LANES)] + [(14, LANES)] * 4 + [(15, LANES)] * 2,
+        [(3, particles + 6 * CAP), (8, LANES)] + [(16, LANES)] * 6,
         [
             pltpu.VMEM((96, LANES), jnp.float32),
             table,
@@ -484,14 +476,25 @@
             contact_particle.reshape(-1, LANES),
             contact_colloid.reshape(-1, LANES),
             contact_weight.reshape(-1, LANES),
-            *faces,
         )
         + rims,
     )
     came = []
-    for number, block in enumerate(blocks):
-        axis, by = ("gx", "gy", "gz")[number // 2], 1 - 2 * (number % 2)
-        came.append(lax.ppermute(block, axis, ring(axis, by)))
+    for dim, axis in enumerate(("gx", "gy", "gz")):
+        rims = []
+        for side, cut in enumerate((last, first)):
+            sent = blocks[2 * dim + side]
+            if dim:
+                rim = cut(mean, dim + 1)
+                shape = rim.shape
+                if dim == 2:
+                    rim = jnp.pad(rim.reshape(1, -1), ((0, 0), (0, LANES - 3 * cells_all)))
+                sent = jnp.concatenate([sent, rim.reshape(-1, LANES)], axis=0)
+            came.append(lax.ppermute(sent, axis, ring(axis, 1 - 2 * side)))
+            rims.append(came[-1][16:])
+        if dim == 1:
+            lower, upper = [x.reshape(shape) for x in rims]
+            mean = jnp.where(up[dim], ahead(mean, upper, dim + 1), behind(mean, lower, dim + 1))
     mean, arrivals, colloid_force = call(
         finish_kernel,
         "finish",

time: 67.7 us -> 64.7 us (0.956)
  the two profiles are of different devices: /device:TPU:6 before, /device:TPU:0 now
where the time goes in v7:
time: 64.7 us; the launch traced here: 64.3 us
  Pallas kernels  25.3 us (39%)
  starting transfers between devices  21.7 us (34%)
  waiting for transfers between devices  10.5 us (16%)
  local copies, waits for them, and re-layouts  4.84 us (7%)
  other arithmetic  1.01 us (2%)
  between operations  0.94 us (1%)
    pallas_call x8, Pallas kernels, call(): pl.pallas_call(kernel, name=name, out_shape=outs, in_specs=[vmem] * len(a...  25.3 us
    ppermute x6, starting transfers between devices, body(): came.append(lax.ppermute(sent, axis, ring(axis, 1 - 2 * side)))  10.2 us
    ppermute x3, starting transfers between devices, axis_round(): upper = lax.ppermute(sent[0], axis, ring(axis, -1))  9.2 us
    ppermute x6, waiting for transfers between devices, body(): came.append(lax.ppermute(sent, axis, ring(axis, 1 - 2 * side)))  5.75 us
    ppermute x3, waiting for transfers between devices, axis_round(): lower = lax.ppermute(sent[1], axis, ring(axis, 1))  3.99 us
    unnamed x18, local copies, waits for them, and re-layouts  2.86 us
    ppermute x3, starting transfers between devices, axis_round(): lower = lax.ppermute(sent[1], axis, ring(axis, 1))  1.51 us
  transfers between devices with their start and end apart: 14, of which 5 were waited for; matrix products, arithmetic and copies ran while one was open for 1% of the time, Pallas kernels for 14%

profile of v7, /device:TPU:0, one launch (start us, length us, event | category | flops | bytes accessed | tf_op | source)
XLA Modules:
  0.0 64.3 jit_solution(16299337652070124562)
XLA Ops:
  0.6 0.7 %slice_bitcast_fusion.4 = s32[3]{0:T(128)S(1)} fusion(s32[2,3]{1,0:T(2,128)} %param.12), kind=kLoop, calls=%fused_computation.39 | loop fusion | bytes 24 | tf_op jit(solution)/shard_map/squeeze | solution.py:396
  1.4 0.8 %pad_add_fusion.all_ref = s32[72,128]{1,0:T(8,128)S(1)} fusion(s32[64,128]{1,0:T(8,128)} %bitcast.67, s32[72]{0:T(128)S(1)} %pad.44), kind=kLoop, calls=%fused_computation.6 | loop fusion | flops 9216 | bytes 69920 | tf_op jit(solution)/shard_map/concatenate | solution.py:403
  2.2 3.5 %collective-permute-start = (s32[1,8,128]{2,1,0:T(8,128)S(1)}, s32[1,8,128]{2,1,0:T(8,128)S(1)}, u32[]{:S(2)}, u32[]{:S(2)}) collective-permute-start(s32[1,8,128]{2,1,0:T(8,128)S(1)} %bitcast.64), channel_id=1, source_target_pairs={{0,96},{32,0},{64,32},{96,64},{1,97},{33,1},{65,33},{97,65},{2,98}... | collective-permute-start | bytes 12296 | tf_op jit(solution)/shard_map/ppermute | solution.py:357
  5.7 1.1 %copy-done.1 = f32[3,40960]{1,0:T(4,128)S(1)} copy-done((f32[3,40960]{1,0:T(4,128)S(1)}, f32[3,40960]{1,0:T(4,128)}, u32[]{:S(2)}) %copy-start.1) | copy-done | bytes 491544
  6.8 1.0 %copy-done.2 = s32[2,40960]{1,0:T(2,128)S(1)} copy-done((s32[2,40960]{1,0:T(2,128)S(1)}, s32[2,40960]{1,0:T(2,128)}, u32[]{:S(2)}) %copy-start.2) | copy-done | bytes 327704
  7.8 1.6 %sums_0.1.refs_0_ = f32[224,128]{1,0:T(8,128)S(1)} custom-call(f32[320,3,128]{2,1,0:T(4,128)S(1)} %bitcast.46, s32[320,2,128]{2,1,0:T(2,128)S(1)} %bitcast.50), custom_call_target="tpu_custom_call" | custom-call | flops 782936768 | bytes 2097152 | tf_op jit(solution)/shard_map/sums_0/pallas_call | solution.py:323
  9.4 0.8 %collective-permute-done.1.refs_2_ = s32[1,8,128]{2,1,0:T(8,128)S(1)} collective-permute-done((s32[1,8,128]{2,1,0:T(8,128)S(1)}, s32[1,8,128]{2,1,0:T(8,128)S(1)}, u32[]{:S(2)}, u32[]{:S(2)}) %collective-permute-start.1) | collective-permute-done | bytes 4128 | tf_op jit(solution)/shard_map/ppermute | solution.py:358
  10.2 3.1 %collective-permute-start.2 = (s32[4,1,128]{2,1,0:T(1,128)S(1)}, s32[4,1,128]{2,1,0:T(1,128)S(1)}, u32[]{:S(2)}, u32[]{:S(2)}) collective-permute-start(s32[4,1,128]{2,1,0:T(1,128)S(1)} %slice.112), channel_id=1, source_target_pairs={{0,24},{8,0},{16,8},{24,16},{1,25},{9,1},{17,9},{25,17},{2,26},{10... | collective-permute-start | bytes 6152 | tf_op jit(solution)/shard_map/ppermute | solution.py:357
  13.3 1.6 %sums_1.1.refs_0_ = f32[224,128]{1,0:T(8,128)S(1)} custom-call(f32[320,3,128]{2,1,0:T(4,128)S(1)} %bitcast.47, s32[320,2,128]{2,1,0:T(2,128)S(1)} %bitcast.51, f32[224,128]{1,0:T(8,128)S(1)} %sums_0.1.refs_0_, s32[1,8,128]{2,1,0:T(8,128)S(1)} %collective-permute-done.refs_1_, s32[1,8,128]{2,1,0:T(8,128)S(1)} %collective-permute-done.1.refs_2_), custom_call_target="tpu_custom_call" | custom-call | flops 782936768 | bytes 2097152 | tf_op jit(solution)/shard_map/sums_1/pallas_call | solution.py:323
  15.0 3.2 %collective-permute-done.3.refs_2_ = s32[4,1,128]{2,1,0:T(1,128)S(1)} collective-permute-done((s32[4,1,128]{2,1,0:T(1,128)S(1)}, s32[4,1,128]{2,1,0:T(1,128)S(1)}, u32[]{:S(2)}, u32[]{:S(2)}) %collective-permute-start.3) | collective-permute-done | bytes 2080 | tf_op jit(solution)/shard_map/ppermute | solution.py:358
  18.2 1.5 %collective-permute-start.5 = (s32[4,8,1]{2,1,0:T(8,128)S(1)}, s32[4,8,1]{2,1,0:T(8,128)S(1)}, u32[]{:S(2)}, u32[]{:S(2)}) collective-permute-start(s32[4,8,1]{2,1,0:T(8,128)S(1)} %slice.118), channel_id=1, source_target_pairs={{0,1},{1,2},{2,3},{3,4},{4,5},{5,6},{6,7},{7,0},{8,9},{9,10},{10,1... | collective-permute-start | bytes 392 | tf_op jit(solution)/shard_map/ppermute | solution.py:358
  19.8 2.6 %collective-permute-start.4 = (s32[4,8,1]{2,1,0:T(8,128)S(1)}, s32[4,8,1]{2,1,0:T(8,128)S(1)}, u32[]{:S(2)}, u32[]{:S(2)}) collective-permute-start(s32[4,8,1]{2,1,0:T(8,128)S(1)} %bitcast.66), channel_id=1, source_target_pairs={{0,7},{1,0},{2,1},{3,2},{4,3},{5,4},{6,5},{7,6},{8,15},{9,8},{10,9... | collective-permute-start | bytes 392 | tf_op jit(solution)/shard_map/ppermute | solution.py:357
  22.5 2.1 %sums_2.1.mean_ref = f32[96,128]{1,0:T(8,128)S(1)} custom-call(f32[320,3,128]{2,1,0:T(4,128)S(1)} %bitcast.48, s32[320,2,128]{2,1,0:T(2,128)S(1)} %bitcast.52, f32[224,128]{1,0:T(8,128)S(1)} %sums_1.1.refs_0_, s32[4,1,128]{2,1,0:T(1,128)S(1)} %collective-permute-done.2.refs_1_, s32[4,1,128]{2,1,0:T(1,128)S(1)} %collective-permute-done.3.refs_2_), custom_call_target="tpu_custom_call" | custom-call | flops 782936768 | bytes 2097152 | tf_op jit(solution)/shard_map/sums_2/pallas_call | solution.py:323
  24.7 9.5 %turn.1 = (f32[3,320,128]{2,1,0:T(8,128)S(1)}, f32[96,128]{1,0:T(8,128)S(1)}) custom-call(f32[320,3,128]{2,1,0:T(4,128)S(1)} %bitcast.49, s32[320,2,128]{2,1,0:T(2,128)S(1)} %bitcast.53, f32[96,128]{1,0:T(8,128)S(1)} %sums_2.1.mean_ref, s32[32,128]{1,0:T(8,128)S(1)} %get-tuple-element.51.axis_ref), custom_call_target="tpu_custom_call" | custom-call | flops 4697620480 | bytes 2097152 | tf_op jit(solution)/shard_map/turn/pallas_call | solution.py:323
  34.2 0.7 %collective-permute-start.6 = (f32[3,1,8,128]{3,2,1,0:T(8,128)S(1)}, f32[3,1,8,128]{3,2,1,0:T(8,128)S(1)}, u32[]{:S(2)}, u32[]{:S(2)}) collective-permute-start(f32[3,1,8,128]{3,2,1,0:T(8,128)S(1)} %get-tuple-element.55), channel_id=1, source_target_pairs={{0,96},{32,0},{64,32},{96,64},{1,97},{33,1},{65,33},{97,65},{2,98}... | collective-permute-start | bytes 36872 | tf_op jit(solution)/shard_map/ppermute | solution.py:364
  35.1 3.6 %part_0.1 = (f32[3,160,128]{2,1,0:T(8,128)S(1)}, f32[96,128]{1,0:T(8,128)S(1)}) custom-call(f32[3,320,128]{2,1,0:T(8,128)S(1)} %get-tuple-element.29.refs_0_, s32[320,2,128]{2,1,0:T(2,128)S(1)} %bitcast.54, f32[96,128]{1,0:T(8,128)S(1)} %get-tuple-element.28.refs_2_, s32[32,128]{1,0:T(8,128)S(1)} %get-tuple-element.50.refs_3_, s32[320,128]{1,0:T(8,128)S(1)} %bitcast.56, ...), custom_call_target="tpu_custom_call" | custom-call | flops 1174405120 | bytes 2097152 | tf_op jit(solution)/shard_map/part_0/pallas_call | solution.py:323
  38.7 0.8 %collective-permute-done.7.refs_12_ = f32[3,1,8,128]{3,2,1,0:T(8,128)S(1)} collective-permute-done((f32[3,1,8,128]{3,2,1,0:T(8,128)S(1)}, f32[3,1,8,128]{3,2,1,0:T(8,128)S(1)}, u32[]{:S(2)}, u32[]{:S(2)}) %collective-permute-start.7) | collective-permute-done | bytes 12320 | tf_op jit(solution)/shard_map/ppermute | solution.py:363
  40.3 6.0 %last.1 = (f32[3,41920]{1,0:T(4,128)}, f32[8,128]{1,0:T(8,128)S(1)}, f32[16,128]{1,0:T(8,128)S(1)}, f32[16,128]{1,0:T(8,128)S(1)}, f32[16,128]{1,0:T(8,128)S(1)}...) custom-call(f32[3,320,128]{2,1,0:T(8,128)S(1)} %get-tuple-element.29.refs_0_, ...), custom_call_target="tpu_custom_call" | custom-call | flops 2348810240 | bytes 2097152 | tf_op jit(solution)/shard_map/last/pallas_call | solution.py:323
  46.4 3.3 %collective-permute-start.8 = (f32[28,128]{1,0:T(8,128)S(1)}, f32[28,128]{1,0:T(8,128)S(1)}, u32[]{:S(2)}, u32[]{:S(2)}) collective-permute-start(f32[28,128]{1,0:T(8,128)S(1)} %pad_maximum_fusion.2), channel_id=1, source_target_pairs={{0,24},{8,0},{16,8},{24,16},{1,25},{9,1},{17,9},{25,17},{2,26},{10... | collective-permute-start | bytes 43016 | tf_op jit(solution)/shard_map/ppermute | solution.py:493
  49.8 3.2 %collective-permute-start.11 = (f32[16,128]{1,0:T(8,128)S(1)}, f32[16,128]{1,0:T(8,128)S(1)}, u32[]{:S(2)}, u32[]{:S(2)}) collective-permute-start(f32[16,128]{1,0:T(8,128)S(1)} %get-tuple-element.36), channel_id=1, source_target_pairs={{0,96},{32,0},{64,32},{96,64},{1,97},{33,1},{65,33},{97,65},{2,98}... | collective-permute-start | bytes 24584 | tf_op jit(solution)/shard_map/ppermute | solution.py:493
  53.4 3.5 %collective-permute-start.13 = (f32[17,128]{1,0:T(8,128)S(1)}, f32[17,128]{1,0:T(8,128)S(1)}, u32[]{:S(2)}, u32[]{:S(2)}) collective-permute-start(f32[17,128]{1,0:T(8,128)S(1)} %select_maximum_fusion), channel_id=1, source_target_pairs={{0,7},{1,0},{2,1},{3,2},{4,3},{5,4},{6,5},{7,6},{8,15},{9,8},{10,9... | collective-permute-start | bytes 26120 | tf_op jit(solution)/shard_map/ppermute | solution.py:493
  57.1 1.2 %collective-permute-done.13.refs_5_ = f32[17,128]{1,0:T(8,128)S(1)} collective-permute-done((f32[17,128]{1,0:T(8,128)S(1)}, f32[17,128]{1,0:T(8,128)S(1)}, u32[]{:S(2)}, u32[]{:S(2)}) %collective-permute-start.13) | collective-permute-done | bytes 8736 | tf_op jit(solution)/shard_map/ppermute | solution.py:493
  58.3 4.6 %collective-permute-done.12.refs_4_ = f32[17,128]{1,0:T(8,128)S(1)} collective-permute-done((f32[17,128]{1,0:T(8,128)S(1)}, f32[17,128]{1,0:T(8,128)S(1)}, u32[]{:S(2)}, u32[]{:S(2)}) %collective-permute-start.12) | collective-permute-done | bytes 8736 | tf_op jit(solution)/shard_map/ppermute | solution.py:493
  62.9 0.9 %finish.1 = (f32[96,128]{1,0:T(8,128)}, f32[3,960]{1,0:T(4,128)S(1)}, f32[3,256]{1,0:T(4,128)}) custom-call(s32[8,128]{1,0:T(8,128)S(1)} %get-tuple-element.23.sign_ref, f32[96,128]{1,0:T(8,128)S(1)} %bitcast_select_fusion.mean_ref, f32[8,128]{1,0:T(8,128)S(1)} %get-tuple-element.34.own_ref, f32[3,256]{1,0:T(4,128)S(1)} %copy-done, ...), custom_call_target="tpu_custom_call" | custom-call | flops 1048576 | bytes 2097152 | tf_op jit(solution)/shard_map/finish/pallas_call | solution.py:323
  (65 shorter events, 2.6 us)
Async XLA Ops:
  2.2 7.2 %collective-permute-start = (s32[1,8,128]{2,1,0:T(8,128)S(1)}, s32[1,8,128]{2,1,0:T(8,128)S(1)}, u32[]{:S(2)}, u32[]{:S(2)}) collective-permute-start(s32[1,8,128]{2,1,0:T(8,128)S(1)} %bitcast.64), channel_id=1, source_target_pairs={{0,96},{32,0},{64,32},{96,64},{1,97},{33,1},{65,33},{97,65},{2,98}... | collective-permute-start | bytes 12296 | tf_op jit(solution)/shard_map/ppermute | solution.py:357
  5.7 4.5 %collective-permute-start.1 = (s32[1,8,128]{2,1,0:T(8,128)S(1)}, s32[1,8,128]{2,1,0:T(8,128)S(1)}, u32[]{:S(2)}, u32[]{:S(2)}) collective-permute-start(s32[1,8,128]{2,1,0:T(8,128)S(1)} %bitcast.63), channel_id=1, source_target_pairs={{0,32},{32,64},{64,96},{96,0},{1,33},{33,65},{65,97},{97,1},{2,34}... | collective-permute-start | bytes 12296 | tf_op jit(solution)/shard_map/ppermute | solution.py:358
  5.7 1.1 %copy-start.1 = (f32[3,40960]{1,0:T(4,128)S(1)}, f32[3,40960]{1,0:T(4,128)}, u32[]{:S(2)}) copy-start(f32[3,40960]{1,0:T(4,128)} %param.10) | copy-start | bytes 1474564
  6.8 1.0 %copy-start.2 = (s32[2,40960]{1,0:T(2,128)S(1)}, s32[2,40960]{1,0:T(2,128)}, u32[]{:S(2)}) copy-start(s32[2,40960]{1,0:T(2,128)} %param.11) | copy-start | bytes 983044
  10.2 4.7 %collective-permute-start.2 = (s32[4,1,128]{2,1,0:T(1,128)S(1)}, s32[4,1,128]{2,1,0:T(1,128)S(1)}, u32[]{:S(2)}, u32[]{:S(2)}) collective-permute-start(s32[4,1,128]{2,1,0:T(1,128)S(1)} %slice.112), channel_id=1, source_target_pairs={{0,24},{8,0},{16,8},{24,16},{1,25},{9,1},{17,9},{25,17},{2,26},{10... | collective-permute-start | bytes 6152 | tf_op jit(solution)/shard_map/ppermute | solution.py:357
  13.3 4.8 %collective-permute-start.3 = (s32[4,1,128]{2,1,0:T(1,128)S(1)}, s32[4,1,128]{2,1,0:T(1,128)S(1)}, u32[]{:S(2)}, u32[]{:S(2)}) collective-permute-start(s32[4,1,128]{2,1,0:T(1,128)S(1)} %slice.113), channel_id=1, source_target_pairs={{0,8},{8,16},{16,24},{24,0},{1,9},{9,17},{17,25},{25,1},{2,10},{10... | collective-permute-start | bytes 6152 | tf_op jit(solution)/shard_map/ppermute | solution.py:358
  18.2 6.3 %collective-permute-start.5 = (s32[4,8,1]{2,1,0:T(8,128)S(1)}, s32[4,8,1]{2,1,0:T(8,128)S(1)}, u32[]{:S(2)}, u32[]{:S(2)}) collective-permute-start(s32[4,8,1]{2,1,0:T(8,128)S(1)} %slice.118), channel_id=1, source_target_pairs={{0,1},{1,2},{2,3},{3,4},{4,5},{5,6},{6,7},{7,0},{8,9},{9,10},{10,1... | collective-permute-start | bytes 392 | tf_op jit(solution)/shard_map/ppermute | solution.py:358
  19.8 4.8 %collective-permute-start.4 = (s32[4,8,1]{2,1,0:T(8,128)S(1)}, s32[4,8,1]{2,1,0:T(8,128)S(1)}, u32[]{:S(2)}, u32[]{:S(2)}) collective-permute-start(s32[4,8,1]{2,1,0:T(8,128)S(1)} %bitcast.66), channel_id=1, source_target_pairs={{0,7},{1,0},{2,1},{3,2},{4,3},{5,4},{6,5},{7,6},{8,15},{9,8},{10,9... | collective-permute-start | bytes 392 | tf_op jit(solution)/shard_map/ppermute | solution.py:357
  24.7 10.3 %copy-start.3 = (s32[2,40960]{1,0:T(2,128)S(1)}, s32[2,40960]{1,0:T(2,128)}, u32[]{:S(2)}) copy-start(s32[2,40960]{1,0:T(2,128)} %param.11) | copy-start | bytes 983044
  24.7 10.3 %copy-start.5 = (s32[40960]{0:T(1024)S(1)}, s32[40960]{0:T(1024)}, u32[]{:S(2)}) copy-start(s32[40960]{0:T(1024)} %param.15) | copy-start | bytes 491524
  34.2 0.9 %copy-start.4 = (s32[40960]{0:T(1024)S(1)}, s32[40960]{0:T(1024)}, u32[]{:S(2)}) copy-start(s32[40960]{0:T(1024)} %param.14) | copy-start | bytes 491524
  34.2 4.5 %collective-permute-start.6 = (f32[3,1,8,128]{3,2,1,0:T(8,128)S(1)}, f32[3,1,8,128]{3,2,1,0:T(8,128)S(1)}, u32[]{:S(2)}, u32[]{:S(2)}) collective-permute-start(f32[3,1,8,128]{3,2,1,0:T(8,128)S(1)} %get-tuple-element.55), channel_id=1, source_target_pairs={{0,96},{32,0},{64,32},{96,64},{1,97},{33,1},{65,33},{97,65},{2,98}... | collective-permute-start | bytes 36872 | tf_op jit(solution)/shard_map/ppermute | solution.py:364
  34.9 4.6 %collective-permute-start.7 = (f32[3,1,8,128]{3,2,1,0:T(8,128)S(1)}, f32[3,1,8,128]{3,2,1,0:T(8,128)S(1)}, u32[]{:S(2)}, u32[]{:S(2)}) collective-permute-start(f32[3,1,8,128]{3,2,1,0:T(8,128)S(1)} %get-tuple-element.54), channel_id=1, source_target_pairs={{0,32},{32,64},{64,96},{96,0},{1,33},{33,65},{65,97},{97,1},{2,34}... | collective-permute-start | bytes 36872 | tf_op jit(solution)/shard_map/ppermute | solution.py:363
  35.1 4.5 %copy-start.7 = (s32[2048]{0:T(1024)S(1)}, s32[2048]{0:T(1024)}, u32[]{:S(2)}) copy-start(s32[2048]{0:T(1024)} %param.16) | copy-start | bytes 24580
  35.1 4.5 %copy-start.8 = (f32[2048]{0:T(1024)S(1)}, f32[2048]{0:T(1024)}, u32[]{:S(2)}) copy-start(f32[2048]{0:T(1024)} %param.18) | copy-start | bytes 24580
  39.6 0.7 %copy-start.6 = (s32[2048]{0:T(1024)S(1)}, s32[2048]{0:T(1024)}, u32[]{:S(2)}) copy-start(s32[2048]{0:T(1024)} %param.17) | copy-start | bytes 24580
  46.3 6.7 %collective-permute-start.9 = (f32[28,128]{1,0:T(8,128)S(1)}, f32[28,128]{1,0:T(8,128)S(1)}, u32[]{:S(2)}, u32[]{:S(2)}) collective-permute-start(f32[28,128]{1,0:T(8,128)S(1)} %pad_maximum_fusion.3), channel_id=1, source_target_pairs={{0,8},{8,16},{16,24},{24,0},{1,9},{9,17},{17,25},{25,1},{2,10},{10... | collective-permute-start | bytes 43016 | tf_op jit(solution)/shard_map/ppermute | solution.py:493
  46.4 6.6 %collective-permute-start.8 = (f32[28,128]{1,0:T(8,128)S(1)}, f32[28,128]{1,0:T(8,128)S(1)}, u32[]{:S(2)}, u32[]{:S(2)}) collective-permute-start(f32[28,128]{1,0:T(8,128)S(1)} %pad_maximum_fusion.2), channel_id=1, source_target_pairs={{0,24},{8,0},{16,8},{24,16},{1,25},{9,1},{17,9},{25,17},{2,26},{10... | collective-permute-start | bytes 43016 | tf_op jit(solution)/shard_map/ppermute | solution.py:493
  49.7 7.4 %collective-permute-start.10 = (f32[16,128]{1,0:T(8,128)S(1)}, f32[16,128]{1,0:T(8,128)S(1)}, u32[]{:S(2)}, u32[]{:S(2)}) collective-permute-start(f32[16,128]{1,0:T(8,128)S(1)} %get-tuple-element.35), channel_id=1, source_target_pairs={{0,32},{32,64},{64,96},{96,0},{1,33},{33,65},{65,97},{97,1},{2,34}... | collective-permute-start | bytes 24584 | tf_op jit(solution)/shard_map/ppermute | solution.py:493
  49.8 7.3 %collective-permute-start.11 = (f32[16,128]{1,0:T(8,128)S(1)}, f32[16,128]{1,0:T(8,128)S(1)}, u32[]{:S(2)}, u32[]{:S(2)}) collective-permute-start(f32[16,128]{1,0:T(8,128)S(1)} %get-tuple-element.36), channel_id=1, source_target_pairs={{0,96},{32,0},{64,32},{96,64},{1,97},{33,1},{65,33},{97,65},{2,98}... | collective-permute-start | bytes 24584 | tf_op jit(solution)/shard_map/ppermute | solution.py:493
  53.4 4.9 %collective-permute-start.13 = (f32[17,128]{1,0:T(8,128)S(1)}, f32[17,128]{1,0:T(8,128)S(1)}, u32[]{:S(2)}, u32[]{:S(2)}) collective-permute-start(f32[17,128]{1,0:T(8,128)S(1)} %select_maximum_fusion), channel_id=1, source_target_pairs={{0,7},{1,0},{2,1},{3,2},{4,3},{5,4},{6,5},{7,6},{8,15},{9,8},{10,9... | collective-permute-start | bytes 26120 | tf_op jit(solution)/shard_map/ppermute | solution.py:493
  57.0 5.9 %collective-permute-start.12 = (f32[17,128]{1,0:T(8,128)S(1)}, f32[17,128]{1,0:T(8,128)S(1)}, u32[]{:S(2)}, u32[]{:S(2)}) collective-permute-start(f32[17,128]{1,0:T(8,128)S(1)} %select_maximum_fusion.1), channel_id=1, source_target_pairs={{0,1},{1,2},{2,3},{3,4},{4,5},{5,6},{6,7},{7,0},{8,9},{9,10},{10,1... | collective-permute-start | bytes 26120 | tf_op jit(solution)/shard_map/ppermute | solution.py:493
  57.1 5.8 %copy-start = (f32[3,256]{1,0:T(4,128)S(1)}, f32[3,256]{1,0:T(4,128)}, u32[]{:S(2)}) copy-start(f32[3,256]{1,0:T(4,128)} %speed_ref.1) | copy-start | bytes 9220
